TPU v7x, 32 devices: a whole 2x2x4 slice. The times are simulated.
32 devices in a mesh: seq: 8 (over z, y), grp: 4 (over x, core).
Axes of the slice: x: 2, y: 2, z: 4, core: 2. Of those that a mesh axis runs over, the one named last changes fastest.
Arguments:
- hidden: bfloat16 [4096, 2688], P(('seq', 'grp')), may hold values from -30 to 30
- conv_input: bfloat16 [4096, 3072], P(('seq', 'grp')), may hold values from -30 to 30
- z_stream: bfloat16 [4096, 2048], P(('seq', 'grp')), may hold values from -6 to 6
- log_decay: float32 [32, 4096], P(None, ('seq', 'grp')), may hold values from -1.5 to 0
- conv_weight: float32 [4, 3072], replicated, may hold values from -3 to 3
- norm_gain: float32 [2048], replicated, may hold values from 0.5 to 1.5
- out_weight: bfloat16 [2048, 2688], P('grp'), may hold values from -0.125 to 0.125
- moe_gain: float32 [2688], replicated, may hold values from 0.5 to 1.5
- routes: int32 [4096, 6], P(('seq', 'grp')), may hold values from 0 to 31, all different within a row; in each aligned block of 128 rows (0 to 127, 128 to 255, ...) at most 36 rows name the same one
- gate_weights: float32 [4096, 6], P(('seq', 'grp')), may hold values from 0.1 to 1
- expert_home: int32 [32], replicated, may hold values from 0 to 31, each once
- up_weight: bfloat16 [32, 2688, 1024], P(('seq', 'grp')), may hold values from -0.125 to 0.125
- down_weight: bfloat16 [32, 1024, 2688], P(('seq', 'grp')), may hold values from -0.1875 to 0.1875
Outputs:
- output: bfloat16 [4096, 2688], P(('seq', 'grp'))
Inputs may be any that keep to these rules, and one draw needn't show every extreme that they name: `routes`: among the rows of one device no expert is named more than 36 times, a bound that some block reaches. `expert_home`: each expert is held by exactly one device, and each device holds one expert.
All inputs are finite; a program needn't handle non-finite values.
Results may differ from a plain program's by a relative error of at most 0.013.
Values may be sent and summed in bfloat16 or wider, within the bound.
No kernel may reach another device: no remote copies, remote signals or barrier semaphores. Data moves between devices by JAX's collectives and lax.ppermute only.
A program may use at most 128 MiB of HBM per device.

v0:
```python
import functools

import jax
import jax.numpy as jnp
from jax import lax
from jax.experimental import pallas as pl
from jax.experimental.pallas import tpu as pltpu
from jax.sharding import PartitionSpec as P

AXES = ("seq", "grp")
N = 64
G = 8
EPS = 1e-05
DEC = 16
VMEM_LIMIT = 24 * 1024 * 1024
f32 = jnp.float32
bf16 = jnp.bfloat16


def dot(a, b, contract, precision=None):
    return lax.dot_general(
        a, b, ((contract[0], contract[1]), ((), ())), preferred_element_type=f32, precision=precision
    )


def spread_lanes(columns, width):
    count = len(columns)
    rows = columns[0].shape[0]
    lane = lax.broadcasted_iota(jnp.int32, (rows, count * width), 1)
    out = jnp.broadcast_to(columns[-1], (rows, count * width))
    for j in range(count - 2, -1, -1):
        out = jnp.where(lane < (j + 1) * width, columns[j], out)
    return out


def split_decay(d):
    whole = jnp.floor(d)
    part = d - whole
    coarse = jnp.floor(part * 256.0) * (1.0 / 256.0)
    fine = part - coarse
    row = lax.broadcasted_iota(jnp.int32, (DEC, d.shape[1]), 0)
    rows = jnp.where(row == 0, whole, jnp.where(row == 1, coarse, jnp.where(row == 2, fine, 0.0)))
    return rows.astype(bf16)


def join_decay(rows):
    return jnp.sum(rows.astype(f32), axis=0, keepdims=True)


def silu(x):
    return x * (1.0 / (1.0 + jnp.exp(-x)))


def columns(blocks, inner, keys, c, width, which):
    start, first = 0, 0
    for extent in (inner, keys, keys):
        size = extent // blocks
        if c < first + size:
            return pl.ds(pl.multiple_of(start + which * size + (c - first), width), width)
        start, first = start + extent, first + size


def pick_kernel(blocks, inner, width, at_ref, x_ref, tail_ref, *outs):
    half = at_ref[1]
    length, channels = x_ref.shape
    keys = (channels - inner) // 2
    tail_ref[...] = x_ref[length - tail_ref.shape[0] :, :]
    for b in range(1, blocks):
        for c in range(0, channels // blocks, width):
            outs[b - 1][:, c : c + width] = x_ref[
                :, columns(blocks, inner, keys, c, width, half ^ b)
            ]


def running(ld):
    length = ld.shape[1]
    low = (
        lax.broadcasted_iota(jnp.int32, (length, length), 0)
        >= lax.broadcasted_iota(jnp.int32, (length, length), 1)
    ).astype(f32)
    return (
        dot(ld, low, ((1,), (1,)), lax.Precision.HIGHEST),
        dot(low, ld, ((1,), (1,)), lax.Precision.HIGHEST),
    )


def start_kernel(members, blocks, at_ref, cw_ref, z_ref, *rest):
    xs, prevs, lds = rest[:blocks], rest[blocks : 2 * blocks], rest[2 * blocks : 3 * blocks]
    rest = rest[3 * blocks :]
    acts, outs, scr = rest[:blocks], rest[blocks : blocks + members], rest[-1]
    z_outs = rest[blocks + members : -1]
    member, half = at_ref[0], at_ref[1]
    length = xs[0].shape[0]
    channels = xs[0].shape[1] // blocks
    heads = lds[0].shape[0] // blocks
    count = scr.shape[0]
    per_group = heads // count
    inner = channels - 2 * count * N
    width = inner // count
    head_size = width // per_group
    halo, taps = prevs[0].shape[0], cw_ref.shape[0]
    for b in range(blocks):
        ld = lds[b][pl.ds(pl.multiple_of(half * heads, heads), heads), :]
        cumt = running(ld)[1]
        last = cumt[length - 1 : length, :]
        to_end = jnp.exp(last - cumt)
        act_ref = acts[b]
        for c in range(0, channels, width):
            cols = slice(c, c + width)
            at = columns(blocks, inner * blocks, count * N * blocks, c, width, half)
            padded = jnp.concatenate(
                [prevs[b][:, at], xs[b][:, cols if b else at]], axis=0
            ).astype(f32)
            first = halo - taps + 1
            total = cw_ref[0:1, at] * padded[first : first + length]
            for k in range(1, taps):
                total = total + cw_ref[k : k + 1, at] * padded[first + k : first + k + length]
            act_ref[:, cols] = silu(total).astype(bf16)
        slot = half ^ b
        for g in range(count):
            v = act_ref[:, g * width : (g + 1) * width].astype(f32)
            ik = act_ref[:, inner + g * N : inner + (g + 1) * N]
            hs = range(g * per_group, (g + 1) * per_group)
            weighted = (v * spread_lanes([to_end[:, h : h + 1] for h in hs], head_size)).astype(bf16)
            scr[g, slot, :N, :] = dot(ik, weighted, ((0,), (0,))).astype(bf16)
            scr[g, slot, N:, :] = split_decay(
                spread_lanes([last[:, h : h + 1] for h in hs], head_size)
            )
    for m in range(members):
        outs[m][...] = scr[member ^ m]
    for b in range(1, blocks):
        for c in range(0, inner, width):
            at = pl.ds(pl.multiple_of((half ^ b) * inner + c, width), width)
            z_outs[b - 1][:, c : c + width] = z_ref[:, at]


def in_order(members, blocks, member, chunks, scr):
    for m in range(members):
        who = member ^ m
        for k in range(blocks):
            scr[(who >> 1) * 2 * blocks + 2 * k + (who & 1)] = chunks[m][k]


def plane_kernel(members, blocks, at_ref, *rest):
    chunks, out, scr = rest[:members], rest[members], rest[members + 1]
    in_order(members, blocks, at_ref[0], chunks, scr)
    state = jnp.zeros((N, out.shape[1]), f32)
    total = jnp.zeros((1, out.shape[1]), f32)
    for s in range(members * blocks):
        decay = join_decay(scr[s, N:, :])
        state = jnp.exp(decay) * state + scr[s, :N, :].astype(f32)
        total = total + decay
    out[:N, :] = state.astype(bf16)
    out[N:, :] = split_decay(total)


def pair_kernel(stage, at_ref, own_ref, other_ref, out_ref):
    later = ((at_ref[3] >> stage) & 1) == 1
    own, other = own_ref[:N, :].astype(f32), other_ref[:N, :].astype(f32)
    own_decay, other_decay = join_decay(own_ref[N:, :]), join_decay(other_ref[N:, :])
    first, second = jnp.where(later, other, own), jnp.where(later, own, other)
    out_ref[:N, :] = (jnp.exp(jnp.where(later, own_decay, other_decay)) * first + second).astype(bf16)
    out_ref[N:, :] = split_decay(own_decay + other_decay)


def enter_kernel(members, blocks, stages, at_ref, scr, *rest):
    earlier, outs, inc = rest[:stages], rest[stages : stages + members], rest[-1]
    member = at_ref[0]
    state = jnp.zeros((N, scr.shape[2]), f32)
    for stage in range(stages - 1, -1, -1):
        e = earlier[stage]
        joined = jnp.exp(join_decay(e[N:, :])) * state + e[:N, :].astype(f32)
        state = jnp.where(((at_ref[3] >> stage) & 1) == 1, joined, state)
    for s in range(members * blocks):
        inc[s] = state.astype(bf16)
        state = jnp.exp(join_decay(scr[s, N:, :])) * state + scr[s, :N, :].astype(f32)
    for m in range(members):
        who = member ^ m
        for k in range(blocks):
            outs[m][k] = inc[(who >> 1) * 2 * blocks + 2 * k + (who & 1)]


def inside_kernel(count, blocks, at_ref, *refs):
    acts, lds, outs = (refs[k * blocks : (k + 1) * blocks] for k in range(3))
    length, channels = acts[0].shape
    heads = lds[0].shape[0] // blocks
    per_group = heads // count
    inner = channels - 2 * count * N
    head_size = inner // heads
    causal = lax.broadcasted_iota(jnp.int32, (length, length), 0) >= lax.broadcasted_iota(
        jnp.int32, (length, length), 1
    )
    for b in range(blocks):
        act_ref, out_ref = acts[b], outs[b]
        cum, cumt = running(lds[b][pl.ds(pl.multiple_of(at_ref[1] * heads, heads), heads), :])
        for g in range(count):
            ik = act_ref[:, inner + g * N : inner + (g + 1) * N]
            ok = act_ref[:, inner + (count + g) * N : inner + (count + g + 1) * N]
            meet = jnp.where(causal, dot(ok, ik, ((1,), (1,))), 0.0)
            for h in range(g * per_group, (g + 1) * per_group):
                gap = jnp.where(causal, cumt[:, h : h + 1] - cum[h : h + 1, :], 0.0)
                mixing = (jnp.exp(gap) * meet).astype(bf16)
                cols = slice(h * head_size, (h + 1) * head_size)
                out_ref[:, cols] = dot(mixing, act_ref[:, cols], ((1,), (0,)))


def norm_kernel(members, blocks, b, at_ref, gain_ref, act_ref, ld_ref, inside_ref, z_ref, *rest):
    incoming, own_ref, pair_ref = rest[:members], rest[members], rest[members + 1]
    out_ref, scr, mix = rest[-3], rest[-2], rest[-1]
    member, half, core = at_ref[0], at_ref[1], at_ref[2]
    for m in range(members):
        scr[member ^ m] = incoming[m][...]
    inner = z_ref.shape[1] if b else z_ref.shape[1] // blocks
    heads = ld_ref.shape[0] // blocks
    count = scr.shape[0]
    per_group = heads // count
    width = inner // count
    head_size = inner // heads
    shard = count // 2
    reach = jnp.exp(running(ld_ref[pl.ds(pl.multiple_of(half * heads, heads), heads), :])[1])
    slot = half ^ b
    for g in range(count):
        cols = slice(g * width, (g + 1) * width)
        ok = act_ref[:, inner + (count + g) * N : inner + (count + g + 1) * N]
        hs = range(g * per_group, (g + 1) * per_group)
        far = dot(ok, scr[g, slot], ((1,), (0,)))
        ssm = inside_ref[:, cols] + far * spread_lanes([reach[:, h : h + 1] for h in hs], head_size)
        at = pl.ds(pl.multiple_of(half * inner + g * width, width), width)
        gated = ssm * silu(z_ref[:, cols if b else at].astype(f32))
        square = jnp.mean(gated * gated, axis=1, keepdims=True)
        mix[((g // shard) ^ core) * shard + g % shard] = (
            gated * lax.rsqrt(square + EPS) * gain_ref[:, at]
        ).astype(bf16)
    model = out_ref.shape[1]
    tile = 384 if model % 384 == 0 else model
    for c in range(0, model, tile):
        total = None
        for g in range(count):
            rows = (own_ref, pair_ref)[g // shard]
            at = (g % shard) * width
            part = dot(mix[g], rows[at : at + width, c : c + tile], ((1,), (0,)))
            total = part if total is None else total + part
        out_ref[:, c : c + tile] = total.astype(out_ref.dtype)


def token_kernel(blocks, gain_ref, hidden_ref, own_ref, meta_ref, *rest):
    others, residual_ref, block_ref = rest[: blocks - 1], rest[blocks - 1], rest[blocks]
    model = hidden_ref.shape[1]
    total = hidden_ref[...].astype(f32) + own_ref[...]
    for other in others:
        total = total + other[...].astype(f32)
    residual = total.astype(bf16)
    residual_ref[...] = residual
    wide = residual.astype(f32)
    square = jnp.mean(wide * wide, axis=1, keepdims=True)
    block_ref[:, :model] = (wide * lax.rsqrt(square + EPS) * gain_ref[...]).astype(bf16)
    block_ref[:, model:] = meta_ref[...]


def dispatch_kernel(devices, capacity, at_ref, block_ref, *rest):
    outs, weigh_ref = rest[:-1], rest[-1]
    length = block_ref.shape[0]
    rows, model = outs[0].shape
    lanes = len(outs) * rows
    device = lax.broadcasted_iota(jnp.int32, (devices, lanes), 0)

    def layout(shape):
        lane = lax.broadcasted_iota(jnp.int32, shape, 1)
        chip, within = jnp.zeros(shape, jnp.int32), lane
        for k in range(1, len(outs)):
            chip = jnp.where(lane >= k * rows, k, chip)
            within = jnp.where(lane >= k * rows, lane - k * rows, within)
        core = jnp.where(within >= capacity, 1, 0)
        return chip, core, within - capacity * core

    chip, core, _ = layout((devices, lanes))
    select = (device == at_ref[1] + (at_ref[0] ^ (2 * chip + core))).astype(f32).astype(bf16)
    place = layout((length, lanes))[2]
    place = jnp.where(place < capacity, place, -2).astype(f32)
    slot = dot(block_ref[:, model : model + devices], select, ((1,), (0,)))
    gate = dot(block_ref[:, model + devices : model + 2 * devices], select, ((1,), (0,))) + dot(
        block_ref[:, model + 2 * devices : model + 3 * devices], select, ((1,), (0,))
    )
    hit = slot == place
    weigh_ref[...] = jnp.where(hit, gate, 0.0).astype(bf16)
    take = jnp.where(hit, 1.0, 0.0).astype(bf16)
    total = dot(take, block_ref[:, :model], ((0,), (0,)))
    for k in range(len(outs)):
        outs[k][...] = total[k * rows : (k + 1) * rows].astype(bf16)


def chosen_rows(shape, dim, chip, core, capacity):
    listed = lax.broadcasted_iota(jnp.int32, shape, 1 - dim)
    within = lax.broadcasted_iota(jnp.int32, shape, dim) - core * capacity
    hit = (listed == chip * capacity + within) & (within >= 0) & (within < capacity)
    return hit.astype(f32).astype(bf16)


def listed_rows(ins, core, capacity, count):
    total = None
    for k, ref in enumerate(ins):
        part = dot(chosen_rows((count, ref.shape[0]), 1, k, core, capacity), ref[...], ((1,), (0,)))
        total = part if total is None else total + part
    return total.astype(bf16)


def other_kernel(capacity, *refs):
    refs[-1][...] = listed_rows(refs[:-1], 1, capacity, refs[-1].shape[0])


def expert_kernel(capacity, tile, *refs):
    ins, (got_ref, up_ref, down_ref, mine_ref, other_ref, rows_ref, act_ref) = refs[:-7], refs[-7:]
    count, model = got_ref.shape
    rows_ref[:count, :] = listed_rows(ins, 0, capacity, count)
    rows_ref[count:, :] = got_ref[...]
    ffw = up_ref.shape[1]
    step = 512 if ffw % 512 == 0 else ffw

    @pl.loop(0, ffw // step)
    def _(f):
        cols = pl.ds(pl.multiple_of(f * step, step), step)
        up = jnp.maximum(dot(rows_ref[...], up_ref[:, cols], ((1,), (0,))), 0.0)
        act_ref[:, cols] = (up * up).astype(bf16)

    @pl.loop(0, model // tile)
    def _(c):
        cols = pl.ds(pl.multiple_of(c * tile, tile), tile)
        part = dot(act_ref[...], down_ref[:, cols], ((1,), (0,)))
        mine_ref[:, cols] = part[:count].astype(bf16)
        other_ref[:, cols] = part[count:].astype(bf16)


def return_kernel(capacity, mine_ref, back_ref, *outs):
    count = mine_ref.shape[0]
    for k, out in enumerate(outs):
        shape = (out.shape[0], count)
        out[...] = (
            dot(chosen_rows(shape, 0, k, 0, capacity), mine_ref[...], ((1,), (0,)))
            + dot(chosen_rows(shape, 0, k, 1, capacity), back_ref[...], ((1,), (0,)))
        ).astype(bf16)


def after(x, *others):
    return lax.optimization_barrier((x,) + others)[0]


def local(
    hidden,
    conv_input,
    z_stream,
    log_decay,
    conv_weight,
    norm_gain,
    out_weight,
    moe_gain,
    routes,
    gate_weights,
    expert_home,
    up_weight,
    down_weight,
):
    n_grp = lax.axis_size("grp")
    devices = lax.axis_size("seq") * n_grp
    plane = 2 * n_grp
    outer = devices // plane
    me = lax.axis_index("seq") * n_grp + lax.axis_index("grp")
    r = lax.rem(me, plane)
    place = lax.div(me, plane)

    def swap(x, m):
        return lax.ppermute(x, AXES, [(d, d ^ m) for d in range(devices)])

    def onward(x, by):
        return lax.ppermute(
            x, AXES, [(d, d + by) for d in range(devices) if d + by < devices]
        )

    def turn(x):
        return lax.ppermute(x, AXES, [(d, (d + plane) % devices) for d in range(devices)])

    length, channels = conv_input.shape
    inner = z_stream.shape[1]
    width = inner // G
    model = hidden.shape[1]
    smem = pl.BlockSpec(memory_space=pltpu.SMEM)
    halo = 16

    blocks = n_grp // 2
    members = plane // blocks
    grp = lax.axis_index("grp")
    half = lax.div(grp, 2)
    core = lax.rem(grp, 2)
    member = lax.div(r, n_grp) * 2 + core
    at_member = jnp.stack([member, half, core, place]).astype(jnp.int32)
    count = G // blocks

    def onward_to(x, by, m):
        return lax.ppermute(
            x, AXES, [(d, (d + by) ^ m) for d in range(devices) if d + by < devices]
        )

    shapes = jax.ShapeDtypeStruct
    vm = pl.BlockSpec(memory_space=pltpu.VMEM)
    wide = channels // blocks
    chunk = (N + DEC, width)

    def kernel_call(kernel, inputs, outs, scratch=(), flops=0, moved=0, scalars=True):
        return pl.pallas_call(
            kernel,
            out_shape=outs,
            in_specs=([smem] if scalars else []) + [vm] * (len(inputs) - (1 if scalars else 0)),
            scratch_shapes=list(scratch),
            compiler_params=pltpu.CompilerParams(vmem_limit_bytes=VMEM_LIMIT),
            cost_estimate=pl.CostEstimate(flops=flops, bytes_accessed=moved, transcendentals=0),
        )(*inputs)

    picked = kernel_call(
        functools.partial(pick_kernel, blocks, inner, width),
        [at_member, conv_input],
        [shapes((halo, channels), bf16)] + [shapes((length, wide), bf16)] * (blocks - 1),
    )
    tail = picked[0]
    xs, prevs, lds = [conv_input], [onward_to(tail, 1, 0)], [log_decay]
    for b in range(1, blocks):
        xs.append(swap(picked[b], 2 * b))
        prevs.append(onward_to(tail, 1, 2 * b))
        lds.append(swap(log_decay, 2 * b))

    rows_own = out_weight
    rows_pair = swap(out_weight, 1)
    shard = out_weight.shape[0]

    first = kernel_call(
        functools.partial(start_kernel, members, blocks),
        [at_member, conv_weight, z_stream] + xs + prevs + lds,
        [shapes((length, wide), bf16)] * blocks
        + [shapes((blocks,) + chunk, bf16)] * members
        + [shapes((length, inner // blocks), bf16)] * (blocks - 1),
        [pltpu.VMEM((count, blocks) + chunk, bf16)],
        50000000,
        8000000,
    )
    acts = first[:blocks]
    sends = first[blocks : blocks + members]
    zs = [z_stream] + [swap(first[blocks + members + b - 1], 2 * b) for b in range(1, blocks)]
    mask = [(m >> 1) * n_grp + (m & 1) for m in range(members)]
    chunks = [sends[0]] + [swap(sends[m], mask[m]) for m in range(1, members)]
    inside = kernel_call(
        functools.partial(inside_kernel, count, blocks),
        [at_member] + list(acts) + lds,
        [shapes((length, inner // blocks), f32)] * blocks,
        (),
        100000000,
        15000000,
    )
    whole, ordered = kernel_call(
        functools.partial(plane_kernel, members, blocks),
        [at_member] + chunks,
        [shapes(chunk, bf16), shapes((plane,) + chunk, bf16)],
    )
    earlier, stage = [], 0
    while (1 << stage) < outer:
        earlier.append(swap(whole, plane << stage))
        stage += 1
        if (1 << stage) < outer:
            whole = kernel_call(
                functools.partial(pair_kernel, stage - 1),
                [at_member, whole, earlier[-1]],
                shapes(chunk, bf16),
            )
    entering = kernel_call(
        functools.partial(enter_kernel, members, blocks, stage),
        [at_member, ordered] + earlier,
        [shapes((blocks, N, width), bf16)] * members,
        [pltpu.VMEM((plane, N, width), bf16)],
        1000000,
        2000000,
    )
    incoming = [entering[0]] + [swap(entering[m], mask[m]) for m in range(1, members)]
    def project(b):
        return kernel_call(
            functools.partial(norm_kernel, members, blocks, b),
            [at_member, norm_gain[None, :], acts[b], lds[b], inside[b], zs[b]]
            + incoming
            + [rows_own, rows_pair],
            shapes((length, model), bf16 if b else f32),
            [pltpu.VMEM((count, blocks, N, width), bf16), pltpu.VMEM((count, length, width), bf16)],
            800000000,
            8000000,
        )

    others = [swap(project(b), 2 * b) for b in range(1, blocks)]
    mine = project(0)

    top_count = routes.shape[1]
    capacity = max(2, 3 * length * top_count // (2 * devices))
    experts = expert_home.shape[0]
    picked = routes[:, :, None] == jnp.arange(experts, dtype=jnp.int32)[None, None, :]
    target = jnp.sum(jnp.where(picked, expert_home[None, None, :], 0), axis=2)
    at_device = target[:, :, None] == jnp.arange(devices, dtype=jnp.int32)[None, None, :]
    chosen = jnp.any(at_device, axis=1)
    gates = jnp.sum(jnp.where(at_device, gate_weights[:, :, None], 0.0), axis=1)
    before = (
        lax.broadcasted_iota(jnp.int32, (length, length), 0)
        > lax.broadcasted_iota(jnp.int32, (length, length), 1)
    ).astype(bf16)
    rank = jnp.dot(before, chosen.astype(bf16), preferred_element_type=f32)
    slots = jnp.where(chosen, rank, -1.0)
    gate_high = jnp.floor(gates * 128.0) * (1.0 / 128.0)
    meta = jnp.concatenate([slots, gate_high, gates - gate_high], axis=1).astype(bf16)
    extra = -(-3 * devices // 128) * 128
    meta = jnp.pad(meta, ((0, 0), (0, extra - 3 * devices)))

    up_local = up_weight[0]
    down_local = down_weight[0]
    hops = list(range(0, plane, 2))
    two = -(-2 * capacity // 8) * 8

    at = jnp.stack([r, place * plane]).astype(jnp.int32)
    count_rows = -(-len(hops) * capacity // 16) * 16
    listed = shapes((count_rows, model), bf16)
    tile = 896 if model % 896 == 0 else model

    def dispatch(block):
        out = kernel_call(
            functools.partial(dispatch_kernel, devices, capacity),
            [at, block],
            [shapes((two, model), bf16)] * len(hops) + [shapes((length, len(hops) * two), bf16)],
        )
        return out[-1], [out[0]] + [swap(out[k], hops[k]) for k in range(1, len(hops))]

    def held(rows, *others):
        return list(lax.optimization_barrier(tuple(rows) + others)[: len(rows)]) if others else list(rows)

    def work(rows, before_list, before_work):
        rows = held(rows, *before_list)
        other = kernel_call(
            functools.partial(other_kernel, capacity), list(rows), listed, scalars=False
        )
        mine, theirs = kernel_call(
            functools.partial(expert_kernel, capacity, tile),
            held(rows, *before_work) + [swap(other, 1), up_local, down_local],
            [listed, listed],
            [
                pltpu.VMEM((2 * count_rows, model), bf16),
                pltpu.VMEM((2 * count_rows, up_local.shape[1]), bf16),
            ],
            scalars=False,
        )
        return mine, swap(theirs, 1)

    def sort_back(mine, theirs):
        return kernel_call(
            functools.partial(return_kernel, capacity),
            [mine, theirs],
            [shapes((two, model), bf16)] * len(hops),
            scalars=False,
        )

    def send_back(parts):
        return [parts[0]] + [swap(parts[k], hops[k]) for k in range(1, len(hops))]

    def gather_up(weigh, back):
        return jnp.dot(weigh, jnp.concatenate(back, axis=0), preferred_element_type=f32)

    residual_one, block = kernel_call(
        functools.partial(token_kernel, blocks),
        [moe_gain[None, :], hidden, mine, meta] + others,
        [shapes((length, model), bf16), shapes((length, model + extra), bf16)],
        scalars=False,
    )
    weighs, arrived, made, results, parts = {}, {}, {}, {}, {}
    end = outer - 1

    def give_back(step, *before):
        mine, theirs = made[step]
        if before:
            mine = after(mine, *before)
        results[step] = sort_back(mine, theirs)
        return send_back(results[step])

    for step in range(outer):
        following = turn(block) if step < end else None
        if step:
            before = arrived[step - 1][1:2] + ([made[step - 2][0]] if step >= 2 else [])
            block = held([block], *before)[0]
        weighs[step], arrived[step] = dispatch(block)
        block = following
        if step:
            made[step - 1] = work(arrived[step - 1], [weighs[step]], [])
        if 1 <= step - 1 < end:
            parts[step - 1] = gather_up(weighs[step - 1], give_back(step - 1))
    before = [made[end - 1][0]] if end else []
    if end >= 3:
        before.append(parts[end - 2])
    made[end] = work(arrived[end], before, [])
    if end:
        parts[end] = gather_up(weighs[end], give_back(end, *([parts[end - 1]] if end >= 2 else [])))
    back = give_back(0, *([results[end][0]] if end else []))
    carried = None
    for step in range(1, outer):
        part = parts[step]
        if carried is not None:
            part = part + carried.astype(f32)
        carried = turn(part.astype(bf16))
    if carried is not None:
        back = held(back, carried)
    part = residual_one.astype(f32) + gather_up(weighs[0], back)
    if carried is not None:
        part = part + carried.astype(f32)
    return part.astype(bf16)


def solution(mesh):
    placed = (
        P(AXES, None),
        P(AXES, None),
        P(AXES, None),
        P(None, AXES),
        P(),
        P(),
        P("grp", None),
        P(),
        P(AXES, None),
        P(AXES, None),
        P(),
        P(AXES, None, None),
        P(AXES, None, None),
    )
    return jax.shard_map(local, mesh=mesh, in_specs=placed, out_specs=P(AXES, None), check_vma=False)
```

profile of v0, /device:TPU:0, one launch (start us, length us, event | category | flops | bytes accessed | tf_op | source)
XLA Modules:
  0.0 245.3 jit_solution(12917262931311253026)
XLA Ops:
  2.3 2.6 %collective-permute-start = (bf16[128,1536]{1,0:T(8,128)(2,1)S(1)}, bf16[128,1536]{1,0:T(8,128)(2,1)S(1)}, u32[]{:S(2)}, u32[]{:S(2)}) collective-permute-start(bf16[128,1536]{1,0:T(8,128)(2,1)S(1)} %get-tuple-element.93), channel_id=1, source_target_pairs={{0,2},{1,3},{2,0},{3,1},{4,6},{5,7},{6,4},{7,5},{8,10},{9,11},{10,... | collective-permute-start | bytes 1179656 | tf_op jit(solution)/shard_map/ppermute | solution.py:371
  4.9 2.3 collective-permute-start.2
  7.2 2.3 collective-permute-start.1
  9.4 1.7 collective-permute-start.3
  11.2 5.9 %collective-permute-done.3.rest_5_.refs_3_.ld_ref = f32[32,128]{1,0:T(8,128)S(1)} collective-permute-done((f32[32,128]{1,0:T(8,128)}, f32[32,128]{1,0:T(8,128)S(1)}, u32[]{:S(2)}, u32[]{:S(2)}) %collective-permute-start.3) | collective-permute-done | bytes 16416 | tf_op jit(solution)/shard_map/ppermute | solution.py:371
  19.7 2.6 %shard_map.128 = (bf16[128,1536]{1,0:T(8,128)(2,1)S(1)}, bf16[128,1536]{1,0:T(8,128)(2,1)S(1)}, bf16[2,80,256]{2,1,0:T(8,128)(2,1)S(1)}, bf16[2,80,256]{2,1,0:T(...) custom-call(s32[4]{0:T(128)S(1)} %pad_add_fusion.at_ref, ...), custom_call_target="tpu_custom_call" | custom-call | flops 50000000 | bytes 8000000 | tf_op jit(solution)/shard_map/pallas_call | solution.py:408
  24.3 3.4 %collective-permute-done.5.rest_2_ = bf16[2,80,256]{2,1,0:T(8,128)(2,1)S(1)} collective-permute-done((bf16[2,80,256]{2,1,0:T(8,128)(2,1)S(1)}, bf16[2,80,256]{2,1,0:T(8,128)(2,1)S(1)}, u32[]{:S(2)}, u32[]{:S(2)}) %collective-permute-start.5) | collective-permute-done | bytes 81952 | tf_op jit(solution)/shard_map/ppermute | solution.py:371
  29.2 2.0 collective-permute-start.7
  31.3 1.5 collective-permute-start.13
  33.9 3.1 %collective-permute-start.8 = (bf16[80,256]{1,0:T(8,128)(2,1)S(1)}, bf16[80,256]{1,0:T(8,128)(2,1)S(1)}, u32[]{:S(2)}, u32[]{:S(2)}) collective-permute-start(bf16[80,256]{1,0:T(8,128)(2,1)S(1)} %shard_map.131), channel_id=1, source_target_pairs={{0,16},{1,17},{2,18},{3,19},{4,20},{5,21},{6,22},{7,23},{8,24},{9,... | collective-permute-start | bytes 122888 | tf_op jit(solution)/shard_map/ppermute | solution.py:371
  37.0 1.9 collective-permute-done.8.rest_1_
  42.2 2.7 %shard_map.129 = (f32[128,1024]{1,0:T(8,128)S(1)}, f32[128,1024]{1,0:T(8,128)S(1)}) custom-call(s32[4]{0:T(128)S(1)} %pad_add_fusion.at_ref, bf16[128,1536]{1,0:T(8,128)(2,1)S(1)} %get-tuple-element.95.refs_0_.act_ref, bf16[128,1536]{1,0:T(8,128)(2,1)S(1)} %get-tuple-element.96.refs_1_.act_ref, f32[32,128]{1,0:T(8,128)S(1)} %copy-done.11, ...), custom_call_target="tpu_custom_call" | custom-call | flops 100000000 | bytes 15000000 | tf_op jit(solution)/shard_map/pallas_call | solution.py:408
  45.8 4.6 %shard_map.134 = bf16[128,2688]{1,0:T(8,128)(2,1)} custom-call(s32[4]{0:T(128)S(1)} %pad_add_fusion.at_ref, f32[1,2048]{1,0:T(1,128)S(1)} %bitcast.24, bf16[128,1536]{1,0:T(8,128)(2,1)S(1)} %get-tuple-element.96.refs_1_.act_ref, f32[32,128]{1,0:T(8,128)S(1)} %collective-permute-done.3.rest_5_.refs_3_.ld_ref, f32[128,1024]{1,0:T(8,128)S(1)} %get-tuple-element.108.inside_ref, ...), custom_call_target="tpu_custom_call" | custom-call | flops 800000000 | bytes 8000000 | tf_op jit(solution)/shard_map/pallas_call | solution.py:408
  50.3 1.8 collective-permute-start.14
  60.1 3.7 %shard_map.133.own_ref = f32[128,2688]{1,0:T(8,128)S(1)} custom-call(s32[4]{0:T(128)S(1)} %copy-done.16, f32[1,2048]{1,0:T(1,128)S(1)} %bitcast.25, bf16[128,1536]{1,0:T(8,128)(2,1)S(1)} %copy-done.7, f32[32,128]{1,0:T(8,128)S(1)} %copy-done.12, f32[128,1024]{1,0:T(8,128)S(1)} %copy-done.10, bf16[128,2048]{1,0:T(8,128)(2,1)S(1)} %copy-done.5, ...), custom_call_target="tpu_custom_call" | custom-call | flops 800000000 | bytes 8000000 | tf_op jit(solution)/shard_map/pallas_call | solution.py:408
  63.9 4.6 %collective-permute-done.14.rest_0_ = bf16[128,2688]{1,0:T(8,128)(2,1)} collective-permute-done((bf16[128,2688]{1,0:T(8,128)(2,1)}, bf16[128,2688]{1,0:T(8,128)(2,1)}, u32[]{:S(2)}, u32[]{:S(2)}) %collective-permute-start.14) | collective-permute-done | bytes 688160 | tf_op jit(solution)/shard_map/ppermute | solution.py:371
  68.4 1.7 shard_map.135
  70.1 2.1 collective-permute-start.18
  73.6 1.6 collective-permute-start.15
  77.1 8.4 %collective-permute-done.15.refs_1_ = bf16[72,2688]{1,0:T(8,128)(2,1)S(1)} collective-permute-done((bf16[72,2688]{1,0:T(8,128)(2,1)S(1)}, bf16[72,2688]{1,0:T(8,128)(2,1)S(1)}, u32[]{:S(2)}, u32[]{:S(2)}) %collective-permute-start.15) | collective-permute-done | bytes 387104 | tf_op jit(solution)/shard_map/ppermute | solution.py:371
  85.5 4.8 %collective-permute-done.18.block_ref = bf16[128,2816]{1,0:T(8,128)(2,1)S(1)} collective-permute-done((bf16[128,2816]{1,0:T(8,128)(2,1)S(1)}, bf16[128,2816]{1,0:T(8,128)(2,1)S(1)}, u32[]{:S(2)}, u32[]{:S(2)}) %collective-permute-start.18) | collective-permute-done | bytes 720928 | tf_op jit(solution)/shard_map/ppermute | solution.py:379
  91.7 1.6 collective-permute-done.16.refs_2_
  94.4 1.7 collective-permute-start.20
  97.9 1.6 collective-permute-start.25
  99.5 2.6 %copy-done = bf16[1,2688,1024]{2,1,0:T(8,128)(2,1)S(1)} copy-done((bf16[1,2688,1024]{2,1,0:T(8,128)(2,1)S(1)}, bf16[1,2688,1024]{2,1,0:T(8,128)(2,1)}, u32[]{:S(2)}) %copy-start) | copy-done | bytes 5505048
  102.1 2.6 %copy-done.1 = bf16[1,1024,2688]{2,1,0:T(8,128)(2,1)S(1)} copy-done((bf16[1,1024,2688]{2,1,0:T(8,128)(2,1)S(1)}, bf16[1,1024,2688]{2,1,0:T(8,128)(2,1)}, u32[]{:S(2)}) %copy-start.1) | copy-done | bytes 5505048
  104.6 5.4 %shard_map.139 = (bf16[144,2688]{1,0:T(8,128)(2,1)S(1)}, bf16[144,2688]{1,0:T(8,128)(2,1)S(1)}) custom-call(bf16[72,2688]{1,0:T(8,128)(2,1)S(1)} %get-tuple-element.119.refs_0_, bf16[72,2688]{1,0:T(8,128)(2,1)S(1)} %collective-permute-done.15.refs_1_, bf16[72,2688]{1,0:T(8,128)(2,1)S(1)} %collective-permute-done.16.refs_2_, ...), custom_call_target="tpu_custom_call" | custom-call | tf_op jit(solution)/shard_map/pallas_call | solution.py:408
  110.0 4.7 %collective-permute-done.20.block_ref = bf16[128,2816]{1,0:T(8,128)(2,1)S(1)} collective-permute-done((bf16[128,2816]{1,0:T(8,128)(2,1)S(1)}, bf16[128,2816]{1,0:T(8,128)(2,1)S(1)}, u32[]{:S(2)}, u32[]{:S(2)}) %collective-permute-start.20) | collective-permute-done | bytes 720928 | tf_op jit(solution)/shard_map/ppermute | solution.py:379
  117.2 1.9 collective-permute-start.21
  122.6 5.4 %shard_map.142 = (bf16[144,2688]{1,0:T(8,128)(2,1)S(1)}, bf16[144,2688]{1,0:T(8,128)(2,1)S(1)}) custom-call(bf16[72,2688]{1,0:T(8,128)(2,1)S(1)} %get-tuple-element.131.refs_0_, bf16[72,2688]{1,0:T(8,128)(2,1)S(1)} %collective-permute-done.22.refs_1_, bf16[72,2688]{1,0:T(8,128)(2,1)S(1)} %collective-permute-done.24.refs_2_, ...), custom_call_target="tpu_custom_call" | custom-call | tf_op jit(solution)/shard_map/pallas_call | solution.py:408
  128.1 2.9 %collective-permute-done.23.refs_1_ = bf16[72,2688]{1,0:T(8,128)(2,1)S(1)} collective-permute-done((bf16[72,2688]{1,0:T(8,128)(2,1)S(1)}, bf16[72,2688]{1,0:T(8,128)(2,1)S(1)}, u32[]{:S(2)}, u32[]{:S(2)}) %collective-permute-start.23) | collective-permute-done | bytes 387104 | tf_op jit(solution)/shard_map/ppermute | solution.py:371
  131.0 6.6 %collective-permute-done.21.block_ref = bf16[128,2816]{1,0:T(8,128)(2,1)S(1)} collective-permute-done((bf16[128,2816]{1,0:T(8,128)(2,1)S(1)}, bf16[128,2816]{1,0:T(8,128)(2,1)S(1)}, u32[]{:S(2)}, u32[]{:S(2)}) %collective-permute-start.21) | collective-permute-done | bytes 720928 | tf_op jit(solution)/shard_map/ppermute | solution.py:379
  146.9 6.2 %collective-permute-done.34 = bf16[72,2688]{1,0:T(8,128)(2,1)S(1)} collective-permute-done((bf16[72,2688]{1,0:T(8,128)(2,1)S(1)}, bf16[72,2688]{1,0:T(8,128)(2,1)S(1)}, u32[]{:S(2)}, u32[]{:S(2)}) %collective-permute-start.34) | collective-permute-done | bytes 387104 | tf_op jit(solution)/shard_map/ppermute | solution.py:371
  153.2 1.5 collective-permute-start.29
  154.7 5.4 %shard_map.145 = (bf16[144,2688]{1,0:T(8,128)(2,1)S(1)}, bf16[144,2688]{1,0:T(8,128)(2,1)S(1)}) custom-call(bf16[72,2688]{1,0:T(8,128)(2,1)S(1)} %get-tuple-element.145.refs_0_, bf16[72,2688]{1,0:T(8,128)(2,1)S(1)} %collective-permute-done.23.refs_1_, bf16[72,2688]{1,0:T(8,128)(2,1)S(1)} %collective-permute-done.30.refs_2_, ...), custom_call_target="tpu_custom_call" | custom-call | tf_op jit(solution)/shard_map/pallas_call | solution.py:408
  160.0 2.6 %collective-permute-done.35 = bf16[72,2688]{1,0:T(8,128)(2,1)S(1)} collective-permute-done((bf16[72,2688]{1,0:T(8,128)(2,1)S(1)}, bf16[72,2688]{1,0:T(8,128)(2,1)S(1)}, u32[]{:S(2)}, u32[]{:S(2)}) %collective-permute-start.35) | collective-permute-done | bytes 387104 | tf_op jit(solution)/shard_map/ppermute | solution.py:371
  163.1 6.7 %collective-permute-done.27.refs_1_ = bf16[72,2688]{1,0:T(8,128)(2,1)S(1)} collective-permute-done((bf16[72,2688]{1,0:T(8,128)(2,1)S(1)}, bf16[72,2688]{1,0:T(8,128)(2,1)S(1)}, u32[]{:S(2)}, u32[]{:S(2)}) %collective-permute-start.27) | collective-permute-done | bytes 387104 | tf_op jit(solution)/shard_map/ppermute | solution.py:371
  170.5 8.0 %collective-permute-done.29.refs_3_ = bf16[72,2688]{1,0:T(8,128)(2,1)S(1)} collective-permute-done((bf16[72,2688]{1,0:T(8,128)(2,1)S(1)}, bf16[72,2688]{1,0:T(8,128)(2,1)S(1)}, u32[]{:S(2)}, u32[]{:S(2)}) %collective-permute-start.29) | collective-permute-done | bytes 387104 | tf_op jit(solution)/shard_map/ppermute | solution.py:371
  184.6 5.4 %shard_map.148 = (bf16[144,2688]{1,0:T(8,128)(2,1)S(1)}, bf16[144,2688]{1,0:T(8,128)(2,1)S(1)}) custom-call(bf16[72,2688]{1,0:T(8,128)(2,1)S(1)} %get-tuple-element.155.refs_0_, bf16[72,2688]{1,0:T(8,128)(2,1)S(1)} %collective-permute-done.27.refs_1_, bf16[72,2688]{1,0:T(8,128)(2,1)S(1)} %collective-permute-done.28.refs_2_, ...), custom_call_target="tpu_custom_call" | custom-call | tf_op jit(solution)/shard_map/pallas_call | solution.py:408
  190.0 2.9 %collective-permute-done.39 = bf16[72,2688]{1,0:T(8,128)(2,1)S(1)} collective-permute-done((bf16[72,2688]{1,0:T(8,128)(2,1)S(1)}, bf16[72,2688]{1,0:T(8,128)(2,1)S(1)}, u32[]{:S(2)}, u32[]{:S(2)}) %collective-permute-start.39) | collective-permute-done | bytes 387104 | tf_op jit(solution)/shard_map/ppermute | solution.py:371
  192.9 8.1 %collective-permute-done.40 = bf16[72,2688]{1,0:T(8,128)(2,1)S(1)} collective-permute-done((bf16[72,2688]{1,0:T(8,128)(2,1)S(1)}, bf16[72,2688]{1,0:T(8,128)(2,1)S(1)}, u32[]{:S(2)}, u32[]{:S(2)}) %collective-permute-start.40) | collective-permute-done | bytes 387104 | tf_op jit(solution)/shard_map/ppermute | solution.py:371
  206.3 1.6 collective-permute-start.49
  207.9 12.5 %collective-permute-done.51 = bf16[128,2688]{1,0:T(8,128)(2,1)S(1)} collective-permute-done((bf16[128,2688]{1,0:T(8,128)(2,1)S(1)}, bf16[128,2688]{1,0:T(8,128)(2,1)S(1)}, u32[]{:S(2)}, u32[]{:S(2)}) %collective-permute-start.51) | collective-permute-done | bytes 688160 | tf_op jit(solution)/shard_map/ppermute | solution.py:379
  220.4 3.0 %collective-permute-done.48 = bf16[72,2688]{1,0:T(8,128)(2,1)S(1)} collective-permute-done((bf16[72,2688]{1,0:T(8,128)(2,1)S(1)}, bf16[72,2688]{1,0:T(8,128)(2,1)S(1)}, u32[]{:S(2)}, u32[]{:S(2)}) %collective-permute-start.48) | collective-permute-done | bytes 387104 | tf_op jit(solution)/shard_map/ppermute | solution.py:371
  224.0 1.7 collective-permute-start.52
  228.6 1.7 collective-permute-start.46
  230.3 8.4 %collective-permute-done.44 = bf16[72,2688]{1,0:T(8,128)(2,1)S(1)} collective-permute-done((bf16[72,2688]{1,0:T(8,128)(2,1)S(1)}, bf16[72,2688]{1,0:T(8,128)(2,1)S(1)}, u32[]{:S(2)}, u32[]{:S(2)}) %collective-permute-start.44) | collective-permute-done | bytes 387104 | tf_op jit(solution)/shard_map/ppermute | solution.py:371
  238.7 4.1 %collective-permute-done.45 = bf16[72,2688]{1,0:T(8,128)(2,1)S(1)} collective-permute-done((bf16[72,2688]{1,0:T(8,128)(2,1)S(1)}, bf16[72,2688]{1,0:T(8,128)(2,1)S(1)}, u32[]{:S(2)}, u32[]{:S(2)}) %collective-permute-start.45) | collective-permute-done | bytes 387104 | tf_op jit(solution)/shard_map/ppermute | solution.py:371
  (152 shorter events, 63.0 us)
Async XLA Ops:
  0.0 45.7 %collective-permute-start.12 = (bf16[512,2688]{1,0:T(8,128)(2,1)}, bf16[512,2688]{1,0:T(8,128)(2,1)}, u32[]{:S(2)}, u32[]{:S(2)}) collective-permute-start(bf16[512,2688]{1,0:T(8,128)(2,1)} %rest_4_.5), channel_id=1, source_target_pairs={{0,1},{1,0},{2,3},{3,2},{4,5},{5,4},{6,7},{7,6},{8,9},{9,8},{10,11... | collective-permute-start | bytes 8257544 | tf_op jit(solution)/shard_map/ppermute | solution.py:371
  2.3 14.8 %collective-permute-start = (bf16[128,1536]{1,0:T(8,128)(2,1)S(1)}, bf16[128,1536]{1,0:T(8,128)(2,1)S(1)}, u32[]{:S(2)}, u32[]{:S(2)}) collective-permute-start(bf16[128,1536]{1,0:T(8,128)(2,1)S(1)} %get-tuple-element.93), channel_id=1, source_target_pairs={{0,2},{1,3},{2,0},{3,1},{4,6},{5,7},{6,4},{7,5},{8,10},{9,11},{10,... | collective-permute-start | bytes 1179656 | tf_op jit(solution)/shard_map/ppermute | solution.py:371
  4.9 12.2 %collective-permute-start.2 = (bf16[16,3072]{1,0:T(8,128)(2,1)S(1)}, bf16[16,3072]{1,0:T(8,128)(2,1)S(1)}, u32[]{:S(2)}, u32[]{:S(2)}) collective-permute-start(bf16[16,3072]{1,0:T(8,128)(2,1)S(1)} %get-tuple-element.94), channel_id=1, source_target_pairs={{0,3},{1,0},{2,1},{3,6},{4,7},{5,4},{6,5},{7,10},{8,11},{9,8},{10,... | collective-permute-start | bytes 294920 | tf_op jit(solution)/shard_map/ppermute | solution.py:398
  7.2 9.9 %collective-permute-start.1 = (bf16[16,3072]{1,0:T(8,128)(2,1)S(1)}, bf16[16,3072]{1,0:T(8,128)(2,1)S(1)}, u32[]{:S(2)}, u32[]{:S(2)}) collective-permute-start(bf16[16,3072]{1,0:T(8,128)(2,1)S(1)} %get-tuple-element.94), channel_id=1, source_target_pairs={{0,1},{1,2},{2,3},{3,4},{4,5},{5,6},{6,7},{7,8},{8,9},{9,10},{10,1... | collective-permute-start | bytes 294920 | tf_op jit(solution)/shard_map/ppermute | solution.py:398
  9.4 7.6 %collective-permute-start.3 = (f32[32,128]{1,0:T(8,128)}, f32[32,128]{1,0:T(8,128)S(1)}, u32[]{:S(2)}, u32[]{:S(2)}) collective-permute-start(f32[32,128]{1,0:T(8,128)} %ld_ref.1), channel_id=1, source_target_pairs={{0,2},{1,3},{2,0},{3,1},{4,6},{5,7},{6,4},{7,5},{8,10},{9,11},{10,... | collective-permute-start | bytes 49160 | tf_op jit(solution)/shard_map/ppermute | solution.py:371
  22.4 5.3 %collective-permute-start.5 = (bf16[2,80,256]{2,1,0:T(8,128)(2,1)S(1)}, bf16[2,80,256]{2,1,0:T(8,128)(2,1)S(1)}, u32[]{:S(2)}, u32[]{:S(2)}) collective-permute-start(bf16[2,80,256]{2,1,0:T(8,128)(2,1)S(1)} %get-tuple-element.100), channel_id=1, source_target_pairs={{0,4},{1,5},{2,6},{3,7},{4,0},{5,1},{6,2},{7,3},{8,12},{9,13},{10,... | collective-permute-start | bytes 245768 | tf_op jit(solution)/shard_map/ppermute | solution.py:371
  23.4 5.2 %collective-permute-start.6 = (bf16[2,80,256]{2,1,0:T(8,128)(2,1)S(1)}, bf16[2,80,256]{2,1,0:T(8,128)(2,1)S(1)}, u32[]{:S(2)}, u32[]{:S(2)}) collective-permute-start(bf16[2,80,256]{2,1,0:T(8,128)(2,1)S(1)} %get-tuple-element.101), channel_id=1, source_target_pairs={{0,5},{1,4},{2,7},{3,6},{4,1},{5,0},{6,3},{7,2},{8,13},{9,12},{10,... | collective-permute-start | bytes 245768 | tf_op jit(solution)/shard_map/ppermute | solution.py:371
  31.3 14.4 %collective-permute-start.13 = (bf16[128,1024]{1,0:T(8,128)(2,1)S(1)}, bf16[128,1024]{1,0:T(8,128)(2,1)S(1)}, u32[]{:S(2)}, u32[]{:S(2)}) collective-permute-start(bf16[128,1024]{1,0:T(8,128)(2,1)S(1)} %get-tuple-element.109), channel_id=1, source_target_pairs={{0,2},{1,3},{2,0},{3,1},{4,6},{5,7},{6,4},{7,5},{8,10},{9,11},{10,... | collective-permute-start | bytes 786440 | tf_op jit(solution)/shard_map/ppermute | solution.py:371
  39.6 6.1 %collective-permute-start.9 = (bf16[2,64,256]{2,1,0:T(8,128)(2,1)S(1)}, bf16[2,64,256]{2,1,0:T(8,128)(2,1)S(1)}, u32[]{:S(2)}, u32[]{:S(2)}) collective-permute-start(bf16[2,64,256]{2,1,0:T(8,128)(2,1)S(1)} %get-tuple-element.105), channel_id=1, source_target_pairs={{0,1},{1,0},{2,3},{3,2},{4,5},{5,4},{6,7},{7,6},{8,9},{9,8},{10,11... | collective-permute-start | bytes 196616 | tf_op jit(solution)/shard_map/ppermute | solution.py:371
  39.7 6.0 %collective-permute-start.10 = (bf16[2,64,256]{2,1,0:T(8,128)(2,1)S(1)}, bf16[2,64,256]{2,1,0:T(8,128)(2,1)S(1)}, u32[]{:S(2)}, u32[]{:S(2)}) collective-permute-start(bf16[2,64,256]{2,1,0:T(8,128)(2,1)S(1)} %get-tuple-element.106), channel_id=1, source_target_pairs={{0,4},{1,5},{2,6},{3,7},{4,0},{5,1},{6,2},{7,3},{8,12},{9,13},{10,... | collective-permute-start | bytes 196616 | tf_op jit(solution)/shard_map/ppermute | solution.py:371
  50.3 18.1 %collective-permute-start.14 = (bf16[128,2688]{1,0:T(8,128)(2,1)}, bf16[128,2688]{1,0:T(8,128)(2,1)}, u32[]{:S(2)}, u32[]{:S(2)}) collective-permute-start(bf16[128,2688]{1,0:T(8,128)(2,1)} %shard_map.134), channel_id=1, source_target_pairs={{0,2},{1,3},{2,0},{3,1},{4,6},{5,7},{6,4},{7,5},{8,10},{9,11},{10,... | collective-permute-start | bytes 2064392 | tf_op jit(solution)/shard_map/ppermute | solution.py:371
  70.1 20.3 %collective-permute-start.18 = (bf16[128,2816]{1,0:T(8,128)(2,1)S(1)}, bf16[128,2816]{1,0:T(8,128)(2,1)S(1)}, u32[]{:S(2)}, u32[]{:S(2)}) collective-permute-start(bf16[128,2816]{1,0:T(8,128)(2,1)S(1)} %get-tuple-element.111.block_ref), channel_id=1, source_target_pairs={{0,8},{1,9},{2,10},{3,11},{4,12},{5,13},{6,14},{7,15},{8,16},{9,17... | collective-permute-start | bytes 2162696 | tf_op jit(solution)/shard_map/ppermute | solution.py:379
  73.6 12.0 %collective-permute-start.15 = (bf16[72,2688]{1,0:T(8,128)(2,1)S(1)}, bf16[72,2688]{1,0:T(8,128)(2,1)S(1)}, u32[]{:S(2)}, u32[]{:S(2)}) collective-permute-start(bf16[72,2688]{1,0:T(8,128)(2,1)S(1)} %get-tuple-element.114), channel_id=1, source_target_pairs={{0,2},{1,3},{2,0},{3,1},{4,6},{5,7},{6,4},{7,5},{8,10},{9,11},{10,... | collective-permute-start | bytes 1161224 | tf_op jit(solution)/shard_map/ppermute | solution.py:371
  75.1 18.2 %collective-permute-start.16 = (bf16[72,2688]{1,0:T(8,128)(2,1)S(1)}, bf16[72,2688]{1,0:T(8,128)(2,1)S(1)}, u32[]{:S(2)}, u32[]{:S(2)}) collective-permute-start(bf16[72,2688]{1,0:T(8,128)(2,1)S(1)} %get-tuple-element.115), channel_id=1, source_target_pairs={{0,4},{1,5},{2,6},{3,7},{4,0},{5,1},{6,2},{7,3},{8,12},{9,13},{10,... | collective-permute-start | bytes 1161224 | tf_op jit(solution)/shard_map/ppermute | solution.py:371
  76.5 16.8 %collective-permute-start.17 = (bf16[72,2688]{1,0:T(8,128)(2,1)S(1)}, bf16[72,2688]{1,0:T(8,128)(2,1)S(1)}, u32[]{:S(2)}, u32[]{:S(2)}) collective-permute-start(bf16[72,2688]{1,0:T(8,128)(2,1)S(1)} %get-tuple-element.116), channel_id=1, source_target_pairs={{0,6},{1,7},{2,4},{3,5},{4,2},{5,3},{6,0},{7,1},{8,14},{9,15},{10,... | collective-permute-start | bytes 1161224 | tf_op jit(solution)/shard_map/ppermute | solution.py:371
  94.3 5.2 %collective-permute-start.19 = (bf16[144,2688]{1,0:T(8,128)(2,1)S(1)}, bf16[144,2688]{1,0:T(8,128)(2,1)S(1)}, u32[]{:S(2)}, u32[]{:S(2)}) collective-permute-start(bf16[144,2688]{1,0:T(8,128)(2,1)S(1)} %shard_map.138), channel_id=1, source_target_pairs={{0,1},{1,0},{2,3},{3,2},{4,5},{5,4},{6,7},{7,6},{8,9},{9,8},{10,11... | collective-permute-start | bytes 2322440 | tf_op jit(solution)/shard_map/ppermute | solution.py:371
  94.4 20.3 %collective-permute-start.20 = (bf16[128,2816]{1,0:T(8,128)(2,1)S(1)}, bf16[128,2816]{1,0:T(8,128)(2,1)S(1)}, u32[]{:S(2)}, u32[]{:S(2)}) collective-permute-start(bf16[128,2816]{1,0:T(8,128)(2,1)S(1)} %collective-permute-done.18.block_ref), channel_id=1, source_target_pairs={{0,8},{1,9},{2,10},{3,11},{4,12},{5,13},{6,14},{7,15},{8,16},{9,17... | collective-permute-start | bytes 2162696 | tf_op jit(solution)/shard_map/ppermute | solution.py:379
  96.0 14.0 %collective-permute-start.22 = (bf16[72,2688]{1,0:T(8,128)(2,1)S(1)}, bf16[72,2688]{1,0:T(8,128)(2,1)S(1)}, u32[]{:S(2)}, u32[]{:S(2)}) collective-permute-start(bf16[72,2688]{1,0:T(8,128)(2,1)S(1)} %get-tuple-element.124), channel_id=1, source_target_pairs={{0,2},{1,3},{2,0},{3,1},{4,6},{5,7},{6,4},{7,5},{8,10},{9,11},{10,... | collective-permute-start | bytes 1161224 | tf_op jit(solution)/shard_map/ppermute | solution.py:371
  97.1 18.9 %collective-permute-start.24 = (bf16[72,2688]{1,0:T(8,128)(2,1)S(1)}, bf16[72,2688]{1,0:T(8,128)(2,1)S(1)}, u32[]{:S(2)}, u32[]{:S(2)}) collective-permute-start(bf16[72,2688]{1,0:T(8,128)(2,1)S(1)} %get-tuple-element.128), channel_id=1, source_target_pairs={{0,4},{1,5},{2,6},{3,7},{4,0},{5,1},{6,2},{7,3},{8,12},{9,13},{10,... | collective-permute-start | bytes 1161224 | tf_op jit(solution)/shard_map/ppermute | solution.py:371
  97.9 18.3 %collective-permute-start.25 = (bf16[72,2688]{1,0:T(8,128)(2,1)S(1)}, bf16[72,2688]{1,0:T(8,128)(2,1)S(1)}, u32[]{:S(2)}, u32[]{:S(2)}) collective-permute-start(bf16[72,2688]{1,0:T(8,128)(2,1)S(1)} %get-tuple-element.129), channel_id=1, source_target_pairs={{0,6},{1,7},{2,4},{3,5},{4,2},{5,3},{6,0},{7,1},{8,14},{9,15},{10,... | collective-permute-start | bytes 1161224 | tf_op jit(solution)/shard_map/ppermute | solution.py:371
  117.1 5.5 %collective-permute-start.26 = (bf16[144,2688]{1,0:T(8,128)(2,1)S(1)}, bf16[144,2688]{1,0:T(8,128)(2,1)S(1)}, u32[]{:S(2)}, u32[]{:S(2)}) collective-permute-start(bf16[144,2688]{1,0:T(8,128)(2,1)S(1)} %shard_map.141), channel_id=1, source_target_pairs={{0,1},{1,0},{2,3},{3,2},{4,5},{5,4},{6,7},{7,6},{8,9},{9,8},{10,11... | collective-permute-start | bytes 2322440 | tf_op jit(solution)/shard_map/ppermute | solution.py:371
  117.2 20.3 %collective-permute-start.21 = (bf16[128,2816]{1,0:T(8,128)(2,1)S(1)}, bf16[128,2816]{1,0:T(8,128)(2,1)S(1)}, u32[]{:S(2)}, u32[]{:S(2)}) collective-permute-start(bf16[128,2816]{1,0:T(8,128)(2,1)S(1)} %collective-permute-done.20.block_ref), channel_id=1, source_target_pairs={{0,8},{1,9},{2,10},{3,11},{4,12},{5,13},{6,14},{7,15},{8,16},{9,17... | collective-permute-start | bytes 2162696 | tf_op jit(solution)/shard_map/ppermute | solution.py:379
  119.1 11.8 %collective-permute-start.23 = (bf16[72,2688]{1,0:T(8,128)(2,1)S(1)}, bf16[72,2688]{1,0:T(8,128)(2,1)S(1)}, u32[]{:S(2)}, u32[]{:S(2)}) collective-permute-start(bf16[72,2688]{1,0:T(8,128)(2,1)S(1)} %get-tuple-element.126), channel_id=1, source_target_pairs={{0,2},{1,3},{2,0},{3,1},{4,6},{5,7},{6,4},{7,5},{8,10},{9,11},{10,... | collective-permute-start | bytes 1161224 | tf_op jit(solution)/shard_map/ppermute | solution.py:371
  120.1 19.1 %collective-permute-start.30 = (bf16[72,2688]{1,0:T(8,128)(2,1)S(1)}, bf16[72,2688]{1,0:T(8,128)(2,1)S(1)}, u32[]{:S(2)}, u32[]{:S(2)}) collective-permute-start(bf16[72,2688]{1,0:T(8,128)(2,1)S(1)} %get-tuple-element.142), channel_id=1, source_target_pairs={{0,4},{1,5},{2,6},{3,7},{4,0},{5,1},{6,2},{7,3},{8,12},{9,13},{10,... | collective-permute-start | bytes 1161224 | tf_op jit(solution)/shard_map/ppermute | solution.py:371
  121.5 17.7 %collective-permute-start.31 = (bf16[72,2688]{1,0:T(8,128)(2,1)S(1)}, bf16[72,2688]{1,0:T(8,128)(2,1)S(1)}, u32[]{:S(2)}, u32[]{:S(2)}) collective-permute-start(bf16[72,2688]{1,0:T(8,128)(2,1)S(1)} %get-tuple-element.143), channel_id=1, source_target_pairs={{0,6},{1,7},{2,4},{3,5},{4,2},{5,3},{6,0},{7,1},{8,14},{9,15},{10,... | collective-permute-start | bytes 1161224 | tf_op jit(solution)/shard_map/ppermute | solution.py:371
  128.0 12.2 %collective-permute-start.33 = (bf16[144,2688]{1,0:T(8,128)(2,1)S(1)}, bf16[144,2688]{1,0:T(8,128)(2,1)S(1)}, u32[]{:S(2)}, u32[]{:S(2)}) collective-permute-start(bf16[144,2688]{1,0:T(8,128)(2,1)S(1)} %get-tuple-element.150), channel_id=1, source_target_pairs={{0,1},{1,0},{2,3},{3,2},{4,5},{5,4},{6,7},{7,6},{8,9},{9,8},{10,11... | collective-permute-start | bytes 2322440 | tf_op jit(solution)/shard_map/ppermute | solution.py:371
  140.1 5.8 %collective-permute-start.32 = (bf16[144,2688]{1,0:T(8,128)(2,1)S(1)}, bf16[144,2688]{1,0:T(8,128)(2,1)S(1)}, u32[]{:S(2)}, u32[]{:S(2)}) collective-permute-start(bf16[144,2688]{1,0:T(8,128)(2,1)S(1)} %shard_map.144), channel_id=1, source_target_pairs={{0,1},{1,0},{2,3},{3,2},{4,5},{5,4},{6,7},{7,6},{8,9},{9,8},{10,11... | collective-permute-start | bytes 2322440 | tf_op jit(solution)/shard_map/ppermute | solution.py:371
  141.3 11.8 %collective-permute-start.34 = (bf16[72,2688]{1,0:T(8,128)(2,1)S(1)}, bf16[72,2688]{1,0:T(8,128)(2,1)S(1)}, u32[]{:S(2)}, u32[]{:S(2)}) collective-permute-start(bf16[72,2688]{1,0:T(8,128)(2,1)S(1)} %get-tuple-element.152), channel_id=1, source_target_pairs={{0,2},{1,3},{2,0},{3,1},{4,6},{5,7},{6,4},{7,5},{8,10},{9,11},{10,... | collective-permute-start | bytes 1161224 | tf_op jit(solution)/shard_map/ppermute | solution.py:371
  142.5 20.1 %collective-permute-start.35 = (bf16[72,2688]{1,0:T(8,128)(2,1)S(1)}, bf16[72,2688]{1,0:T(8,128)(2,1)S(1)}, u32[]{:S(2)}, u32[]{:S(2)}) collective-permute-start(bf16[72,2688]{1,0:T(8,128)(2,1)S(1)} %get-tuple-element.153), channel_id=1, source_target_pairs={{0,4},{1,5},{2,6},{3,7},{4,0},{5,1},{6,2},{7,3},{8,12},{9,13},{10,... | collective-permute-start | bytes 1161224 | tf_op jit(solution)/shard_map/ppermute | solution.py:371
  143.4 19.2 %collective-permute-start.36 = (bf16[72,2688]{1,0:T(8,128)(2,1)S(1)}, bf16[72,2688]{1,0:T(8,128)(2,1)S(1)}, u32[]{:S(2)}, u32[]{:S(2)}) collective-permute-start(bf16[72,2688]{1,0:T(8,128)(2,1)S(1)} %get-tuple-element.154), channel_id=1, source_target_pairs={{0,6},{1,7},{2,4},{3,5},{4,2},{5,3},{6,0},{7,1},{8,14},{9,15},{10,... | collective-permute-start | bytes 1161224 | tf_op jit(solution)/shard_map/ppermute | solution.py:371
  144.9 24.9 %collective-permute-start.27 = (bf16[72,2688]{1,0:T(8,128)(2,1)S(1)}, bf16[72,2688]{1,0:T(8,128)(2,1)S(1)}, u32[]{:S(2)}, u32[]{:S(2)}) collective-permute-start(bf16[72,2688]{1,0:T(8,128)(2,1)S(1)} %get-tuple-element.138), channel_id=1, source_target_pairs={{0,2},{1,3},{2,0},{3,1},{4,6},{5,7},{6,4},{7,5},{8,10},{9,11},{10,... | collective-permute-start | bytes 1161224 | tf_op jit(solution)/shard_map/ppermute | solution.py:371
  146.0 24.5 %collective-permute-start.28 = (bf16[72,2688]{1,0:T(8,128)(2,1)S(1)}, bf16[72,2688]{1,0:T(8,128)(2,1)S(1)}, u32[]{:S(2)}, u32[]{:S(2)}) collective-permute-start(bf16[72,2688]{1,0:T(8,128)(2,1)S(1)} %get-tuple-element.139), channel_id=1, source_target_pairs={{0,4},{1,5},{2,6},{3,7},{4,0},{5,1},{6,2},{7,3},{8,12},{9,13},{10,... | collective-permute-start | bytes 1161224 | tf_op jit(solution)/shard_map/ppermute | solution.py:371
  153.2 25.3 %collective-permute-start.29 = (bf16[72,2688]{1,0:T(8,128)(2,1)S(1)}, bf16[72,2688]{1,0:T(8,128)(2,1)S(1)}, u32[]{:S(2)}, u32[]{:S(2)}) collective-permute-start(bf16[72,2688]{1,0:T(8,128)(2,1)S(1)} %get-tuple-element.140), channel_id=1, source_target_pairs={{0,6},{1,7},{2,4},{3,5},{4,2},{5,3},{6,0},{7,1},{8,14},{9,15},{10,... | collective-permute-start | bytes 1161224 | tf_op jit(solution)/shard_map/ppermute | solution.py:371
  162.6 17.3 %collective-permute-start.38 = (bf16[144,2688]{1,0:T(8,128)(2,1)S(1)}, bf16[144,2688]{1,0:T(8,128)(2,1)S(1)}, u32[]{:S(2)}, u32[]{:S(2)}) collective-permute-start(bf16[144,2688]{1,0:T(8,128)(2,1)S(1)} %get-tuple-element.160), channel_id=1, source_target_pairs={{0,1},{1,0},{2,3},{3,2},{4,5},{5,4},{6,7},{7,6},{8,9},{9,8},{10,11... | collective-permute-start | bytes 2322440 | tf_op jit(solution)/shard_map/ppermute | solution.py:371
  179.6 22.0 %collective-permute-start.50 = (bf16[128,2688]{1,0:T(8,128)(2,1)S(1)}, bf16[128,2688]{1,0:T(8,128)(2,1)S(1)}, u32[]{:S(2)}, u32[]{:S(2)}) collective-permute-start(bf16[128,2688]{1,0:T(8,128)(2,1)S(1)} %fusion.1), channel_id=1, source_target_pairs={{0,8},{1,9},{2,10},{3,11},{4,12},{5,13},{6,14},{7,15},{8,16},{9,17... | collective-permute-start | bytes 2064392 | tf_op jit(solution)/shard_map/ppermute | solution.py:379
  181.0 11.9 %collective-permute-start.39 = (bf16[72,2688]{1,0:T(8,128)(2,1)S(1)}, bf16[72,2688]{1,0:T(8,128)(2,1)S(1)}, u32[]{:S(2)}, u32[]{:S(2)}) collective-permute-start(bf16[72,2688]{1,0:T(8,128)(2,1)S(1)} %get-tuple-element.162), channel_id=1, source_target_pairs={{0,2},{1,3},{2,0},{3,1},{4,6},{5,7},{6,4},{7,5},{8,10},{9,11},{10,... | collective-permute-start | bytes 1161224 | tf_op jit(solution)/shard_map/ppermute | solution.py:371
  182.0 19.1 %collective-permute-start.40 = (bf16[72,2688]{1,0:T(8,128)(2,1)S(1)}, bf16[72,2688]{1,0:T(8,128)(2,1)S(1)}, u32[]{:S(2)}, u32[]{:S(2)}) collective-permute-start(bf16[72,2688]{1,0:T(8,128)(2,1)S(1)} %get-tuple-element.163), channel_id=1, source_target_pairs={{0,4},{1,5},{2,6},{3,7},{4,0},{5,1},{6,2},{7,3},{8,12},{9,13},{10,... | collective-permute-start | bytes 1161224 | tf_op jit(solution)/shard_map/ppermute | solution.py:371
  183.3 17.7 %collective-permute-start.41 = (bf16[72,2688]{1,0:T(8,128)(2,1)S(1)}, bf16[72,2688]{1,0:T(8,128)(2,1)S(1)}, u32[]{:S(2)}, u32[]{:S(2)}) collective-permute-start(bf16[72,2688]{1,0:T(8,128)(2,1)S(1)} %get-tuple-element.164), channel_id=1, source_target_pairs={{0,6},{1,7},{2,4},{3,5},{4,2},{5,3},{6,0},{7,1},{8,14},{9,15},{10,... | collective-permute-start | bytes 1161224 | tf_op jit(solution)/shard_map/ppermute | solution.py:371
  189.9 13.3 %collective-permute-start.42 = (bf16[144,2688]{1,0:T(8,128)(2,1)S(1)}, bf16[144,2688]{1,0:T(8,128)(2,1)S(1)}, u32[]{:S(2)}, u32[]{:S(2)}) collective-permute-start(bf16[144,2688]{1,0:T(8,128)(2,1)S(1)} %get-tuple-element.166), channel_id=1, source_target_pairs={{0,1},{1,0},{2,3},{3,2},{4,5},{5,4},{6,7},{7,6},{8,9},{9,8},{10,11... | collective-permute-start | bytes 2322440 | tf_op jit(solution)/shard_map/ppermute | solution.py:371
  201.7 18.6 %collective-permute-start.51 = (bf16[128,2688]{1,0:T(8,128)(2,1)S(1)}, bf16[128,2688]{1,0:T(8,128)(2,1)S(1)}, u32[]{:S(2)}, u32[]{:S(2)}) collective-permute-start(bf16[128,2688]{1,0:T(8,128)(2,1)S(1)} %add_convert_fusion.1), channel_id=1, source_target_pairs={{0,8},{1,9},{2,10},{3,11},{4,12},{5,13},{6,14},{7,15},{8,16},{9,17... | collective-permute-start | bytes 2064392 | tf_op jit(solution)/shard_map/ppermute | solution.py:379
  204.3 16.1 %collective-permute-start.47 = (bf16[72,2688]{1,0:T(8,128)(2,1)S(1)}, bf16[72,2688]{1,0:T(8,128)(2,1)S(1)}, u32[]{:S(2)}, u32[]{:S(2)}) collective-permute-start(bf16[72,2688]{1,0:T(8,128)(2,1)S(1)} %get-tuple-element.174), channel_id=1, source_target_pairs={{0,2},{1,3},{2,0},{3,1},{4,6},{5,7},{6,4},{7,5},{8,10},{9,11},{10,... | collective-permute-start | bytes 1161224 | tf_op jit(solution)/shard_map/ppermute | solution.py:371
  205.5 17.9 %collective-permute-start.48 = (bf16[72,2688]{1,0:T(8,128)(2,1)S(1)}, bf16[72,2688]{1,0:T(8,128)(2,1)S(1)}, u32[]{:S(2)}, u32[]{:S(2)}) collective-permute-start(bf16[72,2688]{1,0:T(8,128)(2,1)S(1)} %get-tuple-element.175), channel_id=1, source_target_pairs={{0,4},{1,5},{2,6},{3,7},{4,0},{5,1},{6,2},{7,3},{8,12},{9,13},{10,... | collective-permute-start | bytes 1161224 | tf_op jit(solution)/shard_map/ppermute | solution.py:371
  206.3 17.1 %collective-permute-start.49 = (bf16[72,2688]{1,0:T(8,128)(2,1)S(1)}, bf16[72,2688]{1,0:T(8,128)(2,1)S(1)}, u32[]{:S(2)}, u32[]{:S(2)}) collective-permute-start(bf16[72,2688]{1,0:T(8,128)(2,1)S(1)} %get-tuple-element.176), channel_id=1, source_target_pairs={{0,6},{1,7},{2,4},{3,5},{4,2},{5,3},{6,0},{7,1},{8,14},{9,15},{10,... | collective-permute-start | bytes 1161224 | tf_op jit(solution)/shard_map/ppermute | solution.py:371
  207.9 17.8 %collective-permute-start.43 = (bf16[144,2688]{1,0:T(8,128)(2,1)S(1)}, bf16[144,2688]{1,0:T(8,128)(2,1)S(1)}, u32[]{:S(2)}, u32[]{:S(2)}) collective-permute-start(bf16[144,2688]{1,0:T(8,128)(2,1)S(1)} %get-tuple-element.169), channel_id=1, source_target_pairs={{0,1},{1,0},{2,3},{3,2},{4,5},{5,4},{6,7},{7,6},{8,9},{9,8},{10,11... | collective-permute-start | bytes 2322440 | tf_op jit(solution)/shard_map/ppermute | solution.py:371
  224.0 19.9 %collective-permute-start.52 = (bf16[128,2688]{1,0:T(8,128)(2,1)S(1)}, bf16[128,2688]{1,0:T(8,128)(2,1)S(1)}, u32[]{:S(2)}, u32[]{:S(2)}) collective-permute-start(bf16[128,2688]{1,0:T(8,128)(2,1)S(1)} %fusion), channel_id=1, source_target_pairs={{0,8},{1,9},{2,10},{3,11},{4,12},{5,13},{6,14},{7,15},{8,16},{9,17... | collective-permute-start | bytes 2064392 | tf_op jit(solution)/shard_map/ppermute | solution.py:379
  226.7 12.0 %collective-permute-start.44 = (bf16[72,2688]{1,0:T(8,128)(2,1)S(1)}, bf16[72,2688]{1,0:T(8,128)(2,1)S(1)}, u32[]{:S(2)}, u32[]{:S(2)}) collective-permute-start(bf16[72,2688]{1,0:T(8,128)(2,1)S(1)} %get-tuple-element.171), channel_id=1, source_target_pairs={{0,2},{1,3},{2,0},{3,1},{4,6},{5,7},{6,4},{7,5},{8,10},{9,11},{10,... | collective-permute-start | bytes 1161224 | tf_op jit(solution)/shard_map/ppermute | solution.py:371
  227.7 15.1 %collective-permute-start.45 = (bf16[72,2688]{1,0:T(8,128)(2,1)S(1)}, bf16[72,2688]{1,0:T(8,128)(2,1)S(1)}, u32[]{:S(2)}, u32[]{:S(2)}) collective-permute-start(bf16[72,2688]{1,0:T(8,128)(2,1)S(1)} %get-tuple-element.172), channel_id=1, source_target_pairs={{0,4},{1,5},{2,6},{3,7},{4,0},{5,1},{6,2},{7,3},{8,12},{9,13},{10,... | collective-permute-start | bytes 1161224 | tf_op jit(solution)/shard_map/ppermute | solution.py:371
  228.6 15.3 %collective-permute-start.46 = (bf16[72,2688]{1,0:T(8,128)(2,1)S(1)}, bf16[72,2688]{1,0:T(8,128)(2,1)S(1)}, u32[]{:S(2)}, u32[]{:S(2)}) collective-permute-start(bf16[72,2688]{1,0:T(8,128)(2,1)S(1)} %get-tuple-element.173), channel_id=1, source_target_pairs={{0,6},{1,7},{2,4},{3,5},{4,2},{5,3},{6,0},{7,1},{8,14},{9,15},{10,... | collective-permute-start | bytes 1161224 | tf_op jit(solution)/shard_map/ppermute | solution.py:371
  (31 other events, 418.9 us)
where the time goes:
time: 246 us; the launch traced here: 245 us
  waiting for transfers between devices  111 us (45%)
  starting transfers between devices  59.4 us (24%)
  Pallas kernels  52.7 us (21%)
  local copies, waits for them, and re-layouts  15.7 us (6%)
  matrix products  3.85 us (2%)
    ppermute x45, waiting for transfers between devices, swap(): return lax.ppermute(x, AXES, [(d, d ^ m) for d in range(devices)])  82.4 us
    pallas_call x25, Pallas kernels, kernel_call(): pl.pallas_call(kernel, out_shape=outs, in_specs=([smem] if scalars else [...  52.7 us
    ppermute x45, starting transfers between devices, swap(): return lax.ppermute(x, AXES, [(d, d ^ m) for d in range(devices)])  45.8 us
    ppermute x6, waiting for transfers between devices, turn(): lax.ppermute(x, AXES, [(d, (d + plane) % devices) for d in range(devices)])  28.6 us
    unnamed x52, local copies, waits for them, and re-layouts  13 us
    ppermute x6, starting transfers between devices, turn(): lax.ppermute(x, AXES, [(d, (d + plane) % devices) for d in range(devices)])  9.11 us
  transfers between devices with their start and end apart: 53, of which 26 were waited for; matrix products, arithmetic and copies ran while one was open for 3% of the time, Pallas kernels for 18%

commit v1 on v0

--- a/solution.py
+++ b/solution.py
@@ -84,11 +84,22 @@
     )
 
 
-def start_kernel(members, blocks, at_ref, cw_ref, z_ref, *rest):
+def prepare_kernel(blocks, inner, width, at_ref, cw_ref, ld_ref, z_ref, cw_out, ld_out, *z_outs):
+    half = at_ref[1]
+    keys = (cw_ref.shape[1] - inner) // 2
+    ld_out[...] = ld_ref[...]
+    for c in range(0, cw_out.shape[1], width):
+        cw_out[:, c : c + width] = cw_ref[:, columns(blocks, inner, keys, c, width, half)]
+    for b in range(1, blocks):
+        for c in range(0, inner // blocks, width):
+            at = pl.ds(pl.multiple_of((half ^ b) * (inner // blocks) + c, width), width)
+            z_outs[b - 1][:, c : c + width] = z_ref[:, at]
+
+
+def start_kernel(members, blocks, at_ref, cw_ref, *rest):
     xs, prevs, lds = rest[:blocks], rest[blocks : 2 * blocks], rest[2 * blocks : 3 * blocks]
     rest = rest[3 * blocks :]
     acts, outs, scr = rest[:blocks], rest[blocks : blocks + members], rest[-1]
-    z_outs = rest[blocks + members : -1]
     member, half = at_ref[0], at_ref[1]
     length = xs[0].shape[0]
     channels = xs[0].shape[1] // blocks
@@ -112,9 +123,9 @@
                 [prevs[b][:, at], xs[b][:, cols if b else at]], axis=0
             ).astype(f32)
             first = halo - taps + 1
-            total = cw_ref[0:1, at] * padded[first : first + length]
+            total = cw_ref[0:1, cols] * padded[first : first + length]
             for k in range(1, taps):
-                total = total + cw_ref[k : k + 1, at] * padded[first + k : first + k + length]
+                total = total + cw_ref[k : k + 1, cols] * padded[first + k : first + k + length]
             act_ref[:, cols] = silu(total).astype(bf16)
         slot = half ^ b
         for g in range(count):
@@ -128,10 +139,6 @@
             )
     for m in range(members):
         outs[m][...] = scr[member ^ m]
-    for b in range(1, blocks):
-        for c in range(0, inner, width):
-            at = pl.ds(pl.multiple_of((half ^ b) * inner + c, width), width)
-            z_outs[b - 1][:, c : c + width] = z_ref[:, at]
 
 
 def in_order(members, blocks, member, chunks, scr):
@@ -420,11 +427,17 @@
         [shapes((halo, channels), bf16)] + [shapes((length, wide), bf16)] * (blocks - 1),
     )
     tail = picked[0]
-    xs, prevs, lds = [conv_input], [onward_to(tail, 1, 0)], [log_decay]
+    prepared = kernel_call(
+        functools.partial(prepare_kernel, blocks, inner, width),
+        [at_member, conv_weight, log_decay, z_stream],
+        [shapes((conv_weight.shape[0], wide), f32), shapes(log_decay.shape, f32)]
+        + [shapes((length, inner // blocks), bf16)] * (blocks - 1),
+    )
+    xs, prevs, lds = [conv_input], [onward_to(tail, 1, 0)], [prepared[1]]
     for b in range(1, blocks):
         xs.append(swap(picked[b], 2 * b))
         prevs.append(onward_to(tail, 1, 2 * b))
-        lds.append(swap(log_decay, 2 * b))
+        lds.append(swap(prepared[1], 2 * b))
 
     rows_own = out_weight
     rows_pair = swap(out_weight, 1)
@@ -432,17 +445,16 @@
 
     first = kernel_call(
         functools.partial(start_kernel, members, blocks),
-        [at_member, conv_weight, z_stream] + xs + prevs + lds,
+        [at_member, prepared[0]] + xs + prevs + lds,
         [shapes((length, wide), bf16)] * blocks
-        + [shapes((blocks,) + chunk, bf16)] * members
-        + [shapes((length, inner // blocks), bf16)] * (blocks - 1),
+        + [shapes((blocks,) + chunk, bf16)] * members,
         [pltpu.VMEM((count, blocks) + chunk, bf16)],
         50000000,
         8000000,
     )
     acts = first[:blocks]
     sends = first[blocks : blocks + members]
-    zs = [z_stream] + [swap(first[blocks + members + b - 1], 2 * b) for b in range(1, blocks)]
+    zs = [z_stream] + [swap(prepared[1 + b], 2 * b) for b in range(1, blocks)]
     mask = [(m >> 1) * n_grp + (m & 1) for m in range(members)]
     chunks = [sends[0]] + [swap(sends[m], mask[m]) for m in range(1, members)]
     inside = kernel_call(

time: 246 us -> 243 us (0.988)
  waiting for transfers between devices: 111 us -> 108 us
    ppermute x45, waiting for transfers between devices: 82.4 us -> 79.5 us  [swap(): return lax.ppermute(x, AXES, [(d, d ^ m) for d in range(devices)])]
    pallas_call x25 -> x26, Pallas kernels: 52.7 us -> 53.3 us  [kernel_call(): pl.pallas_call(kernel, out_shape=outs, in_specs=([smem] if scalars else [...]
  transfers between devices with their start and end apart: 53 -> 53, of which waited for: 26 -> 26; matrix products, arithmetic and copies ran while one was open for 3% -> 3% of each run, Pallas kernels for 18% -> 19%
where the time goes in v1:
time: 243 us
  waiting for transfers between devices  108 us (44%)
  starting transfers between devices  59.2 us (24%)
  Pallas kernels  53.3 us (22%)
  local copies, waits for them, and re-layouts  15.8 us (7%)
  matrix products  3.85 us (2%)
    ppermute x45, waiting for transfers between devices, swap(): return lax.ppermute(x, AXES, [(d, d ^ m) for d in range(devices)])  79.5 us
    pallas_call x26, Pallas kernels, kernel_call(): pl.pallas_call(kernel, out_shape=outs, in_specs=([smem] if scalars else [...  53.3 us
    ppermute x45, starting transfers between devices, swap(): return lax.ppermute(x, AXES, [(d, d ^ m) for d in range(devices)])  45.7 us
    ppermute x6, waiting for transfers between devices, turn(): lax.ppermute(x, AXES, [(d, (d + plane) % devices) for d in range(devices)])  28.6 us
    unnamed x52, local copies, waits for them, and re-layouts  13 us
    ppermute x6, starting transfers between devices, turn(): lax.ppermute(x, AXES, [(d, (d + plane) % devices) for d in range(devices)])  9.14 us
  transfers between devices with their start and end apart: 53, of which 26 were waited for; matrix products, arithmetic and copies ran while one was open for 3% of the time, Pallas kernels for 19%

profile of v1, /device:TPU:0, one launch (start us, length us, event | category | flops | bytes accessed | tf_op | source)
XLA Modules:
  0.0 242.8 jit_solution(11798111174533739920)
XLA Ops:
  2.3 2.6 %collective-permute-start = (bf16[128,1536]{1,0:T(8,128)(2,1)S(1)}, bf16[128,1536]{1,0:T(8,128)(2,1)S(1)}, u32[]{:S(2)}, u32[]{:S(2)}) collective-permute-start(bf16[128,1536]{1,0:T(8,128)(2,1)S(1)} %get-tuple-element.96), channel_id=1, source_target_pairs={{0,2},{1,3},{2,0},{3,1},{4,6},{5,7},{6,4},{7,5},{8,10},{9,11},{10,... | collective-permute-start | bytes 1179656 | tf_op jit(solution)/shard_map/ppermute | solution.py:378
  4.8 2.0 collective-permute-start.2
  6.9 2.3 collective-permute-start.1
  12.3 1.7 collective-permute-start.3
  14.0 3.0 %collective-permute-done.3.rest_5_.refs_3_.ld_ref = f32[32,128]{1,0:T(8,128)S(1)} collective-permute-done((f32[32,128]{1,0:T(8,128)S(1)}, f32[32,128]{1,0:T(8,128)S(1)}, u32[]{:S(2)}, u32[]{:S(2)}) %collective-permute-start.3) | collective-permute-done | bytes 16416 | tf_op jit(solution)/shard_map/ppermute | solution.py:378
  17.1 2.7 %shard_map.129 = (bf16[128,1536]{1,0:T(8,128)(2,1)S(1)}, bf16[128,1536]{1,0:T(8,128)(2,1)S(1)}, bf16[2,80,256]{2,1,0:T(8,128)(2,1)S(1)}, bf16[2,80,256]{2,1,0:T(...) custom-call(s32[4]{0:T(128)S(1)} %pad_add_fusion.at_ref, ...), custom_call_target="tpu_custom_call" | custom-call | flops 50000000 | bytes 8000000 | tf_op jit(solution)/shard_map/pallas_call | solution.py:415
  21.8 3.4 %collective-permute-done.5.rest_2_ = bf16[2,80,256]{2,1,0:T(8,128)(2,1)S(1)} collective-permute-done((bf16[2,80,256]{2,1,0:T(8,128)(2,1)S(1)}, bf16[2,80,256]{2,1,0:T(8,128)(2,1)S(1)}, u32[]{:S(2)}, u32[]{:S(2)}) %collective-permute-start.5) | collective-permute-done | bytes 81952 | tf_op jit(solution)/shard_map/ppermute | solution.py:378
  26.7 2.0 collective-permute-start.7
  28.8 1.5 collective-permute-start.13
  31.4 3.1 %collective-permute-start.8 = (bf16[80,256]{1,0:T(8,128)(2,1)S(1)}, bf16[80,256]{1,0:T(8,128)(2,1)S(1)}, u32[]{:S(2)}, u32[]{:S(2)}) collective-permute-start(bf16[80,256]{1,0:T(8,128)(2,1)S(1)} %shard_map.132), channel_id=1, source_target_pairs={{0,16},{1,17},{2,18},{3,19},{4,20},{5,21},{6,22},{7,23},{8,24},{9,... | collective-permute-start | bytes 122888 | tf_op jit(solution)/shard_map/ppermute | solution.py:378
  34.5 1.9 collective-permute-done.8.rest_1_
  39.6 2.7 %shard_map.130 = (f32[128,1024]{1,0:T(8,128)S(1)}, f32[128,1024]{1,0:T(8,128)S(1)}) custom-call(s32[4]{0:T(128)S(1)} %pad_add_fusion.at_ref, bf16[128,1536]{1,0:T(8,128)(2,1)S(1)} %get-tuple-element.99.refs_0_.act_ref, bf16[128,1536]{1,0:T(8,128)(2,1)S(1)} %get-tuple-element.100.refs_1_.act_ref, f32[32,128]{1,0:T(8,128)S(1)} %get-tuple-element.98.rest_4_.refs_2_.ld_ref, ...), custom_call_target="tpu_custom_call" | custom-call | flops 100000000 | bytes 15000000 | tf_op jit(solution)/shard_map/pallas_call | solution.py:415
  43.2 4.6 %shard_map.135 = bf16[128,2688]{1,0:T(8,128)(2,1)} custom-call(s32[4]{0:T(128)S(1)} %pad_add_fusion.at_ref, f32[1,2048]{1,0:T(1,128)S(1)} %bitcast.24, bf16[128,1536]{1,0:T(8,128)(2,1)S(1)} %get-tuple-element.100.refs_1_.act_ref, f32[32,128]{1,0:T(8,128)S(1)} %collective-permute-done.3.rest_5_.refs_3_.ld_ref, f32[128,1024]{1,0:T(8,128)S(1)} %get-tuple-element.112.inside_ref, ...), custom_call_target="tpu_custom_call" | custom-call | flops 800000000 | bytes 8000000 | tf_op jit(solution)/shard_map/pallas_call | solution.py:415
  47.8 1.8 collective-permute-start.14
  57.6 3.7 %shard_map.134.own_ref = f32[128,2688]{1,0:T(8,128)S(1)} custom-call(s32[4]{0:T(128)S(1)} %copy-done.13, f32[1,2048]{1,0:T(1,128)S(1)} %bitcast.25, bf16[128,1536]{1,0:T(8,128)(2,1)S(1)} %copy-done.8, f32[32,128]{1,0:T(8,128)S(1)} %get-tuple-element.98.rest_4_.refs_2_.ld_ref, f32[128,1024]{1,0:T(8,128)S(1)} %copy-done.11, bf16[128,2048]{1,0:T(8,128)(2,1)S(1)} %copy-done.6, ...), custom_call_target="tpu_custom_call" | custom-call | flops 800000000 | bytes 8000000 | tf_op jit(solution)/shard_map/pallas_call | solution.py:415
  61.3 4.6 %collective-permute-done.14.rest_0_ = bf16[128,2688]{1,0:T(8,128)(2,1)} collective-permute-done((bf16[128,2688]{1,0:T(8,128)(2,1)}, bf16[128,2688]{1,0:T(8,128)(2,1)}, u32[]{:S(2)}, u32[]{:S(2)}) %collective-permute-start.14) | collective-permute-done | bytes 688160 | tf_op jit(solution)/shard_map/ppermute | solution.py:378
  65.9 1.7 shard_map.136
  67.6 2.1 collective-permute-start.18
  71.0 1.6 collective-permute-start.15
  74.6 8.4 %collective-permute-done.15.refs_1_ = bf16[72,2688]{1,0:T(8,128)(2,1)S(1)} collective-permute-done((bf16[72,2688]{1,0:T(8,128)(2,1)S(1)}, bf16[72,2688]{1,0:T(8,128)(2,1)S(1)}, u32[]{:S(2)}, u32[]{:S(2)}) %collective-permute-start.15) | collective-permute-done | bytes 387104 | tf_op jit(solution)/shard_map/ppermute | solution.py:378
  83.0 4.8 %collective-permute-done.18.block_ref = bf16[128,2816]{1,0:T(8,128)(2,1)S(1)} collective-permute-done((bf16[128,2816]{1,0:T(8,128)(2,1)S(1)}, bf16[128,2816]{1,0:T(8,128)(2,1)S(1)}, u32[]{:S(2)}, u32[]{:S(2)}) %collective-permute-start.18) | collective-permute-done | bytes 720928 | tf_op jit(solution)/shard_map/ppermute | solution.py:386
  89.1 1.6 collective-permute-done.16.refs_2_
  91.8 1.6 collective-permute-start.20
  95.4 1.6 collective-permute-start.25
  97.0 2.6 %copy-done = bf16[1,2688,1024]{2,1,0:T(8,128)(2,1)S(1)} copy-done((bf16[1,2688,1024]{2,1,0:T(8,128)(2,1)S(1)}, bf16[1,2688,1024]{2,1,0:T(8,128)(2,1)}, u32[]{:S(2)}) %copy-start) | copy-done | bytes 5505048
  99.5 2.6 %copy-done.1 = bf16[1,1024,2688]{2,1,0:T(8,128)(2,1)S(1)} copy-done((bf16[1,1024,2688]{2,1,0:T(8,128)(2,1)S(1)}, bf16[1,1024,2688]{2,1,0:T(8,128)(2,1)}, u32[]{:S(2)}) %copy-start.1) | copy-done | bytes 5505048
  102.1 5.4 %shard_map.140 = (bf16[144,2688]{1,0:T(8,128)(2,1)S(1)}, bf16[144,2688]{1,0:T(8,128)(2,1)S(1)}) custom-call(bf16[72,2688]{1,0:T(8,128)(2,1)S(1)} %get-tuple-element.123.refs_0_, bf16[72,2688]{1,0:T(8,128)(2,1)S(1)} %collective-permute-done.15.refs_1_, bf16[72,2688]{1,0:T(8,128)(2,1)S(1)} %collective-permute-done.16.refs_2_, ...), custom_call_target="tpu_custom_call" | custom-call | tf_op jit(solution)/shard_map/pallas_call | solution.py:415
  107.5 4.7 %collective-permute-done.20.block_ref = bf16[128,2816]{1,0:T(8,128)(2,1)S(1)} collective-permute-done((bf16[128,2816]{1,0:T(8,128)(2,1)S(1)}, bf16[128,2816]{1,0:T(8,128)(2,1)S(1)}, u32[]{:S(2)}, u32[]{:S(2)}) %collective-permute-start.20) | collective-permute-done | bytes 720928 | tf_op jit(solution)/shard_map/ppermute | solution.py:386
  114.7 1.9 collective-permute-start.21
  120.1 5.4 %shard_map.143 = (bf16[144,2688]{1,0:T(8,128)(2,1)S(1)}, bf16[144,2688]{1,0:T(8,128)(2,1)S(1)}) custom-call(bf16[72,2688]{1,0:T(8,128)(2,1)S(1)} %get-tuple-element.135.refs_0_, bf16[72,2688]{1,0:T(8,128)(2,1)S(1)} %collective-permute-done.22.refs_1_, bf16[72,2688]{1,0:T(8,128)(2,1)S(1)} %collective-permute-done.24.refs_2_, ...), custom_call_target="tpu_custom_call" | custom-call | tf_op jit(solution)/shard_map/pallas_call | solution.py:415
  125.6 2.9 %collective-permute-done.23.refs_1_ = bf16[72,2688]{1,0:T(8,128)(2,1)S(1)} collective-permute-done((bf16[72,2688]{1,0:T(8,128)(2,1)S(1)}, bf16[72,2688]{1,0:T(8,128)(2,1)S(1)}, u32[]{:S(2)}, u32[]{:S(2)}) %collective-permute-start.23) | collective-permute-done | bytes 387104 | tf_op jit(solution)/shard_map/ppermute | solution.py:378
  128.4 6.6 %collective-permute-done.21.block_ref = bf16[128,2816]{1,0:T(8,128)(2,1)S(1)} collective-permute-done((bf16[128,2816]{1,0:T(8,128)(2,1)S(1)}, bf16[128,2816]{1,0:T(8,128)(2,1)S(1)}, u32[]{:S(2)}, u32[]{:S(2)}) %collective-permute-start.21) | collective-permute-done | bytes 720928 | tf_op jit(solution)/shard_map/ppermute | solution.py:386
  144.4 6.2 %collective-permute-done.34 = bf16[72,2688]{1,0:T(8,128)(2,1)S(1)} collective-permute-done((bf16[72,2688]{1,0:T(8,128)(2,1)S(1)}, bf16[72,2688]{1,0:T(8,128)(2,1)S(1)}, u32[]{:S(2)}, u32[]{:S(2)}) %collective-permute-start.34) | collective-permute-done | bytes 387104 | tf_op jit(solution)/shard_map/ppermute | solution.py:378
  150.6 1.5 collective-permute-start.29
  152.1 5.4 %shard_map.146 = (bf16[144,2688]{1,0:T(8,128)(2,1)S(1)}, bf16[144,2688]{1,0:T(8,128)(2,1)S(1)}) custom-call(bf16[72,2688]{1,0:T(8,128)(2,1)S(1)} %get-tuple-element.149.refs_0_, bf16[72,2688]{1,0:T(8,128)(2,1)S(1)} %collective-permute-done.23.refs_1_, bf16[72,2688]{1,0:T(8,128)(2,1)S(1)} %collective-permute-done.30.refs_2_, ...), custom_call_target="tpu_custom_call" | custom-call | tf_op jit(solution)/shard_map/pallas_call | solution.py:415
  157.5 2.6 %collective-permute-done.35 = bf16[72,2688]{1,0:T(8,128)(2,1)S(1)} collective-permute-done((bf16[72,2688]{1,0:T(8,128)(2,1)S(1)}, bf16[72,2688]{1,0:T(8,128)(2,1)S(1)}, u32[]{:S(2)}, u32[]{:S(2)}) %collective-permute-start.35) | collective-permute-done | bytes 387104 | tf_op jit(solution)/shard_map/ppermute | solution.py:378
  160.6 6.7 %collective-permute-done.27.refs_1_ = bf16[72,2688]{1,0:T(8,128)(2,1)S(1)} collective-permute-done((bf16[72,2688]{1,0:T(8,128)(2,1)S(1)}, bf16[72,2688]{1,0:T(8,128)(2,1)S(1)}, u32[]{:S(2)}, u32[]{:S(2)}) %collective-permute-start.27) | collective-permute-done | bytes 387104 | tf_op jit(solution)/shard_map/ppermute | solution.py:378
  168.0 8.0 %collective-permute-done.29.refs_3_ = bf16[72,2688]{1,0:T(8,128)(2,1)S(1)} collective-permute-done((bf16[72,2688]{1,0:T(8,128)(2,1)S(1)}, bf16[72,2688]{1,0:T(8,128)(2,1)S(1)}, u32[]{:S(2)}, u32[]{:S(2)}) %collective-permute-start.29) | collective-permute-done | bytes 387104 | tf_op jit(solution)/shard_map/ppermute | solution.py:378
  182.0 5.4 %shard_map.149 = (bf16[144,2688]{1,0:T(8,128)(2,1)S(1)}, bf16[144,2688]{1,0:T(8,128)(2,1)S(1)}) custom-call(bf16[72,2688]{1,0:T(8,128)(2,1)S(1)} %get-tuple-element.159.refs_0_, bf16[72,2688]{1,0:T(8,128)(2,1)S(1)} %collective-permute-done.27.refs_1_, bf16[72,2688]{1,0:T(8,128)(2,1)S(1)} %collective-permute-done.28.refs_2_, ...), custom_call_target="tpu_custom_call" | custom-call | tf_op jit(solution)/shard_map/pallas_call | solution.py:415
  187.5 2.9 %collective-permute-done.39 = bf16[72,2688]{1,0:T(8,128)(2,1)S(1)} collective-permute-done((bf16[72,2688]{1,0:T(8,128)(2,1)S(1)}, bf16[72,2688]{1,0:T(8,128)(2,1)S(1)}, u32[]{:S(2)}, u32[]{:S(2)}) %collective-permute-start.39) | collective-permute-done | bytes 387104 | tf_op jit(solution)/shard_map/ppermute | solution.py:378
  190.4 8.1 %collective-permute-done.40 = bf16[72,2688]{1,0:T(8,128)(2,1)S(1)} collective-permute-done((bf16[72,2688]{1,0:T(8,128)(2,1)S(1)}, bf16[72,2688]{1,0:T(8,128)(2,1)S(1)}, u32[]{:S(2)}, u32[]{:S(2)}) %collective-permute-start.40) | collective-permute-done | bytes 387104 | tf_op jit(solution)/shard_map/ppermute | solution.py:378
  203.8 1.6 collective-permute-start.49
  205.3 12.5 %collective-permute-done.51 = bf16[128,2688]{1,0:T(8,128)(2,1)S(1)} collective-permute-done((bf16[128,2688]{1,0:T(8,128)(2,1)S(1)}, bf16[128,2688]{1,0:T(8,128)(2,1)S(1)}, u32[]{:S(2)}, u32[]{:S(2)}) %collective-permute-start.51) | collective-permute-done | bytes 688160 | tf_op jit(solution)/shard_map/ppermute | solution.py:386
  217.8 3.0 %collective-permute-done.48 = bf16[72,2688]{1,0:T(8,128)(2,1)S(1)} collective-permute-done((bf16[72,2688]{1,0:T(8,128)(2,1)S(1)}, bf16[72,2688]{1,0:T(8,128)(2,1)S(1)}, u32[]{:S(2)}, u32[]{:S(2)}) %collective-permute-start.48) | collective-permute-done | bytes 387104 | tf_op jit(solution)/shard_map/ppermute | solution.py:378
  221.4 1.7 collective-permute-start.52
  226.1 1.7 collective-permute-start.46
  227.8 8.4 %collective-permute-done.44 = bf16[72,2688]{1,0:T(8,128)(2,1)S(1)} collective-permute-done((bf16[72,2688]{1,0:T(8,128)(2,1)S(1)}, bf16[72,2688]{1,0:T(8,128)(2,1)S(1)}, u32[]{:S(2)}, u32[]{:S(2)}) %collective-permute-start.44) | collective-permute-done | bytes 387104 | tf_op jit(solution)/shard_map/ppermute | solution.py:378
  236.2 4.1 %collective-permute-done.45 = bf16[72,2688]{1,0:T(8,128)(2,1)S(1)} collective-permute-done((bf16[72,2688]{1,0:T(8,128)(2,1)S(1)}, bf16[72,2688]{1,0:T(8,128)(2,1)S(1)}, u32[]{:S(2)}, u32[]{:S(2)}) %collective-permute-start.45) | collective-permute-done | bytes 387104 | tf_op jit(solution)/shard_map/ppermute | solution.py:378
  (153 shorter events, 63.7 us)
Async XLA Ops:
  0.0 43.2 %collective-permute-start.12 = (bf16[512,2688]{1,0:T(8,128)(2,1)}, bf16[512,2688]{1,0:T(8,128)(2,1)}, u32[]{:S(2)}, u32[]{:S(2)}) collective-permute-start(bf16[512,2688]{1,0:T(8,128)(2,1)} %rest_4_.3), channel_id=1, source_target_pairs={{0,1},{1,0},{2,3},{3,2},{4,5},{5,4},{6,7},{7,6},{8,9},{9,8},{10,11... | collective-permute-start | bytes 8257544 | tf_op jit(solution)/shard_map/ppermute | solution.py:378
  2.3 14.8 %collective-permute-start = (bf16[128,1536]{1,0:T(8,128)(2,1)S(1)}, bf16[128,1536]{1,0:T(8,128)(2,1)S(1)}, u32[]{:S(2)}, u32[]{:S(2)}) collective-permute-start(bf16[128,1536]{1,0:T(8,128)(2,1)S(1)} %get-tuple-element.96), channel_id=1, source_target_pairs={{0,2},{1,3},{2,0},{3,1},{4,6},{5,7},{6,4},{7,5},{8,10},{9,11},{10,... | collective-permute-start | bytes 1179656 | tf_op jit(solution)/shard_map/ppermute | solution.py:378
  4.8 12.2 %collective-permute-start.2 = (bf16[16,3072]{1,0:T(8,128)(2,1)S(1)}, bf16[16,3072]{1,0:T(8,128)(2,1)S(1)}, u32[]{:S(2)}, u32[]{:S(2)}) collective-permute-start(bf16[16,3072]{1,0:T(8,128)(2,1)S(1)} %get-tuple-element.97), channel_id=1, source_target_pairs={{0,3},{1,0},{2,1},{3,6},{4,7},{5,4},{6,5},{7,10},{8,11},{9,8},{10,... | collective-permute-start | bytes 294920 | tf_op jit(solution)/shard_map/ppermute | solution.py:405
  6.9 10.2 %collective-permute-start.1 = (bf16[16,3072]{1,0:T(8,128)(2,1)S(1)}, bf16[16,3072]{1,0:T(8,128)(2,1)S(1)}, u32[]{:S(2)}, u32[]{:S(2)}) collective-permute-start(bf16[16,3072]{1,0:T(8,128)(2,1)S(1)} %get-tuple-element.97), channel_id=1, source_target_pairs={{0,1},{1,2},{2,3},{3,4},{4,5},{5,6},{6,7},{7,8},{8,9},{9,10},{10,1... | collective-permute-start | bytes 294920 | tf_op jit(solution)/shard_map/ppermute | solution.py:405
  19.9 5.3 %collective-permute-start.5 = (bf16[2,80,256]{2,1,0:T(8,128)(2,1)S(1)}, bf16[2,80,256]{2,1,0:T(8,128)(2,1)S(1)}, u32[]{:S(2)}, u32[]{:S(2)}) collective-permute-start(bf16[2,80,256]{2,1,0:T(8,128)(2,1)S(1)} %get-tuple-element.104), channel_id=1, source_target_pairs={{0,4},{1,5},{2,6},{3,7},{4,0},{5,1},{6,2},{7,3},{8,12},{9,13},{10,... | collective-permute-start | bytes 245768 | tf_op jit(solution)/shard_map/ppermute | solution.py:378
  20.9 5.1 %collective-permute-start.6 = (bf16[2,80,256]{2,1,0:T(8,128)(2,1)S(1)}, bf16[2,80,256]{2,1,0:T(8,128)(2,1)S(1)}, u32[]{:S(2)}, u32[]{:S(2)}) collective-permute-start(bf16[2,80,256]{2,1,0:T(8,128)(2,1)S(1)} %get-tuple-element.105), channel_id=1, source_target_pairs={{0,5},{1,4},{2,7},{3,6},{4,1},{5,0},{6,3},{7,2},{8,13},{9,12},{10,... | collective-permute-start | bytes 245768 | tf_op jit(solution)/shard_map/ppermute | solution.py:378
  28.8 14.4 %collective-permute-start.13 = (bf16[128,1024]{1,0:T(8,128)(2,1)S(1)}, bf16[128,1024]{1,0:T(8,128)(2,1)S(1)}, u32[]{:S(2)}, u32[]{:S(2)}) collective-permute-start(bf16[128,1024]{1,0:T(8,128)(2,1)S(1)} %get-tuple-element.113), channel_id=1, source_target_pairs={{0,2},{1,3},{2,0},{3,1},{4,6},{5,7},{6,4},{7,5},{8,10},{9,11},{10,... | collective-permute-start | bytes 786440 | tf_op jit(solution)/shard_map/ppermute | solution.py:378
  37.1 6.1 %collective-permute-start.9 = (bf16[2,64,256]{2,1,0:T(8,128)(2,1)S(1)}, bf16[2,64,256]{2,1,0:T(8,128)(2,1)S(1)}, u32[]{:S(2)}, u32[]{:S(2)}) collective-permute-start(bf16[2,64,256]{2,1,0:T(8,128)(2,1)S(1)} %get-tuple-element.109), channel_id=1, source_target_pairs={{0,1},{1,0},{2,3},{3,2},{4,5},{5,4},{6,7},{7,6},{8,9},{9,8},{10,11... | collective-permute-start | bytes 196616 | tf_op jit(solution)/shard_map/ppermute | solution.py:378
  37.1 6.0 %collective-permute-start.10 = (bf16[2,64,256]{2,1,0:T(8,128)(2,1)S(1)}, bf16[2,64,256]{2,1,0:T(8,128)(2,1)S(1)}, u32[]{:S(2)}, u32[]{:S(2)}) collective-permute-start(bf16[2,64,256]{2,1,0:T(8,128)(2,1)S(1)} %get-tuple-element.110), channel_id=1, source_target_pairs={{0,4},{1,5},{2,6},{3,7},{4,0},{5,1},{6,2},{7,3},{8,12},{9,13},{10,... | collective-permute-start | bytes 196616 | tf_op jit(solution)/shard_map/ppermute | solution.py:378
  47.8 18.1 %collective-permute-start.14 = (bf16[128,2688]{1,0:T(8,128)(2,1)}, bf16[128,2688]{1,0:T(8,128)(2,1)}, u32[]{:S(2)}, u32[]{:S(2)}) collective-permute-start(bf16[128,2688]{1,0:T(8,128)(2,1)} %shard_map.135), channel_id=1, source_target_pairs={{0,2},{1,3},{2,0},{3,1},{4,6},{5,7},{6,4},{7,5},{8,10},{9,11},{10,... | collective-permute-start | bytes 2064392 | tf_op jit(solution)/shard_map/ppermute | solution.py:378
  67.6 20.3 %collective-permute-start.18 = (bf16[128,2816]{1,0:T(8,128)(2,1)S(1)}, bf16[128,2816]{1,0:T(8,128)(2,1)S(1)}, u32[]{:S(2)}, u32[]{:S(2)}) collective-permute-start(bf16[128,2816]{1,0:T(8,128)(2,1)S(1)} %get-tuple-element.115.block_ref), channel_id=1, source_target_pairs={{0,8},{1,9},{2,10},{3,11},{4,12},{5,13},{6,14},{7,15},{8,16},{9,17... | collective-permute-start | bytes 2162696 | tf_op jit(solution)/shard_map/ppermute | solution.py:386
  71.0 12.0 %collective-permute-start.15 = (bf16[72,2688]{1,0:T(8,128)(2,1)S(1)}, bf16[72,2688]{1,0:T(8,128)(2,1)S(1)}, u32[]{:S(2)}, u32[]{:S(2)}) collective-permute-start(bf16[72,2688]{1,0:T(8,128)(2,1)S(1)} %get-tuple-element.118), channel_id=1, source_target_pairs={{0,2},{1,3},{2,0},{3,1},{4,6},{5,7},{6,4},{7,5},{8,10},{9,11},{10,... | collective-permute-start | bytes 1161224 | tf_op jit(solution)/shard_map/ppermute | solution.py:378
  72.6 18.2 %collective-permute-start.16 = (bf16[72,2688]{1,0:T(8,128)(2,1)S(1)}, bf16[72,2688]{1,0:T(8,128)(2,1)S(1)}, u32[]{:S(2)}, u32[]{:S(2)}) collective-permute-start(bf16[72,2688]{1,0:T(8,128)(2,1)S(1)} %get-tuple-element.119), channel_id=1, source_target_pairs={{0,4},{1,5},{2,6},{3,7},{4,0},{5,1},{6,2},{7,3},{8,12},{9,13},{10,... | collective-permute-start | bytes 1161224 | tf_op jit(solution)/shard_map/ppermute | solution.py:378
  73.9 16.8 %collective-permute-start.17 = (bf16[72,2688]{1,0:T(8,128)(2,1)S(1)}, bf16[72,2688]{1,0:T(8,128)(2,1)S(1)}, u32[]{:S(2)}, u32[]{:S(2)}) collective-permute-start(bf16[72,2688]{1,0:T(8,128)(2,1)S(1)} %get-tuple-element.120), channel_id=1, source_target_pairs={{0,6},{1,7},{2,4},{3,5},{4,2},{5,3},{6,0},{7,1},{8,14},{9,15},{10,... | collective-permute-start | bytes 1161224 | tf_op jit(solution)/shard_map/ppermute | solution.py:378
  91.7 5.2 %collective-permute-start.19 = (bf16[144,2688]{1,0:T(8,128)(2,1)S(1)}, bf16[144,2688]{1,0:T(8,128)(2,1)S(1)}, u32[]{:S(2)}, u32[]{:S(2)}) collective-permute-start(bf16[144,2688]{1,0:T(8,128)(2,1)S(1)} %shard_map.139), channel_id=1, source_target_pairs={{0,1},{1,0},{2,3},{3,2},{4,5},{5,4},{6,7},{7,6},{8,9},{9,8},{10,11... | collective-permute-start | bytes 2322440 | tf_op jit(solution)/shard_map/ppermute | solution.py:378
  91.8 20.3 %collective-permute-start.20 = (bf16[128,2816]{1,0:T(8,128)(2,1)S(1)}, bf16[128,2816]{1,0:T(8,128)(2,1)S(1)}, u32[]{:S(2)}, u32[]{:S(2)}) collective-permute-start(bf16[128,2816]{1,0:T(8,128)(2,1)S(1)} %collective-permute-done.18.block_ref), channel_id=1, source_target_pairs={{0,8},{1,9},{2,10},{3,11},{4,12},{5,13},{6,14},{7,15},{8,16},{9,17... | collective-permute-start | bytes 2162696 | tf_op jit(solution)/shard_map/ppermute | solution.py:386
  93.5 14.0 %collective-permute-start.22 = (bf16[72,2688]{1,0:T(8,128)(2,1)S(1)}, bf16[72,2688]{1,0:T(8,128)(2,1)S(1)}, u32[]{:S(2)}, u32[]{:S(2)}) collective-permute-start(bf16[72,2688]{1,0:T(8,128)(2,1)S(1)} %get-tuple-element.128), channel_id=1, source_target_pairs={{0,2},{1,3},{2,0},{3,1},{4,6},{5,7},{6,4},{7,5},{8,10},{9,11},{10,... | collective-permute-start | bytes 1161224 | tf_op jit(solution)/shard_map/ppermute | solution.py:378
  94.6 18.9 %collective-permute-start.24 = (bf16[72,2688]{1,0:T(8,128)(2,1)S(1)}, bf16[72,2688]{1,0:T(8,128)(2,1)S(1)}, u32[]{:S(2)}, u32[]{:S(2)}) collective-permute-start(bf16[72,2688]{1,0:T(8,128)(2,1)S(1)} %get-tuple-element.132), channel_id=1, source_target_pairs={{0,4},{1,5},{2,6},{3,7},{4,0},{5,1},{6,2},{7,3},{8,12},{9,13},{10,... | collective-permute-start | bytes 1161224 | tf_op jit(solution)/shard_map/ppermute | solution.py:378
  95.4 18.2 %collective-permute-start.25 = (bf16[72,2688]{1,0:T(8,128)(2,1)S(1)}, bf16[72,2688]{1,0:T(8,128)(2,1)S(1)}, u32[]{:S(2)}, u32[]{:S(2)}) collective-permute-start(bf16[72,2688]{1,0:T(8,128)(2,1)S(1)} %get-tuple-element.133), channel_id=1, source_target_pairs={{0,6},{1,7},{2,4},{3,5},{4,2},{5,3},{6,0},{7,1},{8,14},{9,15},{10,... | collective-permute-start | bytes 1161224 | tf_op jit(solution)/shard_map/ppermute | solution.py:378
  114.6 5.5 %collective-permute-start.26 = (bf16[144,2688]{1,0:T(8,128)(2,1)S(1)}, bf16[144,2688]{1,0:T(8,128)(2,1)S(1)}, u32[]{:S(2)}, u32[]{:S(2)}) collective-permute-start(bf16[144,2688]{1,0:T(8,128)(2,1)S(1)} %shard_map.142), channel_id=1, source_target_pairs={{0,1},{1,0},{2,3},{3,2},{4,5},{5,4},{6,7},{7,6},{8,9},{9,8},{10,11... | collective-permute-start | bytes 2322440 | tf_op jit(solution)/shard_map/ppermute | solution.py:378
  114.7 20.3 %collective-permute-start.21 = (bf16[128,2816]{1,0:T(8,128)(2,1)S(1)}, bf16[128,2816]{1,0:T(8,128)(2,1)S(1)}, u32[]{:S(2)}, u32[]{:S(2)}) collective-permute-start(bf16[128,2816]{1,0:T(8,128)(2,1)S(1)} %collective-permute-done.20.block_ref), channel_id=1, source_target_pairs={{0,8},{1,9},{2,10},{3,11},{4,12},{5,13},{6,14},{7,15},{8,16},{9,17... | collective-permute-start | bytes 2162696 | tf_op jit(solution)/shard_map/ppermute | solution.py:386
  116.6 11.8 %collective-permute-start.23 = (bf16[72,2688]{1,0:T(8,128)(2,1)S(1)}, bf16[72,2688]{1,0:T(8,128)(2,1)S(1)}, u32[]{:S(2)}, u32[]{:S(2)}) collective-permute-start(bf16[72,2688]{1,0:T(8,128)(2,1)S(1)} %get-tuple-element.130), channel_id=1, source_target_pairs={{0,2},{1,3},{2,0},{3,1},{4,6},{5,7},{6,4},{7,5},{8,10},{9,11},{10,... | collective-permute-start | bytes 1161224 | tf_op jit(solution)/shard_map/ppermute | solution.py:378
  117.5 19.1 %collective-permute-start.30 = (bf16[72,2688]{1,0:T(8,128)(2,1)S(1)}, bf16[72,2688]{1,0:T(8,128)(2,1)S(1)}, u32[]{:S(2)}, u32[]{:S(2)}) collective-permute-start(bf16[72,2688]{1,0:T(8,128)(2,1)S(1)} %get-tuple-element.146), channel_id=1, source_target_pairs={{0,4},{1,5},{2,6},{3,7},{4,0},{5,1},{6,2},{7,3},{8,12},{9,13},{10,... | collective-permute-start | bytes 1161224 | tf_op jit(solution)/shard_map/ppermute | solution.py:378
  118.9 17.7 %collective-permute-start.31 = (bf16[72,2688]{1,0:T(8,128)(2,1)S(1)}, bf16[72,2688]{1,0:T(8,128)(2,1)S(1)}, u32[]{:S(2)}, u32[]{:S(2)}) collective-permute-start(bf16[72,2688]{1,0:T(8,128)(2,1)S(1)} %get-tuple-element.147), channel_id=1, source_target_pairs={{0,6},{1,7},{2,4},{3,5},{4,2},{5,3},{6,0},{7,1},{8,14},{9,15},{10,... | collective-permute-start | bytes 1161224 | tf_op jit(solution)/shard_map/ppermute | solution.py:378
  125.5 12.2 %collective-permute-start.33 = (bf16[144,2688]{1,0:T(8,128)(2,1)S(1)}, bf16[144,2688]{1,0:T(8,128)(2,1)S(1)}, u32[]{:S(2)}, u32[]{:S(2)}) collective-permute-start(bf16[144,2688]{1,0:T(8,128)(2,1)S(1)} %get-tuple-element.154), channel_id=1, source_target_pairs={{0,1},{1,0},{2,3},{3,2},{4,5},{5,4},{6,7},{7,6},{8,9},{9,8},{10,11... | collective-permute-start | bytes 2322440 | tf_op jit(solution)/shard_map/ppermute | solution.py:378
  137.6 5.8 %collective-permute-start.32 = (bf16[144,2688]{1,0:T(8,128)(2,1)S(1)}, bf16[144,2688]{1,0:T(8,128)(2,1)S(1)}, u32[]{:S(2)}, u32[]{:S(2)}) collective-permute-start(bf16[144,2688]{1,0:T(8,128)(2,1)S(1)} %shard_map.145), channel_id=1, source_target_pairs={{0,1},{1,0},{2,3},{3,2},{4,5},{5,4},{6,7},{7,6},{8,9},{9,8},{10,11... | collective-permute-start | bytes 2322440 | tf_op jit(solution)/shard_map/ppermute | solution.py:378
  138.8 11.8 %collective-permute-start.34 = (bf16[72,2688]{1,0:T(8,128)(2,1)S(1)}, bf16[72,2688]{1,0:T(8,128)(2,1)S(1)}, u32[]{:S(2)}, u32[]{:S(2)}) collective-permute-start(bf16[72,2688]{1,0:T(8,128)(2,1)S(1)} %get-tuple-element.156), channel_id=1, source_target_pairs={{0,2},{1,3},{2,0},{3,1},{4,6},{5,7},{6,4},{7,5},{8,10},{9,11},{10,... | collective-permute-start | bytes 1161224 | tf_op jit(solution)/shard_map/ppermute | solution.py:378
  139.9 20.1 %collective-permute-start.35 = (bf16[72,2688]{1,0:T(8,128)(2,1)S(1)}, bf16[72,2688]{1,0:T(8,128)(2,1)S(1)}, u32[]{:S(2)}, u32[]{:S(2)}) collective-permute-start(bf16[72,2688]{1,0:T(8,128)(2,1)S(1)} %get-tuple-element.157), channel_id=1, source_target_pairs={{0,4},{1,5},{2,6},{3,7},{4,0},{5,1},{6,2},{7,3},{8,12},{9,13},{10,... | collective-permute-start | bytes 1161224 | tf_op jit(solution)/shard_map/ppermute | solution.py:378
  140.9 19.2 %collective-permute-start.36 = (bf16[72,2688]{1,0:T(8,128)(2,1)S(1)}, bf16[72,2688]{1,0:T(8,128)(2,1)S(1)}, u32[]{:S(2)}, u32[]{:S(2)}) collective-permute-start(bf16[72,2688]{1,0:T(8,128)(2,1)S(1)} %get-tuple-element.158), channel_id=1, source_target_pairs={{0,6},{1,7},{2,4},{3,5},{4,2},{5,3},{6,0},{7,1},{8,14},{9,15},{10,... | collective-permute-start | bytes 1161224 | tf_op jit(solution)/shard_map/ppermute | solution.py:378
  142.3 24.9 %collective-permute-start.27 = (bf16[72,2688]{1,0:T(8,128)(2,1)S(1)}, bf16[72,2688]{1,0:T(8,128)(2,1)S(1)}, u32[]{:S(2)}, u32[]{:S(2)}) collective-permute-start(bf16[72,2688]{1,0:T(8,128)(2,1)S(1)} %get-tuple-element.142), channel_id=1, source_target_pairs={{0,2},{1,3},{2,0},{3,1},{4,6},{5,7},{6,4},{7,5},{8,10},{9,11},{10,... | collective-permute-start | bytes 1161224 | tf_op jit(solution)/shard_map/ppermute | solution.py:378
  143.4 24.5 %collective-permute-start.28 = (bf16[72,2688]{1,0:T(8,128)(2,1)S(1)}, bf16[72,2688]{1,0:T(8,128)(2,1)S(1)}, u32[]{:S(2)}, u32[]{:S(2)}) collective-permute-start(bf16[72,2688]{1,0:T(8,128)(2,1)S(1)} %get-tuple-element.143), channel_id=1, source_target_pairs={{0,4},{1,5},{2,6},{3,7},{4,0},{5,1},{6,2},{7,3},{8,12},{9,13},{10,... | collective-permute-start | bytes 1161224 | tf_op jit(solution)/shard_map/ppermute | solution.py:378
  150.6 25.3 %collective-permute-start.29 = (bf16[72,2688]{1,0:T(8,128)(2,1)S(1)}, bf16[72,2688]{1,0:T(8,128)(2,1)S(1)}, u32[]{:S(2)}, u32[]{:S(2)}) collective-permute-start(bf16[72,2688]{1,0:T(8,128)(2,1)S(1)} %get-tuple-element.144), channel_id=1, source_target_pairs={{0,6},{1,7},{2,4},{3,5},{4,2},{5,3},{6,0},{7,1},{8,14},{9,15},{10,... | collective-permute-start | bytes 1161224 | tf_op jit(solution)/shard_map/ppermute | solution.py:378
  160.1 17.3 %collective-permute-start.38 = (bf16[144,2688]{1,0:T(8,128)(2,1)S(1)}, bf16[144,2688]{1,0:T(8,128)(2,1)S(1)}, u32[]{:S(2)}, u32[]{:S(2)}) collective-permute-start(bf16[144,2688]{1,0:T(8,128)(2,1)S(1)} %get-tuple-element.164), channel_id=1, source_target_pairs={{0,1},{1,0},{2,3},{3,2},{4,5},{5,4},{6,7},{7,6},{8,9},{9,8},{10,11... | collective-permute-start | bytes 2322440 | tf_op jit(solution)/shard_map/ppermute | solution.py:378
  176.9 5.1 %collective-permute-start.37 = (bf16[144,2688]{1,0:T(8,128)(2,1)S(1)}, bf16[144,2688]{1,0:T(8,128)(2,1)S(1)}, u32[]{:S(2)}, u32[]{:S(2)}) collective-permute-start(bf16[144,2688]{1,0:T(8,128)(2,1)S(1)} %shard_map.148), channel_id=1, source_target_pairs={{0,1},{1,0},{2,3},{3,2},{4,5},{5,4},{6,7},{7,6},{8,9},{9,8},{10,11... | collective-permute-start | bytes 2322440 | tf_op jit(solution)/shard_map/ppermute | solution.py:378
  177.0 22.0 %collective-permute-start.50 = (bf16[128,2688]{1,0:T(8,128)(2,1)S(1)}, bf16[128,2688]{1,0:T(8,128)(2,1)S(1)}, u32[]{:S(2)}, u32[]{:S(2)}) collective-permute-start(bf16[128,2688]{1,0:T(8,128)(2,1)S(1)} %fusion.1), channel_id=1, source_target_pairs={{0,8},{1,9},{2,10},{3,11},{4,12},{5,13},{6,14},{7,15},{8,16},{9,17... | collective-permute-start | bytes 2064392 | tf_op jit(solution)/shard_map/ppermute | solution.py:386
  178.5 11.9 %collective-permute-start.39 = (bf16[72,2688]{1,0:T(8,128)(2,1)S(1)}, bf16[72,2688]{1,0:T(8,128)(2,1)S(1)}, u32[]{:S(2)}, u32[]{:S(2)}) collective-permute-start(bf16[72,2688]{1,0:T(8,128)(2,1)S(1)} %get-tuple-element.166), channel_id=1, source_target_pairs={{0,2},{1,3},{2,0},{3,1},{4,6},{5,7},{6,4},{7,5},{8,10},{9,11},{10,... | collective-permute-start | bytes 1161224 | tf_op jit(solution)/shard_map/ppermute | solution.py:378
  179.4 19.1 %collective-permute-start.40 = (bf16[72,2688]{1,0:T(8,128)(2,1)S(1)}, bf16[72,2688]{1,0:T(8,128)(2,1)S(1)}, u32[]{:S(2)}, u32[]{:S(2)}) collective-permute-start(bf16[72,2688]{1,0:T(8,128)(2,1)S(1)} %get-tuple-element.167), channel_id=1, source_target_pairs={{0,4},{1,5},{2,6},{3,7},{4,0},{5,1},{6,2},{7,3},{8,12},{9,13},{10,... | collective-permute-start | bytes 1161224 | tf_op jit(solution)/shard_map/ppermute | solution.py:378
  180.8 17.7 %collective-permute-start.41 = (bf16[72,2688]{1,0:T(8,128)(2,1)S(1)}, bf16[72,2688]{1,0:T(8,128)(2,1)S(1)}, u32[]{:S(2)}, u32[]{:S(2)}) collective-permute-start(bf16[72,2688]{1,0:T(8,128)(2,1)S(1)} %get-tuple-element.168), channel_id=1, source_target_pairs={{0,6},{1,7},{2,4},{3,5},{4,2},{5,3},{6,0},{7,1},{8,14},{9,15},{10,... | collective-permute-start | bytes 1161224 | tf_op jit(solution)/shard_map/ppermute | solution.py:378
  187.4 13.3 %collective-permute-start.42 = (bf16[144,2688]{1,0:T(8,128)(2,1)S(1)}, bf16[144,2688]{1,0:T(8,128)(2,1)S(1)}, u32[]{:S(2)}, u32[]{:S(2)}) collective-permute-start(bf16[144,2688]{1,0:T(8,128)(2,1)S(1)} %get-tuple-element.170), channel_id=1, source_target_pairs={{0,1},{1,0},{2,3},{3,2},{4,5},{5,4},{6,7},{7,6},{8,9},{9,8},{10,11... | collective-permute-start | bytes 2322440 | tf_op jit(solution)/shard_map/ppermute | solution.py:378
  199.2 18.6 %collective-permute-start.51 = (bf16[128,2688]{1,0:T(8,128)(2,1)S(1)}, bf16[128,2688]{1,0:T(8,128)(2,1)S(1)}, u32[]{:S(2)}, u32[]{:S(2)}) collective-permute-start(bf16[128,2688]{1,0:T(8,128)(2,1)S(1)} %add_convert_fusion.1), channel_id=1, source_target_pairs={{0,8},{1,9},{2,10},{3,11},{4,12},{5,13},{6,14},{7,15},{8,16},{9,17... | collective-permute-start | bytes 2064392 | tf_op jit(solution)/shard_map/ppermute | solution.py:386
  201.8 16.1 %collective-permute-start.47 = (bf16[72,2688]{1,0:T(8,128)(2,1)S(1)}, bf16[72,2688]{1,0:T(8,128)(2,1)S(1)}, u32[]{:S(2)}, u32[]{:S(2)}) collective-permute-start(bf16[72,2688]{1,0:T(8,128)(2,1)S(1)} %get-tuple-element.178), channel_id=1, source_target_pairs={{0,2},{1,3},{2,0},{3,1},{4,6},{5,7},{6,4},{7,5},{8,10},{9,11},{10,... | collective-permute-start | bytes 1161224 | tf_op jit(solution)/shard_map/ppermute | solution.py:378
  202.9 17.9 %collective-permute-start.48 = (bf16[72,2688]{1,0:T(8,128)(2,1)S(1)}, bf16[72,2688]{1,0:T(8,128)(2,1)S(1)}, u32[]{:S(2)}, u32[]{:S(2)}) collective-permute-start(bf16[72,2688]{1,0:T(8,128)(2,1)S(1)} %get-tuple-element.179), channel_id=1, source_target_pairs={{0,4},{1,5},{2,6},{3,7},{4,0},{5,1},{6,2},{7,3},{8,12},{9,13},{10,... | collective-permute-start | bytes 1161224 | tf_op jit(solution)/shard_map/ppermute | solution.py:378
  203.8 17.1 %collective-permute-start.49 = (bf16[72,2688]{1,0:T(8,128)(2,1)S(1)}, bf16[72,2688]{1,0:T(8,128)(2,1)S(1)}, u32[]{:S(2)}, u32[]{:S(2)}) collective-permute-start(bf16[72,2688]{1,0:T(8,128)(2,1)S(1)} %get-tuple-element.180), channel_id=1, source_target_pairs={{0,6},{1,7},{2,4},{3,5},{4,2},{5,3},{6,0},{7,1},{8,14},{9,15},{10,... | collective-permute-start | bytes 1161224 | tf_op jit(solution)/shard_map/ppermute | solution.py:378
  205.3 17.8 %collective-permute-start.43 = (bf16[144,2688]{1,0:T(8,128)(2,1)S(1)}, bf16[144,2688]{1,0:T(8,128)(2,1)S(1)}, u32[]{:S(2)}, u32[]{:S(2)}) collective-permute-start(bf16[144,2688]{1,0:T(8,128)(2,1)S(1)} %get-tuple-element.173), channel_id=1, source_target_pairs={{0,1},{1,0},{2,3},{3,2},{4,5},{5,4},{6,7},{7,6},{8,9},{9,8},{10,11... | collective-permute-start | bytes 2322440 | tf_op jit(solution)/shard_map/ppermute | solution.py:378
  221.4 19.9 %collective-permute-start.52 = (bf16[128,2688]{1,0:T(8,128)(2,1)S(1)}, bf16[128,2688]{1,0:T(8,128)(2,1)S(1)}, u32[]{:S(2)}, u32[]{:S(2)}) collective-permute-start(bf16[128,2688]{1,0:T(8,128)(2,1)S(1)} %fusion), channel_id=1, source_target_pairs={{0,8},{1,9},{2,10},{3,11},{4,12},{5,13},{6,14},{7,15},{8,16},{9,17... | collective-permute-start | bytes 2064392 | tf_op jit(solution)/shard_map/ppermute | solution.py:386
  224.2 12.0 %collective-permute-start.44 = (bf16[72,2688]{1,0:T(8,128)(2,1)S(1)}, bf16[72,2688]{1,0:T(8,128)(2,1)S(1)}, u32[]{:S(2)}, u32[]{:S(2)}) collective-permute-start(bf16[72,2688]{1,0:T(8,128)(2,1)S(1)} %get-tuple-element.175), channel_id=1, source_target_pairs={{0,2},{1,3},{2,0},{3,1},{4,6},{5,7},{6,4},{7,5},{8,10},{9,11},{10,... | collective-permute-start | bytes 1161224 | tf_op jit(solution)/shard_map/ppermute | solution.py:378
  225.2 15.1 %collective-permute-start.45 = (bf16[72,2688]{1,0:T(8,128)(2,1)S(1)}, bf16[72,2688]{1,0:T(8,128)(2,1)S(1)}, u32[]{:S(2)}, u32[]{:S(2)}) collective-permute-start(bf16[72,2688]{1,0:T(8,128)(2,1)S(1)} %get-tuple-element.176), channel_id=1, source_target_pairs={{0,4},{1,5},{2,6},{3,7},{4,0},{5,1},{6,2},{7,3},{8,12},{9,13},{10,... | collective-permute-start | bytes 1161224 | tf_op jit(solution)/shard_map/ppermute | solution.py:378
  226.1 15.3 %collective-permute-start.46 = (bf16[72,2688]{1,0:T(8,128)(2,1)S(1)}, bf16[72,2688]{1,0:T(8,128)(2,1)S(1)}, u32[]{:S(2)}, u32[]{:S(2)}) collective-permute-start(bf16[72,2688]{1,0:T(8,128)(2,1)S(1)} %get-tuple-element.177), channel_id=1, source_target_pairs={{0,6},{1,7},{2,4},{3,5},{4,2},{5,3},{6,0},{7,1},{8,14},{9,15},{10,... | collective-permute-start | bytes 1161224 | tf_op jit(solution)/shard_map/ppermute | solution.py:378
  (31 other events, 382.6 us)

commit v2 on v1

--- a/solution.py
+++ b/solution.py
@@ -606,9 +606,11 @@
     if end >= 3:
         before.append(parts[end - 2])
     made[end] = work(arrived[end], before, [])
+    results[0] = sort_back(*made[0])
     if end:
-        parts[end] = gather_up(weighs[end], give_back(end, *([parts[end - 1]] if end >= 2 else [])))
-    back = give_back(0, *([results[end][0]] if end else []))
+        back = give_back(end, *([parts[end - 1]] if end >= 2 else []))
+        parts[end] = gather_up(weighs[end], held(back, results[0][0]))
+    back = send_back(held(results[0], *([results[end][0]] if end else [])))
     carried = None
     for step in range(1, outer):
         part = parts[step]

time: 243 us -> 242 us (level)
    ppermute x6, waiting for transfers between devices: 28.6 us -> 16.1 us  [turn(): lax.ppermute(x, AXES, [(d, (d + plane) % devices) for d in range(devices)])]
    ppermute x45, waiting for transfers between devices: 79.5 us -> 90.9 us  [swap(): return lax.ppermute(x, AXES, [(d, d ^ m) for d in range(devices)])]
where the time goes in v2:
time: 242 us
  waiting for transfers between devices  107 us (44%)
  starting transfers between devices  59.1 us (24%)
  Pallas kernels  53.4 us (22%)
  local copies, waits for them, and re-layouts  15.8 us (7%)
  matrix products  3.85 us (2%)
    ppermute x45, waiting for transfers between devices, swap(): return lax.ppermute(x, AXES, [(d, d ^ m) for d in range(devices)])  90.9 us
    pallas_call x26, Pallas kernels, kernel_call(): pl.pallas_call(kernel, out_shape=outs, in_specs=([smem] if scalars else [...  53.4 us
    ppermute x45, starting transfers between devices, swap(): return lax.ppermute(x, AXES, [(d, d ^ m) for d in range(devices)])  45.6 us
    ppermute x6, waiting for transfers between devices, turn(): lax.ppermute(x, AXES, [(d, (d + plane) % devices) for d in range(devices)])  16.1 us
    unnamed x52, local copies, waits for them, and re-layouts  13 us
    ppermute x6, starting transfers between devices, turn(): lax.ppermute(x, AXES, [(d, (d + plane) % devices) for d in range(devices)])  9.14 us
  transfers between devices with their start and end apart: 53, of which 26 were waited for; matrix products, arithmetic and copies ran while one was open for 3% of the time, Pallas kernels for 19%

profile of v2, /device:TPU:0, one launch (start us, length us, event | category | flops | bytes accessed | tf_op | source)
XLA Modules:
  0.0 241.6 jit_solution(12852456642211088947)
XLA Ops:
  2.3 2.6 %collective-permute-start = (bf16[128,1536]{1,0:T(8,128)(2,1)S(1)}, bf16[128,1536]{1,0:T(8,128)(2,1)S(1)}, u32[]{:S(2)}, u32[]{:S(2)}) collective-permute-start(bf16[128,1536]{1,0:T(8,128)(2,1)S(1)} %get-tuple-element.103), channel_id=1, source_target_pairs={{0,2},{1,3},{2,0},{3,1},{4,6},{5,7},{6,4},{7,5},{8,10},{9,11},{10,... | collective-permute-start | bytes 1179656 | tf_op jit(solution)/shard_map/ppermute | solution.py:378
  4.8 2.0 collective-permute-start.2
  6.9 2.3 collective-permute-start.1
  12.3 1.7 collective-permute-start.3
  14.0 3.0 %collective-permute-done.3.rest_5_.refs_3_.ld_ref = f32[32,128]{1,0:T(8,128)S(1)} collective-permute-done((f32[32,128]{1,0:T(8,128)S(1)}, f32[32,128]{1,0:T(8,128)S(1)}, u32[]{:S(2)}, u32[]{:S(2)}) %collective-permute-start.3) | collective-permute-done | bytes 16416 | tf_op jit(solution)/shard_map/ppermute | solution.py:378
  17.1 2.7 %shard_map.129 = (bf16[128,1536]{1,0:T(8,128)(2,1)S(1)}, bf16[128,1536]{1,0:T(8,128)(2,1)S(1)}, bf16[2,80,256]{2,1,0:T(8,128)(2,1)S(1)}, bf16[2,80,256]{2,1,0:T(...) custom-call(s32[4]{0:T(128)S(1)} %pad_add_fusion.at_ref, ...), custom_call_target="tpu_custom_call" | custom-call | flops 50000000 | bytes 8000000 | tf_op jit(solution)/shard_map/pallas_call | solution.py:415
  21.8 3.4 %collective-permute-done.5.rest_2_ = bf16[2,80,256]{2,1,0:T(8,128)(2,1)S(1)} collective-permute-done((bf16[2,80,256]{2,1,0:T(8,128)(2,1)S(1)}, bf16[2,80,256]{2,1,0:T(8,128)(2,1)S(1)}, u32[]{:S(2)}, u32[]{:S(2)}) %collective-permute-start.5) | collective-permute-done | bytes 81952 | tf_op jit(solution)/shard_map/ppermute | solution.py:378
  26.7 2.0 collective-permute-start.7
  28.8 1.5 collective-permute-start.13
  31.4 3.1 %collective-permute-start.8 = (bf16[80,256]{1,0:T(8,128)(2,1)S(1)}, bf16[80,256]{1,0:T(8,128)(2,1)S(1)}, u32[]{:S(2)}, u32[]{:S(2)}) collective-permute-start(bf16[80,256]{1,0:T(8,128)(2,1)S(1)} %shard_map.132), channel_id=1, source_target_pairs={{0,16},{1,17},{2,18},{3,19},{4,20},{5,21},{6,22},{7,23},{8,24},{9,... | collective-permute-start | bytes 122888 | tf_op jit(solution)/shard_map/ppermute | solution.py:378
  34.5 1.9 collective-permute-done.8.rest_1_
  39.6 2.7 %shard_map.130 = (f32[128,1024]{1,0:T(8,128)S(1)}, f32[128,1024]{1,0:T(8,128)S(1)}) custom-call(s32[4]{0:T(128)S(1)} %pad_add_fusion.at_ref, bf16[128,1536]{1,0:T(8,128)(2,1)S(1)} %get-tuple-element.106.refs_0_.act_ref, bf16[128,1536]{1,0:T(8,128)(2,1)S(1)} %get-tuple-element.107.refs_1_.act_ref, f32[32,128]{1,0:T(8,128)S(1)} %get-tuple-element.105.rest_4_.refs_2_.ld_ref, ...), custom_call_target="tpu_custom_call" | custom-call | flops 100000000 | bytes 15000000 | tf_op jit(solution)/shard_map/pallas_call | solution.py:415
  43.2 4.6 %shard_map.135 = bf16[128,2688]{1,0:T(8,128)(2,1)} custom-call(s32[4]{0:T(128)S(1)} %pad_add_fusion.at_ref, f32[1,2048]{1,0:T(1,128)S(1)} %bitcast.24, bf16[128,1536]{1,0:T(8,128)(2,1)S(1)} %get-tuple-element.107.refs_1_.act_ref, f32[32,128]{1,0:T(8,128)S(1)} %collective-permute-done.3.rest_5_.refs_3_.ld_ref, f32[128,1024]{1,0:T(8,128)S(1)} %get-tuple-element.119.inside_ref, ...), custom_call_target="tpu_custom_call" | custom-call | flops 800000000 | bytes 8000000 | tf_op jit(solution)/shard_map/pallas_call | solution.py:415
  47.8 1.8 collective-permute-start.14
  57.6 3.7 %shard_map.134.own_ref = f32[128,2688]{1,0:T(8,128)S(1)} custom-call(s32[4]{0:T(128)S(1)} %copy-done.13, f32[1,2048]{1,0:T(1,128)S(1)} %bitcast.25, bf16[128,1536]{1,0:T(8,128)(2,1)S(1)} %copy-done.8, f32[32,128]{1,0:T(8,128)S(1)} %get-tuple-element.105.rest_4_.refs_2_.ld_ref, f32[128,1024]{1,0:T(8,128)S(1)} %copy-done.11, bf16[128,2048]{1,0:T(8,128)(2,1)S(1)} %copy-done.6, ...), custom_call_target="tpu_custom_call" | custom-call | flops 800000000 | bytes 8000000 | tf_op jit(solution)/shard_map/pallas_call | solution.py:415
  61.3 4.6 %collective-permute-done.14.rest_0_ = bf16[128,2688]{1,0:T(8,128)(2,1)} collective-permute-done((bf16[128,2688]{1,0:T(8,128)(2,1)}, bf16[128,2688]{1,0:T(8,128)(2,1)}, u32[]{:S(2)}, u32[]{:S(2)}) %collective-permute-start.14) | collective-permute-done | bytes 688160 | tf_op jit(solution)/shard_map/ppermute | solution.py:378
  65.9 1.7 shard_map.136
  67.6 2.1 collective-permute-start.18
  71.0 1.6 collective-permute-start.15
  74.6 8.4 %collective-permute-done.15.refs_1_ = bf16[72,2688]{1,0:T(8,128)(2,1)S(1)} collective-permute-done((bf16[72,2688]{1,0:T(8,128)(2,1)S(1)}, bf16[72,2688]{1,0:T(8,128)(2,1)S(1)}, u32[]{:S(2)}, u32[]{:S(2)}) %collective-permute-start.15) | collective-permute-done | bytes 387104 | tf_op jit(solution)/shard_map/ppermute | solution.py:378
  83.0 4.8 %collective-permute-done.18.block_ref = bf16[128,2816]{1,0:T(8,128)(2,1)S(1)} collective-permute-done((bf16[128,2816]{1,0:T(8,128)(2,1)S(1)}, bf16[128,2816]{1,0:T(8,128)(2,1)S(1)}, u32[]{:S(2)}, u32[]{:S(2)}) %collective-permute-start.18) | collective-permute-done | bytes 720928 | tf_op jit(solution)/shard_map/ppermute | solution.py:386
  89.1 1.6 collective-permute-done.16.refs_2_
  91.8 1.6 collective-permute-start.21
  95.4 1.6 collective-permute-start.26
  97.0 2.6 %copy-done = bf16[1,2688,1024]{2,1,0:T(8,128)(2,1)S(1)} copy-done((bf16[1,2688,1024]{2,1,0:T(8,128)(2,1)S(1)}, bf16[1,2688,1024]{2,1,0:T(8,128)(2,1)}, u32[]{:S(2)}) %copy-start) | copy-done | bytes 5505048
  99.5 2.6 %copy-done.1 = bf16[1,1024,2688]{2,1,0:T(8,128)(2,1)S(1)} copy-done((bf16[1,1024,2688]{2,1,0:T(8,128)(2,1)S(1)}, bf16[1,1024,2688]{2,1,0:T(8,128)(2,1)}, u32[]{:S(2)}) %copy-start.1) | copy-done | bytes 5505048
  102.1 5.4 %shard_map.140 = (bf16[144,2688]{1,0:T(8,128)(2,1)S(1)}, bf16[144,2688]{1,0:T(8,128)(2,1)S(1)}) custom-call(bf16[72,2688]{1,0:T(8,128)(2,1)S(1)} %get-tuple-element.130.refs_0_, bf16[72,2688]{1,0:T(8,128)(2,1)S(1)} %collective-permute-done.15.refs_1_, bf16[72,2688]{1,0:T(8,128)(2,1)S(1)} %collective-permute-done.16.refs_2_, ...), custom_call_target="tpu_custom_call" | custom-call | tf_op jit(solution)/shard_map/pallas_call | solution.py:415
  107.5 4.7 %collective-permute-done.21.block_ref = bf16[128,2816]{1,0:T(8,128)(2,1)S(1)} collective-permute-done((bf16[128,2816]{1,0:T(8,128)(2,1)S(1)}, bf16[128,2816]{1,0:T(8,128)(2,1)S(1)}, u32[]{:S(2)}, u32[]{:S(2)}) %collective-permute-start.21) | collective-permute-done | bytes 720928 | tf_op jit(solution)/shard_map/ppermute | solution.py:386
  114.7 1.9 collective-permute-start.22
  120.1 5.4 %shard_map.144 = (bf16[144,2688]{1,0:T(8,128)(2,1)S(1)}, bf16[144,2688]{1,0:T(8,128)(2,1)S(1)}) custom-call(bf16[72,2688]{1,0:T(8,128)(2,1)S(1)} %get-tuple-element.147.refs_0_, bf16[72,2688]{1,0:T(8,128)(2,1)S(1)} %collective-permute-done.23.refs_1_, bf16[72,2688]{1,0:T(8,128)(2,1)S(1)} %collective-permute-done.25.refs_2_, ...), custom_call_target="tpu_custom_call" | custom-call | tf_op jit(solution)/shard_map/pallas_call | solution.py:415
  125.6 2.9 %collective-permute-done.24.refs_1_ = bf16[72,2688]{1,0:T(8,128)(2,1)S(1)} collective-permute-done((bf16[72,2688]{1,0:T(8,128)(2,1)S(1)}, bf16[72,2688]{1,0:T(8,128)(2,1)S(1)}, u32[]{:S(2)}, u32[]{:S(2)}) %collective-permute-start.24) | collective-permute-done | bytes 387104 | tf_op jit(solution)/shard_map/ppermute | solution.py:378
  128.4 6.6 %collective-permute-done.22.block_ref = bf16[128,2816]{1,0:T(8,128)(2,1)S(1)} collective-permute-done((bf16[128,2816]{1,0:T(8,128)(2,1)S(1)}, bf16[128,2816]{1,0:T(8,128)(2,1)S(1)}, u32[]{:S(2)}, u32[]{:S(2)}) %collective-permute-start.22) | collective-permute-done | bytes 720928 | tf_op jit(solution)/shard_map/ppermute | solution.py:386
  144.4 6.2 %collective-permute-done.35 = bf16[72,2688]{1,0:T(8,128)(2,1)S(1)} collective-permute-done((bf16[72,2688]{1,0:T(8,128)(2,1)S(1)}, bf16[72,2688]{1,0:T(8,128)(2,1)S(1)}, u32[]{:S(2)}, u32[]{:S(2)}) %collective-permute-start.35) | collective-permute-done | bytes 387104 | tf_op jit(solution)/shard_map/ppermute | solution.py:378
  150.6 1.5 collective-permute-start.30
  152.1 5.4 %shard_map.147 = (bf16[144,2688]{1,0:T(8,128)(2,1)S(1)}, bf16[144,2688]{1,0:T(8,128)(2,1)S(1)}) custom-call(bf16[72,2688]{1,0:T(8,128)(2,1)S(1)} %get-tuple-element.161.refs_0_, bf16[72,2688]{1,0:T(8,128)(2,1)S(1)} %collective-permute-done.24.refs_1_, bf16[72,2688]{1,0:T(8,128)(2,1)S(1)} %collective-permute-done.31.refs_2_, ...), custom_call_target="tpu_custom_call" | custom-call | tf_op jit(solution)/shard_map/pallas_call | solution.py:415
  157.5 2.6 %collective-permute-done.36 = bf16[72,2688]{1,0:T(8,128)(2,1)S(1)} collective-permute-done((bf16[72,2688]{1,0:T(8,128)(2,1)S(1)}, bf16[72,2688]{1,0:T(8,128)(2,1)S(1)}, u32[]{:S(2)}, u32[]{:S(2)}) %collective-permute-start.36) | collective-permute-done | bytes 387104 | tf_op jit(solution)/shard_map/ppermute | solution.py:378
  160.6 6.7 %collective-permute-done.28.refs_1_ = bf16[72,2688]{1,0:T(8,128)(2,1)S(1)} collective-permute-done((bf16[72,2688]{1,0:T(8,128)(2,1)S(1)}, bf16[72,2688]{1,0:T(8,128)(2,1)S(1)}, u32[]{:S(2)}, u32[]{:S(2)}) %collective-permute-start.28) | collective-permute-done | bytes 387104 | tf_op jit(solution)/shard_map/ppermute | solution.py:378
  168.0 8.0 %collective-permute-done.30.refs_3_ = bf16[72,2688]{1,0:T(8,128)(2,1)S(1)} collective-permute-done((bf16[72,2688]{1,0:T(8,128)(2,1)S(1)}, bf16[72,2688]{1,0:T(8,128)(2,1)S(1)}, u32[]{:S(2)}, u32[]{:S(2)}) %collective-permute-start.30) | collective-permute-done | bytes 387104 | tf_op jit(solution)/shard_map/ppermute | solution.py:378
  182.1 5.4 %shard_map.150 = (bf16[144,2688]{1,0:T(8,128)(2,1)S(1)}, bf16[144,2688]{1,0:T(8,128)(2,1)S(1)}) custom-call(bf16[72,2688]{1,0:T(8,128)(2,1)S(1)} %get-tuple-element.171.refs_0_, bf16[72,2688]{1,0:T(8,128)(2,1)S(1)} %collective-permute-done.28.refs_1_, bf16[72,2688]{1,0:T(8,128)(2,1)S(1)} %collective-permute-done.29.refs_2_, ...), custom_call_target="tpu_custom_call" | custom-call | tf_op jit(solution)/shard_map/pallas_call | solution.py:415
  187.4 3.0 %collective-permute-done.40 = bf16[72,2688]{1,0:T(8,128)(2,1)S(1)} collective-permute-done((bf16[72,2688]{1,0:T(8,128)(2,1)S(1)}, bf16[72,2688]{1,0:T(8,128)(2,1)S(1)}, u32[]{:S(2)}, u32[]{:S(2)}) %collective-permute-start.40) | collective-permute-done | bytes 387104 | tf_op jit(solution)/shard_map/ppermute | solution.py:378
  190.4 8.1 %collective-permute-done.41 = bf16[72,2688]{1,0:T(8,128)(2,1)S(1)} collective-permute-done((bf16[72,2688]{1,0:T(8,128)(2,1)S(1)}, bf16[72,2688]{1,0:T(8,128)(2,1)S(1)}, u32[]{:S(2)}, u32[]{:S(2)}) %collective-permute-start.41) | collective-permute-done | bytes 387104 | tf_op jit(solution)/shard_map/ppermute | solution.py:378
  203.8 1.6 collective-permute-start.49
  206.4 7.3 %collective-permute-done.47 = bf16[72,2688]{1,0:T(8,128)(2,1)S(1)} collective-permute-done((bf16[72,2688]{1,0:T(8,128)(2,1)S(1)}, bf16[72,2688]{1,0:T(8,128)(2,1)S(1)}, u32[]{:S(2)}, u32[]{:S(2)}) %collective-permute-start.47) | collective-permute-done | bytes 387104 | tf_op jit(solution)/shard_map/ppermute | solution.py:378
  213.8 7.1 %collective-permute-done.48 = bf16[72,2688]{1,0:T(8,128)(2,1)S(1)} collective-permute-done((bf16[72,2688]{1,0:T(8,128)(2,1)S(1)}, bf16[72,2688]{1,0:T(8,128)(2,1)S(1)}, u32[]{:S(2)}, u32[]{:S(2)}) %collective-permute-start.48) | collective-permute-done | bytes 387104 | tf_op jit(solution)/shard_map/ppermute | solution.py:378
  221.4 1.7 collective-permute-start.52
  224.9 1.7 collective-permute-start.46
  226.6 8.4 %collective-permute-done.44 = bf16[72,2688]{1,0:T(8,128)(2,1)S(1)} collective-permute-done((bf16[72,2688]{1,0:T(8,128)(2,1)S(1)}, bf16[72,2688]{1,0:T(8,128)(2,1)S(1)}, u32[]{:S(2)}, u32[]{:S(2)}) %collective-permute-start.44) | collective-permute-done | bytes 387104 | tf_op jit(solution)/shard_map/ppermute | solution.py:378
  235.0 4.1 %collective-permute-done.45 = bf16[72,2688]{1,0:T(8,128)(2,1)S(1)} collective-permute-done((bf16[72,2688]{1,0:T(8,128)(2,1)S(1)}, bf16[72,2688]{1,0:T(8,128)(2,1)S(1)}, u32[]{:S(2)}, u32[]{:S(2)}) %collective-permute-start.45) | collective-permute-done | bytes 387104 | tf_op jit(solution)/shard_map/ppermute | solution.py:378
  (153 shorter events, 63.6 us)
Async XLA Ops:
  0.0 43.2 %collective-permute-start.12 = (bf16[512,2688]{1,0:T(8,128)(2,1)}, bf16[512,2688]{1,0:T(8,128)(2,1)}, u32[]{:S(2)}, u32[]{:S(2)}) collective-permute-start(bf16[512,2688]{1,0:T(8,128)(2,1)} %rest_4_.3), channel_id=1, source_target_pairs={{0,1},{1,0},{2,3},{3,2},{4,5},{5,4},{6,7},{7,6},{8,9},{9,8},{10,11... | collective-permute-start | bytes 8257544 | tf_op jit(solution)/shard_map/ppermute | solution.py:378
  2.3 14.8 %collective-permute-start = (bf16[128,1536]{1,0:T(8,128)(2,1)S(1)}, bf16[128,1536]{1,0:T(8,128)(2,1)S(1)}, u32[]{:S(2)}, u32[]{:S(2)}) collective-permute-start(bf16[128,1536]{1,0:T(8,128)(2,1)S(1)} %get-tuple-element.103), channel_id=1, source_target_pairs={{0,2},{1,3},{2,0},{3,1},{4,6},{5,7},{6,4},{7,5},{8,10},{9,11},{10,... | collective-permute-start | bytes 1179656 | tf_op jit(solution)/shard_map/ppermute | solution.py:378
  4.8 12.2 %collective-permute-start.2 = (bf16[16,3072]{1,0:T(8,128)(2,1)S(1)}, bf16[16,3072]{1,0:T(8,128)(2,1)S(1)}, u32[]{:S(2)}, u32[]{:S(2)}) collective-permute-start(bf16[16,3072]{1,0:T(8,128)(2,1)S(1)} %get-tuple-element.104), channel_id=1, source_target_pairs={{0,3},{1,0},{2,1},{3,6},{4,7},{5,4},{6,5},{7,10},{8,11},{9,8},{10,... | collective-permute-start | bytes 294920 | tf_op jit(solution)/shard_map/ppermute | solution.py:405
  6.9 10.2 %collective-permute-start.1 = (bf16[16,3072]{1,0:T(8,128)(2,1)S(1)}, bf16[16,3072]{1,0:T(8,128)(2,1)S(1)}, u32[]{:S(2)}, u32[]{:S(2)}) collective-permute-start(bf16[16,3072]{1,0:T(8,128)(2,1)S(1)} %get-tuple-element.104), channel_id=1, source_target_pairs={{0,1},{1,2},{2,3},{3,4},{4,5},{5,6},{6,7},{7,8},{8,9},{9,10},{10,1... | collective-permute-start | bytes 294920 | tf_op jit(solution)/shard_map/ppermute | solution.py:405
  19.9 5.3 %collective-permute-start.5 = (bf16[2,80,256]{2,1,0:T(8,128)(2,1)S(1)}, bf16[2,80,256]{2,1,0:T(8,128)(2,1)S(1)}, u32[]{:S(2)}, u32[]{:S(2)}) collective-permute-start(bf16[2,80,256]{2,1,0:T(8,128)(2,1)S(1)} %get-tuple-element.111), channel_id=1, source_target_pairs={{0,4},{1,5},{2,6},{3,7},{4,0},{5,1},{6,2},{7,3},{8,12},{9,13},{10,... | collective-permute-start | bytes 245768 | tf_op jit(solution)/shard_map/ppermute | solution.py:378
  20.9 5.1 %collective-permute-start.6 = (bf16[2,80,256]{2,1,0:T(8,128)(2,1)S(1)}, bf16[2,80,256]{2,1,0:T(8,128)(2,1)S(1)}, u32[]{:S(2)}, u32[]{:S(2)}) collective-permute-start(bf16[2,80,256]{2,1,0:T(8,128)(2,1)S(1)} %get-tuple-element.112), channel_id=1, source_target_pairs={{0,5},{1,4},{2,7},{3,6},{4,1},{5,0},{6,3},{7,2},{8,13},{9,12},{10,... | collective-permute-start | bytes 245768 | tf_op jit(solution)/shard_map/ppermute | solution.py:378
  28.8 14.4 %collective-permute-start.13 = (bf16[128,1024]{1,0:T(8,128)(2,1)S(1)}, bf16[128,1024]{1,0:T(8,128)(2,1)S(1)}, u32[]{:S(2)}, u32[]{:S(2)}) collective-permute-start(bf16[128,1024]{1,0:T(8,128)(2,1)S(1)} %get-tuple-element.120), channel_id=1, source_target_pairs={{0,2},{1,3},{2,0},{3,1},{4,6},{5,7},{6,4},{7,5},{8,10},{9,11},{10,... | collective-permute-start | bytes 786440 | tf_op jit(solution)/shard_map/ppermute | solution.py:378
  37.1 6.1 %collective-permute-start.9 = (bf16[2,64,256]{2,1,0:T(8,128)(2,1)S(1)}, bf16[2,64,256]{2,1,0:T(8,128)(2,1)S(1)}, u32[]{:S(2)}, u32[]{:S(2)}) collective-permute-start(bf16[2,64,256]{2,1,0:T(8,128)(2,1)S(1)} %get-tuple-element.116), channel_id=1, source_target_pairs={{0,1},{1,0},{2,3},{3,2},{4,5},{5,4},{6,7},{7,6},{8,9},{9,8},{10,11... | collective-permute-start | bytes 196616 | tf_op jit(solution)/shard_map/ppermute | solution.py:378
  37.1 6.0 %collective-permute-start.10 = (bf16[2,64,256]{2,1,0:T(8,128)(2,1)S(1)}, bf16[2,64,256]{2,1,0:T(8,128)(2,1)S(1)}, u32[]{:S(2)}, u32[]{:S(2)}) collective-permute-start(bf16[2,64,256]{2,1,0:T(8,128)(2,1)S(1)} %get-tuple-element.117), channel_id=1, source_target_pairs={{0,4},{1,5},{2,6},{3,7},{4,0},{5,1},{6,2},{7,3},{8,12},{9,13},{10,... | collective-permute-start | bytes 196616 | tf_op jit(solution)/shard_map/ppermute | solution.py:378
  47.8 18.1 %collective-permute-start.14 = (bf16[128,2688]{1,0:T(8,128)(2,1)}, bf16[128,2688]{1,0:T(8,128)(2,1)}, u32[]{:S(2)}, u32[]{:S(2)}) collective-permute-start(bf16[128,2688]{1,0:T(8,128)(2,1)} %shard_map.135), channel_id=1, source_target_pairs={{0,2},{1,3},{2,0},{3,1},{4,6},{5,7},{6,4},{7,5},{8,10},{9,11},{10,... | collective-permute-start | bytes 2064392 | tf_op jit(solution)/shard_map/ppermute | solution.py:378
  67.6 20.3 %collective-permute-start.18 = (bf16[128,2816]{1,0:T(8,128)(2,1)S(1)}, bf16[128,2816]{1,0:T(8,128)(2,1)S(1)}, u32[]{:S(2)}, u32[]{:S(2)}) collective-permute-start(bf16[128,2816]{1,0:T(8,128)(2,1)S(1)} %get-tuple-element.122.block_ref), channel_id=1, source_target_pairs={{0,8},{1,9},{2,10},{3,11},{4,12},{5,13},{6,14},{7,15},{8,16},{9,17... | collective-permute-start | bytes 2162696 | tf_op jit(solution)/shard_map/ppermute | solution.py:386
  71.0 12.0 %collective-permute-start.15 = (bf16[72,2688]{1,0:T(8,128)(2,1)S(1)}, bf16[72,2688]{1,0:T(8,128)(2,1)S(1)}, u32[]{:S(2)}, u32[]{:S(2)}) collective-permute-start(bf16[72,2688]{1,0:T(8,128)(2,1)S(1)} %get-tuple-element.125), channel_id=1, source_target_pairs={{0,2},{1,3},{2,0},{3,1},{4,6},{5,7},{6,4},{7,5},{8,10},{9,11},{10,... | collective-permute-start | bytes 1161224 | tf_op jit(solution)/shard_map/ppermute | solution.py:378
  72.6 18.2 %collective-permute-start.16 = (bf16[72,2688]{1,0:T(8,128)(2,1)S(1)}, bf16[72,2688]{1,0:T(8,128)(2,1)S(1)}, u32[]{:S(2)}, u32[]{:S(2)}) collective-permute-start(bf16[72,2688]{1,0:T(8,128)(2,1)S(1)} %get-tuple-element.126), channel_id=1, source_target_pairs={{0,4},{1,5},{2,6},{3,7},{4,0},{5,1},{6,2},{7,3},{8,12},{9,13},{10,... | collective-permute-start | bytes 1161224 | tf_op jit(solution)/shard_map/ppermute | solution.py:378
  73.9 16.8 %collective-permute-start.17 = (bf16[72,2688]{1,0:T(8,128)(2,1)S(1)}, bf16[72,2688]{1,0:T(8,128)(2,1)S(1)}, u32[]{:S(2)}, u32[]{:S(2)}) collective-permute-start(bf16[72,2688]{1,0:T(8,128)(2,1)S(1)} %get-tuple-element.127), channel_id=1, source_target_pairs={{0,6},{1,7},{2,4},{3,5},{4,2},{5,3},{6,0},{7,1},{8,14},{9,15},{10,... | collective-permute-start | bytes 1161224 | tf_op jit(solution)/shard_map/ppermute | solution.py:378
  91.7 5.2 %collective-permute-start.19 = (bf16[144,2688]{1,0:T(8,128)(2,1)S(1)}, bf16[144,2688]{1,0:T(8,128)(2,1)S(1)}, u32[]{:S(2)}, u32[]{:S(2)}) collective-permute-start(bf16[144,2688]{1,0:T(8,128)(2,1)S(1)} %shard_map.139), channel_id=1, source_target_pairs={{0,1},{1,0},{2,3},{3,2},{4,5},{5,4},{6,7},{7,6},{8,9},{9,8},{10,11... | collective-permute-start | bytes 2322440 | tf_op jit(solution)/shard_map/ppermute | solution.py:378
  91.8 20.3 %collective-permute-start.21 = (bf16[128,2816]{1,0:T(8,128)(2,1)S(1)}, bf16[128,2816]{1,0:T(8,128)(2,1)S(1)}, u32[]{:S(2)}, u32[]{:S(2)}) collective-permute-start(bf16[128,2816]{1,0:T(8,128)(2,1)S(1)} %collective-permute-done.18.block_ref), channel_id=1, source_target_pairs={{0,8},{1,9},{2,10},{3,11},{4,12},{5,13},{6,14},{7,15},{8,16},{9,17... | collective-permute-start | bytes 2162696 | tf_op jit(solution)/shard_map/ppermute | solution.py:386
  93.5 14.0 %collective-permute-start.23 = (bf16[72,2688]{1,0:T(8,128)(2,1)S(1)}, bf16[72,2688]{1,0:T(8,128)(2,1)S(1)}, u32[]{:S(2)}, u32[]{:S(2)}) collective-permute-start(bf16[72,2688]{1,0:T(8,128)(2,1)S(1)} %get-tuple-element.140), channel_id=1, source_target_pairs={{0,2},{1,3},{2,0},{3,1},{4,6},{5,7},{6,4},{7,5},{8,10},{9,11},{10,... | collective-permute-start | bytes 1161224 | tf_op jit(solution)/shard_map/ppermute | solution.py:378
  94.6 18.9 %collective-permute-start.25 = (bf16[72,2688]{1,0:T(8,128)(2,1)S(1)}, bf16[72,2688]{1,0:T(8,128)(2,1)S(1)}, u32[]{:S(2)}, u32[]{:S(2)}) collective-permute-start(bf16[72,2688]{1,0:T(8,128)(2,1)S(1)} %get-tuple-element.144), channel_id=1, source_target_pairs={{0,4},{1,5},{2,6},{3,7},{4,0},{5,1},{6,2},{7,3},{8,12},{9,13},{10,... | collective-permute-start | bytes 1161224 | tf_op jit(solution)/shard_map/ppermute | solution.py:378
  95.4 18.2 %collective-permute-start.26 = (bf16[72,2688]{1,0:T(8,128)(2,1)S(1)}, bf16[72,2688]{1,0:T(8,128)(2,1)S(1)}, u32[]{:S(2)}, u32[]{:S(2)}) collective-permute-start(bf16[72,2688]{1,0:T(8,128)(2,1)S(1)} %get-tuple-element.145), channel_id=1, source_target_pairs={{0,6},{1,7},{2,4},{3,5},{4,2},{5,3},{6,0},{7,1},{8,14},{9,15},{10,... | collective-permute-start | bytes 1161224 | tf_op jit(solution)/shard_map/ppermute | solution.py:378
  114.6 5.5 %collective-permute-start.27 = (bf16[144,2688]{1,0:T(8,128)(2,1)S(1)}, bf16[144,2688]{1,0:T(8,128)(2,1)S(1)}, u32[]{:S(2)}, u32[]{:S(2)}) collective-permute-start(bf16[144,2688]{1,0:T(8,128)(2,1)S(1)} %shard_map.143), channel_id=1, source_target_pairs={{0,1},{1,0},{2,3},{3,2},{4,5},{5,4},{6,7},{7,6},{8,9},{9,8},{10,11... | collective-permute-start | bytes 2322440 | tf_op jit(solution)/shard_map/ppermute | solution.py:378
  114.7 20.3 %collective-permute-start.22 = (bf16[128,2816]{1,0:T(8,128)(2,1)S(1)}, bf16[128,2816]{1,0:T(8,128)(2,1)S(1)}, u32[]{:S(2)}, u32[]{:S(2)}) collective-permute-start(bf16[128,2816]{1,0:T(8,128)(2,1)S(1)} %collective-permute-done.21.block_ref), channel_id=1, source_target_pairs={{0,8},{1,9},{2,10},{3,11},{4,12},{5,13},{6,14},{7,15},{8,16},{9,17... | collective-permute-start | bytes 2162696 | tf_op jit(solution)/shard_map/ppermute | solution.py:386
  116.6 11.8 %collective-permute-start.24 = (bf16[72,2688]{1,0:T(8,128)(2,1)S(1)}, bf16[72,2688]{1,0:T(8,128)(2,1)S(1)}, u32[]{:S(2)}, u32[]{:S(2)}) collective-permute-start(bf16[72,2688]{1,0:T(8,128)(2,1)S(1)} %get-tuple-element.142), channel_id=1, source_target_pairs={{0,2},{1,3},{2,0},{3,1},{4,6},{5,7},{6,4},{7,5},{8,10},{9,11},{10,... | collective-permute-start | bytes 1161224 | tf_op jit(solution)/shard_map/ppermute | solution.py:378
  117.5 19.1 %collective-permute-start.31 = (bf16[72,2688]{1,0:T(8,128)(2,1)S(1)}, bf16[72,2688]{1,0:T(8,128)(2,1)S(1)}, u32[]{:S(2)}, u32[]{:S(2)}) collective-permute-start(bf16[72,2688]{1,0:T(8,128)(2,1)S(1)} %get-tuple-element.158), channel_id=1, source_target_pairs={{0,4},{1,5},{2,6},{3,7},{4,0},{5,1},{6,2},{7,3},{8,12},{9,13},{10,... | collective-permute-start | bytes 1161224 | tf_op jit(solution)/shard_map/ppermute | solution.py:378
  118.9 17.7 %collective-permute-start.32 = (bf16[72,2688]{1,0:T(8,128)(2,1)S(1)}, bf16[72,2688]{1,0:T(8,128)(2,1)S(1)}, u32[]{:S(2)}, u32[]{:S(2)}) collective-permute-start(bf16[72,2688]{1,0:T(8,128)(2,1)S(1)} %get-tuple-element.159), channel_id=1, source_target_pairs={{0,6},{1,7},{2,4},{3,5},{4,2},{5,3},{6,0},{7,1},{8,14},{9,15},{10,... | collective-permute-start | bytes 1161224 | tf_op jit(solution)/shard_map/ppermute | solution.py:378
  125.5 12.2 %collective-permute-start.34 = (bf16[144,2688]{1,0:T(8,128)(2,1)S(1)}, bf16[144,2688]{1,0:T(8,128)(2,1)S(1)}, u32[]{:S(2)}, u32[]{:S(2)}) collective-permute-start(bf16[144,2688]{1,0:T(8,128)(2,1)S(1)} %get-tuple-element.166), channel_id=1, source_target_pairs={{0,1},{1,0},{2,3},{3,2},{4,5},{5,4},{6,7},{7,6},{8,9},{9,8},{10,11... | collective-permute-start | bytes 2322440 | tf_op jit(solution)/shard_map/ppermute | solution.py:378
  137.6 5.8 %collective-permute-start.33 = (bf16[144,2688]{1,0:T(8,128)(2,1)S(1)}, bf16[144,2688]{1,0:T(8,128)(2,1)S(1)}, u32[]{:S(2)}, u32[]{:S(2)}) collective-permute-start(bf16[144,2688]{1,0:T(8,128)(2,1)S(1)} %shard_map.146), channel_id=1, source_target_pairs={{0,1},{1,0},{2,3},{3,2},{4,5},{5,4},{6,7},{7,6},{8,9},{9,8},{10,11... | collective-permute-start | bytes 2322440 | tf_op jit(solution)/shard_map/ppermute | solution.py:378
  138.8 11.8 %collective-permute-start.35 = (bf16[72,2688]{1,0:T(8,128)(2,1)S(1)}, bf16[72,2688]{1,0:T(8,128)(2,1)S(1)}, u32[]{:S(2)}, u32[]{:S(2)}) collective-permute-start(bf16[72,2688]{1,0:T(8,128)(2,1)S(1)} %get-tuple-element.168), channel_id=1, source_target_pairs={{0,2},{1,3},{2,0},{3,1},{4,6},{5,7},{6,4},{7,5},{8,10},{9,11},{10,... | collective-permute-start | bytes 1161224 | tf_op jit(solution)/shard_map/ppermute | solution.py:378
  139.9 20.1 %collective-permute-start.36 = (bf16[72,2688]{1,0:T(8,128)(2,1)S(1)}, bf16[72,2688]{1,0:T(8,128)(2,1)S(1)}, u32[]{:S(2)}, u32[]{:S(2)}) collective-permute-start(bf16[72,2688]{1,0:T(8,128)(2,1)S(1)} %get-tuple-element.169), channel_id=1, source_target_pairs={{0,4},{1,5},{2,6},{3,7},{4,0},{5,1},{6,2},{7,3},{8,12},{9,13},{10,... | collective-permute-start | bytes 1161224 | tf_op jit(solution)/shard_map/ppermute | solution.py:378
  140.9 19.2 %collective-permute-start.37 = (bf16[72,2688]{1,0:T(8,128)(2,1)S(1)}, bf16[72,2688]{1,0:T(8,128)(2,1)S(1)}, u32[]{:S(2)}, u32[]{:S(2)}) collective-permute-start(bf16[72,2688]{1,0:T(8,128)(2,1)S(1)} %get-tuple-element.170), channel_id=1, source_target_pairs={{0,6},{1,7},{2,4},{3,5},{4,2},{5,3},{6,0},{7,1},{8,14},{9,15},{10,... | collective-permute-start | bytes 1161224 | tf_op jit(solution)/shard_map/ppermute | solution.py:378
  142.3 24.9 %collective-permute-start.28 = (bf16[72,2688]{1,0:T(8,128)(2,1)S(1)}, bf16[72,2688]{1,0:T(8,128)(2,1)S(1)}, u32[]{:S(2)}, u32[]{:S(2)}) collective-permute-start(bf16[72,2688]{1,0:T(8,128)(2,1)S(1)} %get-tuple-element.154), channel_id=1, source_target_pairs={{0,2},{1,3},{2,0},{3,1},{4,6},{5,7},{6,4},{7,5},{8,10},{9,11},{10,... | collective-permute-start | bytes 1161224 | tf_op jit(solution)/shard_map/ppermute | solution.py:378
  143.4 24.5 %collective-permute-start.29 = (bf16[72,2688]{1,0:T(8,128)(2,1)S(1)}, bf16[72,2688]{1,0:T(8,128)(2,1)S(1)}, u32[]{:S(2)}, u32[]{:S(2)}) collective-permute-start(bf16[72,2688]{1,0:T(8,128)(2,1)S(1)} %get-tuple-element.155), channel_id=1, source_target_pairs={{0,4},{1,5},{2,6},{3,7},{4,0},{5,1},{6,2},{7,3},{8,12},{9,13},{10,... | collective-permute-start | bytes 1161224 | tf_op jit(solution)/shard_map/ppermute | solution.py:378
  150.6 25.3 %collective-permute-start.30 = (bf16[72,2688]{1,0:T(8,128)(2,1)S(1)}, bf16[72,2688]{1,0:T(8,128)(2,1)S(1)}, u32[]{:S(2)}, u32[]{:S(2)}) collective-permute-start(bf16[72,2688]{1,0:T(8,128)(2,1)S(1)} %get-tuple-element.156), channel_id=1, source_target_pairs={{0,6},{1,7},{2,4},{3,5},{4,2},{5,3},{6,0},{7,1},{8,14},{9,15},{10,... | collective-permute-start | bytes 1161224 | tf_op jit(solution)/shard_map/ppermute | solution.py:378
  160.1 17.3 %collective-permute-start.39 = (bf16[144,2688]{1,0:T(8,128)(2,1)S(1)}, bf16[144,2688]{1,0:T(8,128)(2,1)S(1)}, u32[]{:S(2)}, u32[]{:S(2)}) collective-permute-start(bf16[144,2688]{1,0:T(8,128)(2,1)S(1)} %get-tuple-element.176), channel_id=1, source_target_pairs={{0,1},{1,0},{2,3},{3,2},{4,5},{5,4},{6,7},{7,6},{8,9},{9,8},{10,11... | collective-permute-start | bytes 2322440 | tf_op jit(solution)/shard_map/ppermute | solution.py:378
  176.9 5.1 %collective-permute-start.38 = (bf16[144,2688]{1,0:T(8,128)(2,1)S(1)}, bf16[144,2688]{1,0:T(8,128)(2,1)S(1)}, u32[]{:S(2)}, u32[]{:S(2)}) collective-permute-start(bf16[144,2688]{1,0:T(8,128)(2,1)S(1)} %shard_map.149), channel_id=1, source_target_pairs={{0,1},{1,0},{2,3},{3,2},{4,5},{5,4},{6,7},{7,6},{8,9},{9,8},{10,11... | collective-permute-start | bytes 2322440 | tf_op jit(solution)/shard_map/ppermute | solution.py:378
  177.0 22.0 %collective-permute-start.50 = (bf16[128,2688]{1,0:T(8,128)(2,1)S(1)}, bf16[128,2688]{1,0:T(8,128)(2,1)S(1)}, u32[]{:S(2)}, u32[]{:S(2)}) collective-permute-start(bf16[128,2688]{1,0:T(8,128)(2,1)S(1)} %fusion), channel_id=1, source_target_pairs={{0,8},{1,9},{2,10},{3,11},{4,12},{5,13},{6,14},{7,15},{8,16},{9,17... | collective-permute-start | bytes 2064392 | tf_op jit(solution)/shard_map/ppermute | solution.py:386
  178.5 11.9 %collective-permute-start.40 = (bf16[72,2688]{1,0:T(8,128)(2,1)S(1)}, bf16[72,2688]{1,0:T(8,128)(2,1)S(1)}, u32[]{:S(2)}, u32[]{:S(2)}) collective-permute-start(bf16[72,2688]{1,0:T(8,128)(2,1)S(1)} %get-tuple-element.178), channel_id=1, source_target_pairs={{0,2},{1,3},{2,0},{3,1},{4,6},{5,7},{6,4},{7,5},{8,10},{9,11},{10,... | collective-permute-start | bytes 1161224 | tf_op jit(solution)/shard_map/ppermute | solution.py:378
  179.4 19.1 %collective-permute-start.41 = (bf16[72,2688]{1,0:T(8,128)(2,1)S(1)}, bf16[72,2688]{1,0:T(8,128)(2,1)S(1)}, u32[]{:S(2)}, u32[]{:S(2)}) collective-permute-start(bf16[72,2688]{1,0:T(8,128)(2,1)S(1)} %get-tuple-element.179), channel_id=1, source_target_pairs={{0,4},{1,5},{2,6},{3,7},{4,0},{5,1},{6,2},{7,3},{8,12},{9,13},{10,... | collective-permute-start | bytes 1161224 | tf_op jit(solution)/shard_map/ppermute | solution.py:378
  180.8 17.7 %collective-permute-start.42 = (bf16[72,2688]{1,0:T(8,128)(2,1)S(1)}, bf16[72,2688]{1,0:T(8,128)(2,1)S(1)}, u32[]{:S(2)}, u32[]{:S(2)}) collective-permute-start(bf16[72,2688]{1,0:T(8,128)(2,1)S(1)} %get-tuple-element.180), channel_id=1, source_target_pairs={{0,6},{1,7},{2,4},{3,5},{4,2},{5,3},{6,0},{7,1},{8,14},{9,15},{10,... | collective-permute-start | bytes 1161224 | tf_op jit(solution)/shard_map/ppermute | solution.py:378
  182.1 23.3 %collective-permute-start.20 = (bf16[144,2688]{1,0:T(8,128)(2,1)S(1)}, bf16[144,2688]{1,0:T(8,128)(2,1)S(1)}, u32[]{:S(2)}, u32[]{:S(2)}) collective-permute-start(bf16[144,2688]{1,0:T(8,128)(2,1)S(1)} %get-tuple-element.135), channel_id=1, source_target_pairs={{0,1},{1,0},{2,3},{3,2},{4,5},{5,4},{6,7},{7,6},{8,9},{9,8},{10,11... | collective-permute-start | bytes 2322440 | tf_op jit(solution)/shard_map/ppermute | solution.py:378
  190.4 10.3 %collective-permute-start.43 = (bf16[144,2688]{1,0:T(8,128)(2,1)S(1)}, bf16[144,2688]{1,0:T(8,128)(2,1)S(1)}, u32[]{:S(2)}, u32[]{:S(2)}) collective-permute-start(bf16[144,2688]{1,0:T(8,128)(2,1)S(1)} %get-tuple-element.182), channel_id=1, source_target_pairs={{0,1},{1,0},{2,3},{3,2},{4,5},{5,4},{6,7},{7,6},{8,9},{9,8},{10,11... | collective-permute-start | bytes 2322440 | tf_op jit(solution)/shard_map/ppermute | solution.py:378
  199.2 21.7 %collective-permute-start.51 = (bf16[128,2688]{1,0:T(8,128)(2,1)S(1)}, bf16[128,2688]{1,0:T(8,128)(2,1)S(1)}, u32[]{:S(2)}, u32[]{:S(2)}) collective-permute-start(bf16[128,2688]{1,0:T(8,128)(2,1)S(1)} %add_convert_fusion.1), channel_id=1, source_target_pairs={{0,8},{1,9},{2,10},{3,11},{4,12},{5,13},{6,14},{7,15},{8,16},{9,17... | collective-permute-start | bytes 2064392 | tf_op jit(solution)/shard_map/ppermute | solution.py:386
  201.8 12.0 %collective-permute-start.47 = (bf16[72,2688]{1,0:T(8,128)(2,1)S(1)}, bf16[72,2688]{1,0:T(8,128)(2,1)S(1)}, u32[]{:S(2)}, u32[]{:S(2)}) collective-permute-start(bf16[72,2688]{1,0:T(8,128)(2,1)S(1)} %get-tuple-element.188), channel_id=1, source_target_pairs={{0,2},{1,3},{2,0},{3,1},{4,6},{5,7},{6,4},{7,5},{8,10},{9,11},{10,... | collective-permute-start | bytes 1161224 | tf_op jit(solution)/shard_map/ppermute | solution.py:378
  203.0 17.9 %collective-permute-start.48 = (bf16[72,2688]{1,0:T(8,128)(2,1)S(1)}, bf16[72,2688]{1,0:T(8,128)(2,1)S(1)}, u32[]{:S(2)}, u32[]{:S(2)}) collective-permute-start(bf16[72,2688]{1,0:T(8,128)(2,1)S(1)} %get-tuple-element.189), channel_id=1, source_target_pairs={{0,4},{1,5},{2,6},{3,7},{4,0},{5,1},{6,2},{7,3},{8,12},{9,13},{10,... | collective-permute-start | bytes 1161224 | tf_op jit(solution)/shard_map/ppermute | solution.py:378
  203.8 17.1 %collective-permute-start.49 = (bf16[72,2688]{1,0:T(8,128)(2,1)S(1)}, bf16[72,2688]{1,0:T(8,128)(2,1)S(1)}, u32[]{:S(2)}, u32[]{:S(2)}) collective-permute-start(bf16[72,2688]{1,0:T(8,128)(2,1)S(1)} %get-tuple-element.190), channel_id=1, source_target_pairs={{0,6},{1,7},{2,4},{3,5},{4,2},{5,3},{6,0},{7,1},{8,14},{9,15},{10,... | collective-permute-start | bytes 1161224 | tf_op jit(solution)/shard_map/ppermute | solution.py:378
  221.4 18.8 %collective-permute-start.52 = (bf16[128,2688]{1,0:T(8,128)(2,1)S(1)}, bf16[128,2688]{1,0:T(8,128)(2,1)S(1)}, u32[]{:S(2)}, u32[]{:S(2)}) collective-permute-start(bf16[128,2688]{1,0:T(8,128)(2,1)S(1)} %fusion.21), channel_id=1, source_target_pairs={{0,8},{1,9},{2,10},{3,11},{4,12},{5,13},{6,14},{7,15},{8,16},{9,17... | collective-permute-start | bytes 2064392 | tf_op jit(solution)/shard_map/ppermute | solution.py:386
  223.1 11.9 %collective-permute-start.44 = (bf16[72,2688]{1,0:T(8,128)(2,1)S(1)}, bf16[72,2688]{1,0:T(8,128)(2,1)S(1)}, u32[]{:S(2)}, u32[]{:S(2)}) collective-permute-start(bf16[72,2688]{1,0:T(8,128)(2,1)S(1)} %get-tuple-element.185), channel_id=1, source_target_pairs={{0,2},{1,3},{2,0},{3,1},{4,6},{5,7},{6,4},{7,5},{8,10},{9,11},{10,... | collective-permute-start | bytes 1161224 | tf_op jit(solution)/shard_map/ppermute | solution.py:378
  224.0 15.1 %collective-permute-start.45 = (bf16[72,2688]{1,0:T(8,128)(2,1)S(1)}, bf16[72,2688]{1,0:T(8,128)(2,1)S(1)}, u32[]{:S(2)}, u32[]{:S(2)}) collective-permute-start(bf16[72,2688]{1,0:T(8,128)(2,1)S(1)} %get-tuple-element.186), channel_id=1, source_target_pairs={{0,4},{1,5},{2,6},{3,7},{4,0},{5,1},{6,2},{7,3},{8,12},{9,13},{10,... | collective-permute-start | bytes 1161224 | tf_op jit(solution)/shard_map/ppermute | solution.py:378
  224.9 15.3 %collective-permute-start.46 = (bf16[72,2688]{1,0:T(8,128)(2,1)S(1)}, bf16[72,2688]{1,0:T(8,128)(2,1)S(1)}, u32[]{:S(2)}, u32[]{:S(2)}) collective-permute-start(bf16[72,2688]{1,0:T(8,128)(2,1)S(1)} %get-tuple-element.187), channel_id=1, source_target_pairs={{0,6},{1,7},{2,4},{3,5},{4,2},{5,3},{6,0},{7,1},{8,14},{9,15},{10,... | collective-permute-start | bytes 1161224 | tf_op jit(solution)/shard_map/ppermute | solution.py:378
  (31 other events, 382.6 us)

commit v3 on v2

--- a/solution.py
+++ b/solution.py
@@ -235,18 +235,14 @@
         at = pl.ds(pl.multiple_of(half * inner + g * width, width), width)
         gated = ssm * silu(z_ref[:, cols if b else at].astype(f32))
         square = jnp.mean(gated * gated, axis=1, keepdims=True)
-        mix[((g // shard) ^ core) * shard + g % shard] = (
+        mix[(g // shard) ^ core, :, g % shard * width : (g % shard + 1) * width] = (
             gated * lax.rsqrt(square + EPS) * gain_ref[:, at]
         ).astype(bf16)
     model = out_ref.shape[1]
     tile = 384 if model % 384 == 0 else model
     for c in range(0, model, tile):
-        total = None
-        for g in range(count):
-            rows = (own_ref, pair_ref)[g // shard]
-            at = (g % shard) * width
-            part = dot(mix[g], rows[at : at + width, c : c + tile], ((1,), (0,)))
-            total = part if total is None else total + part
+        total = dot(mix[0], own_ref[:, c : c + tile], ((1,), (0,)))
+        total = total + dot(mix[1], pair_ref[:, c : c + tile], ((1,), (0,)))
         out_ref[:, c : c + tile] = total.astype(out_ref.dtype)
 
 
@@ -496,7 +492,7 @@
             + incoming
             + [rows_own, rows_pair],
             shapes((length, model), bf16 if b else f32),
-            [pltpu.VMEM((count, blocks, N, width), bf16), pltpu.VMEM((count, length, width), bf16)],
+            [pltpu.VMEM((count, blocks, N, width), bf16), pltpu.VMEM((2, length, shard), bf16)],
             800000000,
             8000000,
         )

time: 242 us -> 242 us (level)
  no operation moved by 1% of the time
where the time goes in v3:
time: 242 us
  waiting for transfers between devices  107 us (44%)
  starting transfers between devices  59 us (24%)
  Pallas kernels  53.4 us (22%)
  local copies, waits for them, and re-layouts  15.8 us (7%)
  matrix products  3.85 us (2%)
    ppermute x45, waiting for transfers between devices, swap(): return lax.ppermute(x, AXES, [(d, d ^ m) for d in range(devices)])  91 us
    pallas_call x26, Pallas kernels, kernel_call(): pl.pallas_call(kernel, out_shape=outs, in_specs=([smem] if scalars else [...  53.4 us
    ppermute x45, starting transfers between devices, swap(): return lax.ppermute(x, AXES, [(d, d ^ m) for d in range(devices)])  45.6 us
    ppermute x6, waiting for transfers between devices, turn(): lax.ppermute(x, AXES, [(d, (d + plane) % devices) for d in range(devices)])  16.1 us
    unnamed x52, local copies, waits for them, and re-layouts  13 us
    ppermute x6, starting transfers between devices, turn(): lax.ppermute(x, AXES, [(d, (d + plane) % devices) for d in range(devices)])  9.12 us
  transfers between devices with their start and end apart: 53, of which 26 were waited for; matrix products, arithmetic and copies ran while one was open for 3% of the time, Pallas kernels for 19%

profile of v3, /device:TPU:0, one launch (start us, length us, event | category | flops | bytes accessed | tf_op | source)
XLA Modules:
  0.0 241.6 jit_solution(14713681798767254308)
XLA Ops:
  2.3 2.6 %collective-permute-start = (bf16[128,1536]{1,0:T(8,128)(2,1)S(1)}, bf16[128,1536]{1,0:T(8,128)(2,1)S(1)}, u32[]{:S(2)}, u32[]{:S(2)}) collective-permute-start(bf16[128,1536]{1,0:T(8,128)(2,1)S(1)} %get-tuple-element.103), channel_id=1, source_target_pairs={{0,2},{1,3},{2,0},{3,1},{4,6},{5,7},{6,4},{7,5},{8,10},{9,11},{10,... | collective-permute-start | bytes 1179656 | tf_op jit(solution)/shard_map/ppermute | solution.py:374
  4.8 2.0 collective-permute-start.2
  6.9 2.3 collective-permute-start.1
  12.3 1.7 collective-permute-start.3
  14.0 3.0 %collective-permute-done.3.rest_5_.refs_3_.ld_ref = f32[32,128]{1,0:T(8,128)S(1)} collective-permute-done((f32[32,128]{1,0:T(8,128)S(1)}, f32[32,128]{1,0:T(8,128)S(1)}, u32[]{:S(2)}, u32[]{:S(2)}) %collective-permute-start.3) | collective-permute-done | bytes 16416 | tf_op jit(solution)/shard_map/ppermute | solution.py:374
  17.1 2.7 %shard_map.129 = (bf16[128,1536]{1,0:T(8,128)(2,1)S(1)}, bf16[128,1536]{1,0:T(8,128)(2,1)S(1)}, bf16[2,80,256]{2,1,0:T(8,128)(2,1)S(1)}, bf16[2,80,256]{2,1,0:T(...) custom-call(s32[4]{0:T(128)S(1)} %pad_add_fusion.at_ref, ...), custom_call_target="tpu_custom_call" | custom-call | flops 50000000 | bytes 8000000 | tf_op jit(solution)/shard_map/pallas_call | solution.py:411
  21.8 3.4 %collective-permute-done.5.rest_2_ = bf16[2,80,256]{2,1,0:T(8,128)(2,1)S(1)} collective-permute-done((bf16[2,80,256]{2,1,0:T(8,128)(2,1)S(1)}, bf16[2,80,256]{2,1,0:T(8,128)(2,1)S(1)}, u32[]{:S(2)}, u32[]{:S(2)}) %collective-permute-start.5) | collective-permute-done | bytes 81952 | tf_op jit(solution)/shard_map/ppermute | solution.py:374
  26.7 2.0 collective-permute-start.7
  28.8 1.5 collective-permute-start.13
  31.4 3.1 %collective-permute-start.8 = (bf16[80,256]{1,0:T(8,128)(2,1)S(1)}, bf16[80,256]{1,0:T(8,128)(2,1)S(1)}, u32[]{:S(2)}, u32[]{:S(2)}) collective-permute-start(bf16[80,256]{1,0:T(8,128)(2,1)S(1)} %shard_map.132), channel_id=1, source_target_pairs={{0,16},{1,17},{2,18},{3,19},{4,20},{5,21},{6,22},{7,23},{8,24},{9,... | collective-permute-start | bytes 122888 | tf_op jit(solution)/shard_map/ppermute | solution.py:374
  34.5 1.9 collective-permute-done.8.rest_1_
  39.6 2.7 %shard_map.130 = (f32[128,1024]{1,0:T(8,128)S(1)}, f32[128,1024]{1,0:T(8,128)S(1)}) custom-call(s32[4]{0:T(128)S(1)} %pad_add_fusion.at_ref, bf16[128,1536]{1,0:T(8,128)(2,1)S(1)} %get-tuple-element.106.refs_0_.act_ref, bf16[128,1536]{1,0:T(8,128)(2,1)S(1)} %get-tuple-element.107.refs_1_.act_ref, f32[32,128]{1,0:T(8,128)S(1)} %get-tuple-element.105.rest_4_.refs_2_.ld_ref, ...), custom_call_target="tpu_custom_call" | custom-call | flops 100000000 | bytes 15000000 | tf_op jit(solution)/shard_map/pallas_call | solution.py:411
  43.2 4.6 %shard_map.135 = bf16[128,2688]{1,0:T(8,128)(2,1)} custom-call(s32[4]{0:T(128)S(1)} %pad_add_fusion.at_ref, f32[1,2048]{1,0:T(1,128)S(1)} %bitcast.24, bf16[128,1536]{1,0:T(8,128)(2,1)S(1)} %get-tuple-element.107.refs_1_.act_ref, f32[32,128]{1,0:T(8,128)S(1)} %collective-permute-done.3.rest_5_.refs_3_.ld_ref, f32[128,1024]{1,0:T(8,128)S(1)} %get-tuple-element.119.inside_ref, ...), custom_call_target="tpu_custom_call" | custom-call | flops 800000000 | bytes 8000000 | tf_op jit(solution)/shard_map/pallas_call | solution.py:411
  47.8 1.8 collective-permute-start.14
  57.6 3.7 %shard_map.134.own_ref = f32[128,2688]{1,0:T(8,128)S(1)} custom-call(s32[4]{0:T(128)S(1)} %copy-done.13, f32[1,2048]{1,0:T(1,128)S(1)} %bitcast.25, bf16[128,1536]{1,0:T(8,128)(2,1)S(1)} %copy-done.8, f32[32,128]{1,0:T(8,128)S(1)} %get-tuple-element.105.rest_4_.refs_2_.ld_ref, f32[128,1024]{1,0:T(8,128)S(1)} %copy-done.11, bf16[128,2048]{1,0:T(8,128)(2,1)S(1)} %copy-done.6, ...), custom_call_target="tpu_custom_call" | custom-call | flops 800000000 | bytes 8000000 | tf_op jit(solution)/shard_map/pallas_call | solution.py:411
  61.3 4.5 %collective-permute-done.14.rest_0_ = bf16[128,2688]{1,0:T(8,128)(2,1)} collective-permute-done((bf16[128,2688]{1,0:T(8,128)(2,1)}, bf16[128,2688]{1,0:T(8,128)(2,1)}, u32[]{:S(2)}, u32[]{:S(2)}) %collective-permute-start.14) | collective-permute-done | bytes 688160 | tf_op jit(solution)/shard_map/ppermute | solution.py:374
  65.9 1.7 shard_map.136
  67.6 2.1 collective-permute-start.18
  71.0 1.6 collective-permute-start.15
  74.6 8.4 %collective-permute-done.15.refs_1_ = bf16[72,2688]{1,0:T(8,128)(2,1)S(1)} collective-permute-done((bf16[72,2688]{1,0:T(8,128)(2,1)S(1)}, bf16[72,2688]{1,0:T(8,128)(2,1)S(1)}, u32[]{:S(2)}, u32[]{:S(2)}) %collective-permute-start.15) | collective-permute-done | bytes 387104 | tf_op jit(solution)/shard_map/ppermute | solution.py:374
  83.0 4.8 %collective-permute-done.18.block_ref = bf16[128,2816]{1,0:T(8,128)(2,1)S(1)} collective-permute-done((bf16[128,2816]{1,0:T(8,128)(2,1)S(1)}, bf16[128,2816]{1,0:T(8,128)(2,1)S(1)}, u32[]{:S(2)}, u32[]{:S(2)}) %collective-permute-start.18) | collective-permute-done | bytes 720928 | tf_op jit(solution)/shard_map/ppermute | solution.py:382
  89.2 1.6 collective-permute-done.16.refs_2_
  91.8 1.7 collective-permute-start.21
  95.4 1.6 collective-permute-start.26
  97.0 2.6 %copy-done = bf16[1,2688,1024]{2,1,0:T(8,128)(2,1)S(1)} copy-done((bf16[1,2688,1024]{2,1,0:T(8,128)(2,1)S(1)}, bf16[1,2688,1024]{2,1,0:T(8,128)(2,1)}, u32[]{:S(2)}) %copy-start) | copy-done | bytes 5505048
  99.5 2.6 %copy-done.1 = bf16[1,1024,2688]{2,1,0:T(8,128)(2,1)S(1)} copy-done((bf16[1,1024,2688]{2,1,0:T(8,128)(2,1)S(1)}, bf16[1,1024,2688]{2,1,0:T(8,128)(2,1)}, u32[]{:S(2)}) %copy-start.1) | copy-done | bytes 5505048
  102.1 5.4 %shard_map.140 = (bf16[144,2688]{1,0:T(8,128)(2,1)S(1)}, bf16[144,2688]{1,0:T(8,128)(2,1)S(1)}) custom-call(bf16[72,2688]{1,0:T(8,128)(2,1)S(1)} %get-tuple-element.130.refs_0_, bf16[72,2688]{1,0:T(8,128)(2,1)S(1)} %collective-permute-done.15.refs_1_, bf16[72,2688]{1,0:T(8,128)(2,1)S(1)} %collective-permute-done.16.refs_2_, ...), custom_call_target="tpu_custom_call" | custom-call | tf_op jit(solution)/shard_map/pallas_call | solution.py:411
  107.5 4.7 %collective-permute-done.21.block_ref = bf16[128,2816]{1,0:T(8,128)(2,1)S(1)} collective-permute-done((bf16[128,2816]{1,0:T(8,128)(2,1)S(1)}, bf16[128,2816]{1,0:T(8,128)(2,1)S(1)}, u32[]{:S(2)}, u32[]{:S(2)}) %collective-permute-start.21) | collective-permute-done | bytes 720928 | tf_op jit(solution)/shard_map/ppermute | solution.py:382
  114.7 1.9 collective-permute-start.22
  120.1 5.4 %shard_map.144 = (bf16[144,2688]{1,0:T(8,128)(2,1)S(1)}, bf16[144,2688]{1,0:T(8,128)(2,1)S(1)}) custom-call(bf16[72,2688]{1,0:T(8,128)(2,1)S(1)} %get-tuple-element.147.refs_0_, bf16[72,2688]{1,0:T(8,128)(2,1)S(1)} %collective-permute-done.23.refs_1_, bf16[72,2688]{1,0:T(8,128)(2,1)S(1)} %collective-permute-done.25.refs_2_, ...), custom_call_target="tpu_custom_call" | custom-call | tf_op jit(solution)/shard_map/pallas_call | solution.py:411
  125.6 2.9 %collective-permute-done.24.refs_1_ = bf16[72,2688]{1,0:T(8,128)(2,1)S(1)} collective-permute-done((bf16[72,2688]{1,0:T(8,128)(2,1)S(1)}, bf16[72,2688]{1,0:T(8,128)(2,1)S(1)}, u32[]{:S(2)}, u32[]{:S(2)}) %collective-permute-start.24) | collective-permute-done | bytes 387104 | tf_op jit(solution)/shard_map/ppermute | solution.py:374
  128.4 6.6 %collective-permute-done.22.block_ref = bf16[128,2816]{1,0:T(8,128)(2,1)S(1)} collective-permute-done((bf16[128,2816]{1,0:T(8,128)(2,1)S(1)}, bf16[128,2816]{1,0:T(8,128)(2,1)S(1)}, u32[]{:S(2)}, u32[]{:S(2)}) %collective-permute-start.22) | collective-permute-done | bytes 720928 | tf_op jit(solution)/shard_map/ppermute | solution.py:382
  144.4 6.2 %collective-permute-done.35 = bf16[72,2688]{1,0:T(8,128)(2,1)S(1)} collective-permute-done((bf16[72,2688]{1,0:T(8,128)(2,1)S(1)}, bf16[72,2688]{1,0:T(8,128)(2,1)S(1)}, u32[]{:S(2)}, u32[]{:S(2)}) %collective-permute-start.35) | collective-permute-done | bytes 387104 | tf_op jit(solution)/shard_map/ppermute | solution.py:374
  150.6 1.5 collective-permute-start.30
  152.1 5.4 %shard_map.147 = (bf16[144,2688]{1,0:T(8,128)(2,1)S(1)}, bf16[144,2688]{1,0:T(8,128)(2,1)S(1)}) custom-call(bf16[72,2688]{1,0:T(8,128)(2,1)S(1)} %get-tuple-element.161.refs_0_, bf16[72,2688]{1,0:T(8,128)(2,1)S(1)} %collective-permute-done.24.refs_1_, bf16[72,2688]{1,0:T(8,128)(2,1)S(1)} %collective-permute-done.31.refs_2_, ...), custom_call_target="tpu_custom_call" | custom-call | tf_op jit(solution)/shard_map/pallas_call | solution.py:411
  157.5 2.6 %collective-permute-done.36 = bf16[72,2688]{1,0:T(8,128)(2,1)S(1)} collective-permute-done((bf16[72,2688]{1,0:T(8,128)(2,1)S(1)}, bf16[72,2688]{1,0:T(8,128)(2,1)S(1)}, u32[]{:S(2)}, u32[]{:S(2)}) %collective-permute-start.36) | collective-permute-done | bytes 387104 | tf_op jit(solution)/shard_map/ppermute | solution.py:374
  160.6 6.7 %collective-permute-done.28.refs_1_ = bf16[72,2688]{1,0:T(8,128)(2,1)S(1)} collective-permute-done((bf16[72,2688]{1,0:T(8,128)(2,1)S(1)}, bf16[72,2688]{1,0:T(8,128)(2,1)S(1)}, u32[]{:S(2)}, u32[]{:S(2)}) %collective-permute-start.28) | collective-permute-done | bytes 387104 | tf_op jit(solution)/shard_map/ppermute | solution.py:374
  168.0 8.0 %collective-permute-done.30.refs_3_ = bf16[72,2688]{1,0:T(8,128)(2,1)S(1)} collective-permute-done((bf16[72,2688]{1,0:T(8,128)(2,1)S(1)}, bf16[72,2688]{1,0:T(8,128)(2,1)S(1)}, u32[]{:S(2)}, u32[]{:S(2)}) %collective-permute-start.30) | collective-permute-done | bytes 387104 | tf_op jit(solution)/shard_map/ppermute | solution.py:374
  182.1 5.4 %shard_map.150 = (bf16[144,2688]{1,0:T(8,128)(2,1)S(1)}, bf16[144,2688]{1,0:T(8,128)(2,1)S(1)}) custom-call(bf16[72,2688]{1,0:T(8,128)(2,1)S(1)} %get-tuple-element.171.refs_0_, bf16[72,2688]{1,0:T(8,128)(2,1)S(1)} %collective-permute-done.28.refs_1_, bf16[72,2688]{1,0:T(8,128)(2,1)S(1)} %collective-permute-done.29.refs_2_, ...), custom_call_target="tpu_custom_call" | custom-call | tf_op jit(solution)/shard_map/pallas_call | solution.py:411
  187.4 2.9 %collective-permute-done.40 = bf16[72,2688]{1,0:T(8,128)(2,1)S(1)} collective-permute-done((bf16[72,2688]{1,0:T(8,128)(2,1)S(1)}, bf16[72,2688]{1,0:T(8,128)(2,1)S(1)}, u32[]{:S(2)}, u32[]{:S(2)}) %collective-permute-start.40) | collective-permute-done | bytes 387104 | tf_op jit(solution)/shard_map/ppermute | solution.py:374
  190.4 8.1 %collective-permute-done.41 = bf16[72,2688]{1,0:T(8,128)(2,1)S(1)} collective-permute-done((bf16[72,2688]{1,0:T(8,128)(2,1)S(1)}, bf16[72,2688]{1,0:T(8,128)(2,1)S(1)}, u32[]{:S(2)}, u32[]{:S(2)}) %collective-permute-start.41) | collective-permute-done | bytes 387104 | tf_op jit(solution)/shard_map/ppermute | solution.py:374
  203.8 1.6 collective-permute-start.49
  206.5 7.3 %collective-permute-done.47 = bf16[72,2688]{1,0:T(8,128)(2,1)S(1)} collective-permute-done((bf16[72,2688]{1,0:T(8,128)(2,1)S(1)}, bf16[72,2688]{1,0:T(8,128)(2,1)S(1)}, u32[]{:S(2)}, u32[]{:S(2)}) %collective-permute-start.47) | collective-permute-done | bytes 387104 | tf_op jit(solution)/shard_map/ppermute | solution.py:374
  213.8 7.1 %collective-permute-done.48 = bf16[72,2688]{1,0:T(8,128)(2,1)S(1)} collective-permute-done((bf16[72,2688]{1,0:T(8,128)(2,1)S(1)}, bf16[72,2688]{1,0:T(8,128)(2,1)S(1)}, u32[]{:S(2)}, u32[]{:S(2)}) %collective-permute-start.48) | collective-permute-done | bytes 387104 | tf_op jit(solution)/shard_map/ppermute | solution.py:374
  221.4 1.7 collective-permute-start.52
  224.9 1.7 collective-permute-start.46
  226.6 8.4 %collective-permute-done.44 = bf16[72,2688]{1,0:T(8,128)(2,1)S(1)} collective-permute-done((bf16[72,2688]{1,0:T(8,128)(2,1)S(1)}, bf16[72,2688]{1,0:T(8,128)(2,1)S(1)}, u32[]{:S(2)}, u32[]{:S(2)}) %collective-permute-start.44) | collective-permute-done | bytes 387104 | tf_op jit(solution)/shard_map/ppermute | solution.py:374
  235.0 4.1 %collective-permute-done.45 = bf16[72,2688]{1,0:T(8,128)(2,1)S(1)} collective-permute-done((bf16[72,2688]{1,0:T(8,128)(2,1)S(1)}, bf16[72,2688]{1,0:T(8,128)(2,1)S(1)}, u32[]{:S(2)}, u32[]{:S(2)}) %collective-permute-start.45) | collective-permute-done | bytes 387104 | tf_op jit(solution)/shard_map/ppermute | solution.py:374
  (153 shorter events, 63.5 us)
Async XLA Ops:
  0.0 43.2 %collective-permute-start.12 = (bf16[512,2688]{1,0:T(8,128)(2,1)}, bf16[512,2688]{1,0:T(8,128)(2,1)}, u32[]{:S(2)}, u32[]{:S(2)}) collective-permute-start(bf16[512,2688]{1,0:T(8,128)(2,1)} %rest_4_.3), channel_id=1, source_target_pairs={{0,1},{1,0},{2,3},{3,2},{4,5},{5,4},{6,7},{7,6},{8,9},{9,8},{10,11... | collective-permute-start | bytes 8257544 | tf_op jit(solution)/shard_map/ppermute | solution.py:374
  2.3 14.8 %collective-permute-start = (bf16[128,1536]{1,0:T(8,128)(2,1)S(1)}, bf16[128,1536]{1,0:T(8,128)(2,1)S(1)}, u32[]{:S(2)}, u32[]{:S(2)}) collective-permute-start(bf16[128,1536]{1,0:T(8,128)(2,1)S(1)} %get-tuple-element.103), channel_id=1, source_target_pairs={{0,2},{1,3},{2,0},{3,1},{4,6},{5,7},{6,4},{7,5},{8,10},{9,11},{10,... | collective-permute-start | bytes 1179656 | tf_op jit(solution)/shard_map/ppermute | solution.py:374
  4.8 12.2 %collective-permute-start.2 = (bf16[16,3072]{1,0:T(8,128)(2,1)S(1)}, bf16[16,3072]{1,0:T(8,128)(2,1)S(1)}, u32[]{:S(2)}, u32[]{:S(2)}) collective-permute-start(bf16[16,3072]{1,0:T(8,128)(2,1)S(1)} %get-tuple-element.104), channel_id=1, source_target_pairs={{0,3},{1,0},{2,1},{3,6},{4,7},{5,4},{6,5},{7,10},{8,11},{9,8},{10,... | collective-permute-start | bytes 294920 | tf_op jit(solution)/shard_map/ppermute | solution.py:401
  6.9 10.2 %collective-permute-start.1 = (bf16[16,3072]{1,0:T(8,128)(2,1)S(1)}, bf16[16,3072]{1,0:T(8,128)(2,1)S(1)}, u32[]{:S(2)}, u32[]{:S(2)}) collective-permute-start(bf16[16,3072]{1,0:T(8,128)(2,1)S(1)} %get-tuple-element.104), channel_id=1, source_target_pairs={{0,1},{1,2},{2,3},{3,4},{4,5},{5,6},{6,7},{7,8},{8,9},{9,10},{10,1... | collective-permute-start | bytes 294920 | tf_op jit(solution)/shard_map/ppermute | solution.py:401
  19.9 5.3 %collective-permute-start.5 = (bf16[2,80,256]{2,1,0:T(8,128)(2,1)S(1)}, bf16[2,80,256]{2,1,0:T(8,128)(2,1)S(1)}, u32[]{:S(2)}, u32[]{:S(2)}) collective-permute-start(bf16[2,80,256]{2,1,0:T(8,128)(2,1)S(1)} %get-tuple-element.111), channel_id=1, source_target_pairs={{0,4},{1,5},{2,6},{3,7},{4,0},{5,1},{6,2},{7,3},{8,12},{9,13},{10,... | collective-permute-start | bytes 245768 | tf_op jit(solution)/shard_map/ppermute | solution.py:374
  20.9 5.1 %collective-permute-start.6 = (bf16[2,80,256]{2,1,0:T(8,128)(2,1)S(1)}, bf16[2,80,256]{2,1,0:T(8,128)(2,1)S(1)}, u32[]{:S(2)}, u32[]{:S(2)}) collective-permute-start(bf16[2,80,256]{2,1,0:T(8,128)(2,1)S(1)} %get-tuple-element.112), channel_id=1, source_target_pairs={{0,5},{1,4},{2,7},{3,6},{4,1},{5,0},{6,3},{7,2},{8,13},{9,12},{10,... | collective-permute-start | bytes 245768 | tf_op jit(solution)/shard_map/ppermute | solution.py:374
  28.8 14.4 %collective-permute-start.13 = (bf16[128,1024]{1,0:T(8,128)(2,1)S(1)}, bf16[128,1024]{1,0:T(8,128)(2,1)S(1)}, u32[]{:S(2)}, u32[]{:S(2)}) collective-permute-start(bf16[128,1024]{1,0:T(8,128)(2,1)S(1)} %get-tuple-element.120), channel_id=1, source_target_pairs={{0,2},{1,3},{2,0},{3,1},{4,6},{5,7},{6,4},{7,5},{8,10},{9,11},{10,... | collective-permute-start | bytes 786440 | tf_op jit(solution)/shard_map/ppermute | solution.py:374
  37.1 6.1 %collective-permute-start.9 = (bf16[2,64,256]{2,1,0:T(8,128)(2,1)S(1)}, bf16[2,64,256]{2,1,0:T(8,128)(2,1)S(1)}, u32[]{:S(2)}, u32[]{:S(2)}) collective-permute-start(bf16[2,64,256]{2,1,0:T(8,128)(2,1)S(1)} %get-tuple-element.116), channel_id=1, source_target_pairs={{0,1},{1,0},{2,3},{3,2},{4,5},{5,4},{6,7},{7,6},{8,9},{9,8},{10,11... | collective-permute-start | bytes 196616 | tf_op jit(solution)/shard_map/ppermute | solution.py:374
  37.1 6.0 %collective-permute-start.10 = (bf16[2,64,256]{2,1,0:T(8,128)(2,1)S(1)}, bf16[2,64,256]{2,1,0:T(8,128)(2,1)S(1)}, u32[]{:S(2)}, u32[]{:S(2)}) collective-permute-start(bf16[2,64,256]{2,1,0:T(8,128)(2,1)S(1)} %get-tuple-element.117), channel_id=1, source_target_pairs={{0,4},{1,5},{2,6},{3,7},{4,0},{5,1},{6,2},{7,3},{8,12},{9,13},{10,... | collective-permute-start | bytes 196616 | tf_op jit(solution)/shard_map/ppermute | solution.py:374
  47.8 18.1 %collective-permute-start.14 = (bf16[128,2688]{1,0:T(8,128)(2,1)}, bf16[128,2688]{1,0:T(8,128)(2,1)}, u32[]{:S(2)}, u32[]{:S(2)}) collective-permute-start(bf16[128,2688]{1,0:T(8,128)(2,1)} %shard_map.135), channel_id=1, source_target_pairs={{0,2},{1,3},{2,0},{3,1},{4,6},{5,7},{6,4},{7,5},{8,10},{9,11},{10,... | collective-permute-start | bytes 2064392 | tf_op jit(solution)/shard_map/ppermute | solution.py:374
  67.6 20.3 %collective-permute-start.18 = (bf16[128,2816]{1,0:T(8,128)(2,1)S(1)}, bf16[128,2816]{1,0:T(8,128)(2,1)S(1)}, u32[]{:S(2)}, u32[]{:S(2)}) collective-permute-start(bf16[128,2816]{1,0:T(8,128)(2,1)S(1)} %get-tuple-element.122.block_ref), channel_id=1, source_target_pairs={{0,8},{1,9},{2,10},{3,11},{4,12},{5,13},{6,14},{7,15},{8,16},{9,17... | collective-permute-start | bytes 2162696 | tf_op jit(solution)/shard_map/ppermute | solution.py:382
  71.0 12.0 %collective-permute-start.15 = (bf16[72,2688]{1,0:T(8,128)(2,1)S(1)}, bf16[72,2688]{1,0:T(8,128)(2,1)S(1)}, u32[]{:S(2)}, u32[]{:S(2)}) collective-permute-start(bf16[72,2688]{1,0:T(8,128)(2,1)S(1)} %get-tuple-element.125), channel_id=1, source_target_pairs={{0,2},{1,3},{2,0},{3,1},{4,6},{5,7},{6,4},{7,5},{8,10},{9,11},{10,... | collective-permute-start | bytes 1161224 | tf_op jit(solution)/shard_map/ppermute | solution.py:374
  72.6 18.2 %collective-permute-start.16 = (bf16[72,2688]{1,0:T(8,128)(2,1)S(1)}, bf16[72,2688]{1,0:T(8,128)(2,1)S(1)}, u32[]{:S(2)}, u32[]{:S(2)}) collective-permute-start(bf16[72,2688]{1,0:T(8,128)(2,1)S(1)} %get-tuple-element.126), channel_id=1, source_target_pairs={{0,4},{1,5},{2,6},{3,7},{4,0},{5,1},{6,2},{7,3},{8,12},{9,13},{10,... | collective-permute-start | bytes 1161224 | tf_op jit(solution)/shard_map/ppermute | solution.py:374
  74.0 16.8 %collective-permute-start.17 = (bf16[72,2688]{1,0:T(8,128)(2,1)S(1)}, bf16[72,2688]{1,0:T(8,128)(2,1)S(1)}, u32[]{:S(2)}, u32[]{:S(2)}) collective-permute-start(bf16[72,2688]{1,0:T(8,128)(2,1)S(1)} %get-tuple-element.127), channel_id=1, source_target_pairs={{0,6},{1,7},{2,4},{3,5},{4,2},{5,3},{6,0},{7,1},{8,14},{9,15},{10,... | collective-permute-start | bytes 1161224 | tf_op jit(solution)/shard_map/ppermute | solution.py:374
  91.7 5.2 %collective-permute-start.19 = (bf16[144,2688]{1,0:T(8,128)(2,1)S(1)}, bf16[144,2688]{1,0:T(8,128)(2,1)S(1)}, u32[]{:S(2)}, u32[]{:S(2)}) collective-permute-start(bf16[144,2688]{1,0:T(8,128)(2,1)S(1)} %shard_map.139), channel_id=1, source_target_pairs={{0,1},{1,0},{2,3},{3,2},{4,5},{5,4},{6,7},{7,6},{8,9},{9,8},{10,11... | collective-permute-start | bytes 2322440 | tf_op jit(solution)/shard_map/ppermute | solution.py:374
  91.8 20.3 %collective-permute-start.21 = (bf16[128,2816]{1,0:T(8,128)(2,1)S(1)}, bf16[128,2816]{1,0:T(8,128)(2,1)S(1)}, u32[]{:S(2)}, u32[]{:S(2)}) collective-permute-start(bf16[128,2816]{1,0:T(8,128)(2,1)S(1)} %collective-permute-done.18.block_ref), channel_id=1, source_target_pairs={{0,8},{1,9},{2,10},{3,11},{4,12},{5,13},{6,14},{7,15},{8,16},{9,17... | collective-permute-start | bytes 2162696 | tf_op jit(solution)/shard_map/ppermute | solution.py:382
  93.5 14.0 %collective-permute-start.23 = (bf16[72,2688]{1,0:T(8,128)(2,1)S(1)}, bf16[72,2688]{1,0:T(8,128)(2,1)S(1)}, u32[]{:S(2)}, u32[]{:S(2)}) collective-permute-start(bf16[72,2688]{1,0:T(8,128)(2,1)S(1)} %get-tuple-element.140), channel_id=1, source_target_pairs={{0,2},{1,3},{2,0},{3,1},{4,6},{5,7},{6,4},{7,5},{8,10},{9,11},{10,... | collective-permute-start | bytes 1161224 | tf_op jit(solution)/shard_map/ppermute | solution.py:374
  94.6 18.9 %collective-permute-start.25 = (bf16[72,2688]{1,0:T(8,128)(2,1)S(1)}, bf16[72,2688]{1,0:T(8,128)(2,1)S(1)}, u32[]{:S(2)}, u32[]{:S(2)}) collective-permute-start(bf16[72,2688]{1,0:T(8,128)(2,1)S(1)} %get-tuple-element.144), channel_id=1, source_target_pairs={{0,4},{1,5},{2,6},{3,7},{4,0},{5,1},{6,2},{7,3},{8,12},{9,13},{10,... | collective-permute-start | bytes 1161224 | tf_op jit(solution)/shard_map/ppermute | solution.py:374
  95.4 18.2 %collective-permute-start.26 = (bf16[72,2688]{1,0:T(8,128)(2,1)S(1)}, bf16[72,2688]{1,0:T(8,128)(2,1)S(1)}, u32[]{:S(2)}, u32[]{:S(2)}) collective-permute-start(bf16[72,2688]{1,0:T(8,128)(2,1)S(1)} %get-tuple-element.145), channel_id=1, source_target_pairs={{0,6},{1,7},{2,4},{3,5},{4,2},{5,3},{6,0},{7,1},{8,14},{9,15},{10,... | collective-permute-start | bytes 1161224 | tf_op jit(solution)/shard_map/ppermute | solution.py:374
  114.6 5.5 %collective-permute-start.27 = (bf16[144,2688]{1,0:T(8,128)(2,1)S(1)}, bf16[144,2688]{1,0:T(8,128)(2,1)S(1)}, u32[]{:S(2)}, u32[]{:S(2)}) collective-permute-start(bf16[144,2688]{1,0:T(8,128)(2,1)S(1)} %shard_map.143), channel_id=1, source_target_pairs={{0,1},{1,0},{2,3},{3,2},{4,5},{5,4},{6,7},{7,6},{8,9},{9,8},{10,11... | collective-permute-start | bytes 2322440 | tf_op jit(solution)/shard_map/ppermute | solution.py:374
  114.7 20.3 %collective-permute-start.22 = (bf16[128,2816]{1,0:T(8,128)(2,1)S(1)}, bf16[128,2816]{1,0:T(8,128)(2,1)S(1)}, u32[]{:S(2)}, u32[]{:S(2)}) collective-permute-start(bf16[128,2816]{1,0:T(8,128)(2,1)S(1)} %collective-permute-done.21.block_ref), channel_id=1, source_target_pairs={{0,8},{1,9},{2,10},{3,11},{4,12},{5,13},{6,14},{7,15},{8,16},{9,17... | collective-permute-start | bytes 2162696 | tf_op jit(solution)/shard_map/ppermute | solution.py:382
  116.6 11.8 %collective-permute-start.24 = (bf16[72,2688]{1,0:T(8,128)(2,1)S(1)}, bf16[72,2688]{1,0:T(8,128)(2,1)S(1)}, u32[]{:S(2)}, u32[]{:S(2)}) collective-permute-start(bf16[72,2688]{1,0:T(8,128)(2,1)S(1)} %get-tuple-element.142), channel_id=1, source_target_pairs={{0,2},{1,3},{2,0},{3,1},{4,6},{5,7},{6,4},{7,5},{8,10},{9,11},{10,... | collective-permute-start | bytes 1161224 | tf_op jit(solution)/shard_map/ppermute | solution.py:374
  117.5 19.1 %collective-permute-start.31 = (bf16[72,2688]{1,0:T(8,128)(2,1)S(1)}, bf16[72,2688]{1,0:T(8,128)(2,1)S(1)}, u32[]{:S(2)}, u32[]{:S(2)}) collective-permute-start(bf16[72,2688]{1,0:T(8,128)(2,1)S(1)} %get-tuple-element.158), channel_id=1, source_target_pairs={{0,4},{1,5},{2,6},{3,7},{4,0},{5,1},{6,2},{7,3},{8,12},{9,13},{10,... | collective-permute-start | bytes 1161224 | tf_op jit(solution)/shard_map/ppermute | solution.py:374
  118.9 17.7 %collective-permute-start.32 = (bf16[72,2688]{1,0:T(8,128)(2,1)S(1)}, bf16[72,2688]{1,0:T(8,128)(2,1)S(1)}, u32[]{:S(2)}, u32[]{:S(2)}) collective-permute-start(bf16[72,2688]{1,0:T(8,128)(2,1)S(1)} %get-tuple-element.159), channel_id=1, source_target_pairs={{0,6},{1,7},{2,4},{3,5},{4,2},{5,3},{6,0},{7,1},{8,14},{9,15},{10,... | collective-permute-start | bytes 1161224 | tf_op jit(solution)/shard_map/ppermute | solution.py:374
  125.5 12.2 %collective-permute-start.34 = (bf16[144,2688]{1,0:T(8,128)(2,1)S(1)}, bf16[144,2688]{1,0:T(8,128)(2,1)S(1)}, u32[]{:S(2)}, u32[]{:S(2)}) collective-permute-start(bf16[144,2688]{1,0:T(8,128)(2,1)S(1)} %get-tuple-element.166), channel_id=1, source_target_pairs={{0,1},{1,0},{2,3},{3,2},{4,5},{5,4},{6,7},{7,6},{8,9},{9,8},{10,11... | collective-permute-start | bytes 2322440 | tf_op jit(solution)/shard_map/ppermute | solution.py:374
  137.6 5.8 %collective-permute-start.33 = (bf16[144,2688]{1,0:T(8,128)(2,1)S(1)}, bf16[144,2688]{1,0:T(8,128)(2,1)S(1)}, u32[]{:S(2)}, u32[]{:S(2)}) collective-permute-start(bf16[144,2688]{1,0:T(8,128)(2,1)S(1)} %shard_map.146), channel_id=1, source_target_pairs={{0,1},{1,0},{2,3},{3,2},{4,5},{5,4},{6,7},{7,6},{8,9},{9,8},{10,11... | collective-permute-start | bytes 2322440 | tf_op jit(solution)/shard_map/ppermute | solution.py:374
  138.8 11.8 %collective-permute-start.35 = (bf16[72,2688]{1,0:T(8,128)(2,1)S(1)}, bf16[72,2688]{1,0:T(8,128)(2,1)S(1)}, u32[]{:S(2)}, u32[]{:S(2)}) collective-permute-start(bf16[72,2688]{1,0:T(8,128)(2,1)S(1)} %get-tuple-element.168), channel_id=1, source_target_pairs={{0,2},{1,3},{2,0},{3,1},{4,6},{5,7},{6,4},{7,5},{8,10},{9,11},{10,... | collective-permute-start | bytes 1161224 | tf_op jit(solution)/shard_map/ppermute | solution.py:374
  139.9 20.1 %collective-permute-start.36 = (bf16[72,2688]{1,0:T(8,128)(2,1)S(1)}, bf16[72,2688]{1,0:T(8,128)(2,1)S(1)}, u32[]{:S(2)}, u32[]{:S(2)}) collective-permute-start(bf16[72,2688]{1,0:T(8,128)(2,1)S(1)} %get-tuple-element.169), channel_id=1, source_target_pairs={{0,4},{1,5},{2,6},{3,7},{4,0},{5,1},{6,2},{7,3},{8,12},{9,13},{10,... | collective-permute-start | bytes 1161224 | tf_op jit(solution)/shard_map/ppermute | solution.py:374
  140.9 19.2 %collective-permute-start.37 = (bf16[72,2688]{1,0:T(8,128)(2,1)S(1)}, bf16[72,2688]{1,0:T(8,128)(2,1)S(1)}, u32[]{:S(2)}, u32[]{:S(2)}) collective-permute-start(bf16[72,2688]{1,0:T(8,128)(2,1)S(1)} %get-tuple-element.170), channel_id=1, source_target_pairs={{0,6},{1,7},{2,4},{3,5},{4,2},{5,3},{6,0},{7,1},{8,14},{9,15},{10,... | collective-permute-start | bytes 1161224 | tf_op jit(solution)/shard_map/ppermute | solution.py:374
  142.3 24.9 %collective-permute-start.28 = (bf16[72,2688]{1,0:T(8,128)(2,1)S(1)}, bf16[72,2688]{1,0:T(8,128)(2,1)S(1)}, u32[]{:S(2)}, u32[]{:S(2)}) collective-permute-start(bf16[72,2688]{1,0:T(8,128)(2,1)S(1)} %get-tuple-element.154), channel_id=1, source_target_pairs={{0,2},{1,3},{2,0},{3,1},{4,6},{5,7},{6,4},{7,5},{8,10},{9,11},{10,... | collective-permute-start | bytes 1161224 | tf_op jit(solution)/shard_map/ppermute | solution.py:374
  143.4 24.5 %collective-permute-start.29 = (bf16[72,2688]{1,0:T(8,128)(2,1)S(1)}, bf16[72,2688]{1,0:T(8,128)(2,1)S(1)}, u32[]{:S(2)}, u32[]{:S(2)}) collective-permute-start(bf16[72,2688]{1,0:T(8,128)(2,1)S(1)} %get-tuple-element.155), channel_id=1, source_target_pairs={{0,4},{1,5},{2,6},{3,7},{4,0},{5,1},{6,2},{7,3},{8,12},{9,13},{10,... | collective-permute-start | bytes 1161224 | tf_op jit(solution)/shard_map/ppermute | solution.py:374
  150.6 25.3 %collective-permute-start.30 = (bf16[72,2688]{1,0:T(8,128)(2,1)S(1)}, bf16[72,2688]{1,0:T(8,128)(2,1)S(1)}, u32[]{:S(2)}, u32[]{:S(2)}) collective-permute-start(bf16[72,2688]{1,0:T(8,128)(2,1)S(1)} %get-tuple-element.156), channel_id=1, source_target_pairs={{0,6},{1,7},{2,4},{3,5},{4,2},{5,3},{6,0},{7,1},{8,14},{9,15},{10,... | collective-permute-start | bytes 1161224 | tf_op jit(solution)/shard_map/ppermute | solution.py:374
  160.1 17.3 %collective-permute-start.39 = (bf16[144,2688]{1,0:T(8,128)(2,1)S(1)}, bf16[144,2688]{1,0:T(8,128)(2,1)S(1)}, u32[]{:S(2)}, u32[]{:S(2)}) collective-permute-start(bf16[144,2688]{1,0:T(8,128)(2,1)S(1)} %get-tuple-element.176), channel_id=1, source_target_pairs={{0,1},{1,0},{2,3},{3,2},{4,5},{5,4},{6,7},{7,6},{8,9},{9,8},{10,11... | collective-permute-start | bytes 2322440 | tf_op jit(solution)/shard_map/ppermute | solution.py:374
  177.0 5.1 %collective-permute-start.38 = (bf16[144,2688]{1,0:T(8,128)(2,1)S(1)}, bf16[144,2688]{1,0:T(8,128)(2,1)S(1)}, u32[]{:S(2)}, u32[]{:S(2)}) collective-permute-start(bf16[144,2688]{1,0:T(8,128)(2,1)S(1)} %shard_map.149), channel_id=1, source_target_pairs={{0,1},{1,0},{2,3},{3,2},{4,5},{5,4},{6,7},{7,6},{8,9},{9,8},{10,11... | collective-permute-start | bytes 2322440 | tf_op jit(solution)/shard_map/ppermute | solution.py:374
  177.0 22.0 %collective-permute-start.50 = (bf16[128,2688]{1,0:T(8,128)(2,1)S(1)}, bf16[128,2688]{1,0:T(8,128)(2,1)S(1)}, u32[]{:S(2)}, u32[]{:S(2)}) collective-permute-start(bf16[128,2688]{1,0:T(8,128)(2,1)S(1)} %fusion), channel_id=1, source_target_pairs={{0,8},{1,9},{2,10},{3,11},{4,12},{5,13},{6,14},{7,15},{8,16},{9,17... | collective-permute-start | bytes 2064392 | tf_op jit(solution)/shard_map/ppermute | solution.py:382
  178.5 11.9 %collective-permute-start.40 = (bf16[72,2688]{1,0:T(8,128)(2,1)S(1)}, bf16[72,2688]{1,0:T(8,128)(2,1)S(1)}, u32[]{:S(2)}, u32[]{:S(2)}) collective-permute-start(bf16[72,2688]{1,0:T(8,128)(2,1)S(1)} %get-tuple-element.178), channel_id=1, source_target_pairs={{0,2},{1,3},{2,0},{3,1},{4,6},{5,7},{6,4},{7,5},{8,10},{9,11},{10,... | collective-permute-start | bytes 1161224 | tf_op jit(solution)/shard_map/ppermute | solution.py:374
  179.5 19.1 %collective-permute-start.41 = (bf16[72,2688]{1,0:T(8,128)(2,1)S(1)}, bf16[72,2688]{1,0:T(8,128)(2,1)S(1)}, u32[]{:S(2)}, u32[]{:S(2)}) collective-permute-start(bf16[72,2688]{1,0:T(8,128)(2,1)S(1)} %get-tuple-element.179), channel_id=1, source_target_pairs={{0,4},{1,5},{2,6},{3,7},{4,0},{5,1},{6,2},{7,3},{8,12},{9,13},{10,... | collective-permute-start | bytes 1161224 | tf_op jit(solution)/shard_map/ppermute | solution.py:374
  180.8 17.7 %collective-permute-start.42 = (bf16[72,2688]{1,0:T(8,128)(2,1)S(1)}, bf16[72,2688]{1,0:T(8,128)(2,1)S(1)}, u32[]{:S(2)}, u32[]{:S(2)}) collective-permute-start(bf16[72,2688]{1,0:T(8,128)(2,1)S(1)} %get-tuple-element.180), channel_id=1, source_target_pairs={{0,6},{1,7},{2,4},{3,5},{4,2},{5,3},{6,0},{7,1},{8,14},{9,15},{10,... | collective-permute-start | bytes 1161224 | tf_op jit(solution)/shard_map/ppermute | solution.py:374
  182.1 23.3 %collective-permute-start.20 = (bf16[144,2688]{1,0:T(8,128)(2,1)S(1)}, bf16[144,2688]{1,0:T(8,128)(2,1)S(1)}, u32[]{:S(2)}, u32[]{:S(2)}) collective-permute-start(bf16[144,2688]{1,0:T(8,128)(2,1)S(1)} %get-tuple-element.135), channel_id=1, source_target_pairs={{0,1},{1,0},{2,3},{3,2},{4,5},{5,4},{6,7},{7,6},{8,9},{9,8},{10,11... | collective-permute-start | bytes 2322440 | tf_op jit(solution)/shard_map/ppermute | solution.py:374
  190.4 10.3 %collective-permute-start.43 = (bf16[144,2688]{1,0:T(8,128)(2,1)S(1)}, bf16[144,2688]{1,0:T(8,128)(2,1)S(1)}, u32[]{:S(2)}, u32[]{:S(2)}) collective-permute-start(bf16[144,2688]{1,0:T(8,128)(2,1)S(1)} %get-tuple-element.182), channel_id=1, source_target_pairs={{0,1},{1,0},{2,3},{3,2},{4,5},{5,4},{6,7},{7,6},{8,9},{9,8},{10,11... | collective-permute-start | bytes 2322440 | tf_op jit(solution)/shard_map/ppermute | solution.py:374
  199.2 21.7 %collective-permute-start.51 = (bf16[128,2688]{1,0:T(8,128)(2,1)S(1)}, bf16[128,2688]{1,0:T(8,128)(2,1)S(1)}, u32[]{:S(2)}, u32[]{:S(2)}) collective-permute-start(bf16[128,2688]{1,0:T(8,128)(2,1)S(1)} %add_convert_fusion.1), channel_id=1, source_target_pairs={{0,8},{1,9},{2,10},{3,11},{4,12},{5,13},{6,14},{7,15},{8,16},{9,17... | collective-permute-start | bytes 2064392 | tf_op jit(solution)/shard_map/ppermute | solution.py:382
  201.8 12.0 %collective-permute-start.47 = (bf16[72,2688]{1,0:T(8,128)(2,1)S(1)}, bf16[72,2688]{1,0:T(8,128)(2,1)S(1)}, u32[]{:S(2)}, u32[]{:S(2)}) collective-permute-start(bf16[72,2688]{1,0:T(8,128)(2,1)S(1)} %get-tuple-element.188), channel_id=1, source_target_pairs={{0,2},{1,3},{2,0},{3,1},{4,6},{5,7},{6,4},{7,5},{8,10},{9,11},{10,... | collective-permute-start | bytes 1161224 | tf_op jit(solution)/shard_map/ppermute | solution.py:374
  203.0 17.9 %collective-permute-start.48 = (bf16[72,2688]{1,0:T(8,128)(2,1)S(1)}, bf16[72,2688]{1,0:T(8,128)(2,1)S(1)}, u32[]{:S(2)}, u32[]{:S(2)}) collective-permute-start(bf16[72,2688]{1,0:T(8,128)(2,1)S(1)} %get-tuple-element.189), channel_id=1, source_target_pairs={{0,4},{1,5},{2,6},{3,7},{4,0},{5,1},{6,2},{7,3},{8,12},{9,13},{10,... | collective-permute-start | bytes 1161224 | tf_op jit(solution)/shard_map/ppermute | solution.py:374
  203.8 17.1 %collective-permute-start.49 = (bf16[72,2688]{1,0:T(8,128)(2,1)S(1)}, bf16[72,2688]{1,0:T(8,128)(2,1)S(1)}, u32[]{:S(2)}, u32[]{:S(2)}) collective-permute-start(bf16[72,2688]{1,0:T(8,128)(2,1)S(1)} %get-tuple-element.190), channel_id=1, source_target_pairs={{0,6},{1,7},{2,4},{3,5},{4,2},{5,3},{6,0},{7,1},{8,14},{9,15},{10,... | collective-permute-start | bytes 1161224 | tf_op jit(solution)/shard_map/ppermute | solution.py:374
  221.4 18.8 %collective-permute-start.52 = (bf16[128,2688]{1,0:T(8,128)(2,1)S(1)}, bf16[128,2688]{1,0:T(8,128)(2,1)S(1)}, u32[]{:S(2)}, u32[]{:S(2)}) collective-permute-start(bf16[128,2688]{1,0:T(8,128)(2,1)S(1)} %fusion.21), channel_id=1, source_target_pairs={{0,8},{1,9},{2,10},{3,11},{4,12},{5,13},{6,14},{7,15},{8,16},{9,17... | collective-permute-start | bytes 2064392 | tf_op jit(solution)/shard_map/ppermute | solution.py:382
  223.1 11.9 %collective-permute-start.44 = (bf16[72,2688]{1,0:T(8,128)(2,1)S(1)}, bf16[72,2688]{1,0:T(8,128)(2,1)S(1)}, u32[]{:S(2)}, u32[]{:S(2)}) collective-permute-start(bf16[72,2688]{1,0:T(8,128)(2,1)S(1)} %get-tuple-element.185), channel_id=1, source_target_pairs={{0,2},{1,3},{2,0},{3,1},{4,6},{5,7},{6,4},{7,5},{8,10},{9,11},{10,... | collective-permute-start | bytes 1161224 | tf_op jit(solution)/shard_map/ppermute | solution.py:374
  224.0 15.1 %collective-permute-start.45 = (bf16[72,2688]{1,0:T(8,128)(2,1)S(1)}, bf16[72,2688]{1,0:T(8,128)(2,1)S(1)}, u32[]{:S(2)}, u32[]{:S(2)}) collective-permute-start(bf16[72,2688]{1,0:T(8,128)(2,1)S(1)} %get-tuple-element.186), channel_id=1, source_target_pairs={{0,4},{1,5},{2,6},{3,7},{4,0},{5,1},{6,2},{7,3},{8,12},{9,13},{10,... | collective-permute-start | bytes 1161224 | tf_op jit(solution)/shard_map/ppermute | solution.py:374
  224.9 15.3 %collective-permute-start.46 = (bf16[72,2688]{1,0:T(8,128)(2,1)S(1)}, bf16[72,2688]{1,0:T(8,128)(2,1)S(1)}, u32[]{:S(2)}, u32[]{:S(2)}) collective-permute-start(bf16[72,2688]{1,0:T(8,128)(2,1)S(1)} %get-tuple-element.187), channel_id=1, source_target_pairs={{0,6},{1,7},{2,4},{3,5},{4,2},{5,3},{6,0},{7,1},{8,14},{9,15},{10,... | collective-permute-start | bytes 1161224 | tf_op jit(solution)/shard_map/ppermute | solution.py:374
  (31 other events, 382.6 us)
